TPU v7x, 512 devices: a whole 4x8x8 slice. The times are simulated.
512 devices in a mesh: section: 4 (over z_lo), dp: 16 (over z_hi, y), mp: 8 (over x, core).
Axes of the slice: x: 4, y: 8, z: 8 (z_hi: 2, z_lo: 4; z = z_hi * 4 + z_lo), core: 2. Of those that a mesh axis runs over, the one named last changes fastest.
Arguments:
- passage_tokens: bfloat16 [128, 128, 2048], P(('section', 'dp'), None, 'mp'), may hold values from -6 to 6
- query_tokens: bfloat16 [256, 32, 2048], P(('section', 'dp'), None, 'mp'), may hold values from -6 to 6
- norm_gain: bfloat16 [2048], P('mp'), may hold values from 0.5 to 1.5
- w_gate: bfloat16 [2048, 5120], P('dp', 'mp'), may hold values from -0.125 to 0.125
- w_up: bfloat16 [2048, 5120], P('dp', 'mp'), may hold values from -0.125 to 0.125
- w_down: bfloat16 [5120, 2048], P('mp', 'dp'), may hold values from -0.078125 to 0.078125
- old_head: bfloat16 [2048, 768], P('mp'), may hold values from -0.125 to 0.125
- new_head: bfloat16 [2048, 768], P('mp'), may hold values from -0.125 to 0.125
- stale_index: bfloat16 [131072, 768], P(('section', 'dp'), 'mp'), may hold values from -6 to 6
- neg_owner: int32 [256, 8], P(('section', 'dp')), may hold values from 0 to 63, all different within a row; in each aligned block of 4 rows (0 to 3, 4 to 7, ...) at most 2 rows name the same one
- neg_row: int32 [256, 8], P(('section', 'dp')), may hold values from 0 to 2047
- pos_slot: int32 [256], P(('section', 'dp')), may hold values from 0 to 1
Outputs:
- refreshed: bfloat16 [128, 768], P(('section', 'dp'), 'mp')
- losses: float32 [256], P(('section', 'dp'))
- head_grad: float32 [2048, 768], P('mp', 'dp')
Inputs may be any that keep to these rules, and one draw needn't show every extreme that they name: `neg_owner`: each query names 8 different index shards; the 4 queries of one shard name one index shard at most 2 times.
All inputs are finite; a program needn't handle non-finite values.
Results may differ from a plain program's by a relative error of at most 0.029.
Values may be sent and summed in bfloat16 or wider, within the bound.
No kernel may reach another device: no remote copies, remote signals or barrier semaphores. Data moves between devices by JAX's collectives and lax.ppermute only.
A program may use at most 64 MiB of HBM per device.

v0:
```python
import jax
import jax.numpy as jnp
from jax import lax
from jax.sharding import PartitionSpec as P

TAU = 0.02


def pool_rows(values, p_count, length, q_count, q_length):
    width = values.shape[1]
    split = p_count * length
    passages = values[:split].astype(jnp.float32).reshape(p_count, length, width)
    queries = values[split:].astype(jnp.float32).reshape(q_count, q_length, width)
    return jnp.concatenate(
        [jnp.sum(passages, axis=1) / length, jnp.sum(queries, axis=1) / q_length], axis=0
    )


def shards(
    passage_tokens,
    query_tokens,
    norm_gain,
    w_gate,
    w_up,
    w_down,
    old_head,
    new_head,
    stale_index,
    neg_owner,
    neg_row,
    pos_slot,
):
    p_count, length, local_width = passage_tokens.shape
    q_count, q_length, _ = query_tokens.shape
    k_count = neg_owner.shape[1]
    token_rows = jnp.concatenate(
        [passage_tokens.reshape(-1, local_width), query_tokens.reshape(-1, local_width)], axis=0
    )
    whole_rows, whole_gain = (
        lax.all_gather(token_rows, "mp", axis=1, tiled=True),
        lax.all_gather(norm_gain, "mp", axis=0, tiled=True),
    )
    values = whole_rows.astype(jnp.float32)
    scale = lax.rsqrt(jnp.mean(values * values, axis=1, keepdims=True) + 1e-06)
    normed = (values * scale * whole_gain.astype(jnp.float32)).astype(jnp.bfloat16)
    gate = jnp.dot(
        normed, lax.all_gather(w_gate, "dp", axis=0, tiled=True), preferred_element_type=jnp.float32
    )
    up = jnp.dot(
        normed, lax.all_gather(w_up, "dp", axis=0, tiled=True), preferred_element_type=jnp.float32
    )
    hidden = (jax.nn.gelu(gate, approximate=True) * up).astype(jnp.bfloat16)
    token_out = jnp.dot(
        hidden, lax.all_gather(w_down, "dp", axis=1, tiled=True), preferred_element_type=jnp.float32
    )
    partial_value = pool_rows(token_out, p_count, length, q_count, q_length)
    summed = lax.psum_scatter(
        partial_value.astype(jnp.bfloat16), "mp", scatter_dimension=1, tiled=True
    ).astype(jnp.float32)
    pooled = (summed + pool_rows(token_rows, p_count, length, q_count, q_length)).astype(
        jnp.bfloat16
    )
    pooled_p = pooled[:p_count]
    pooled_q = pooled[p_count:]
    term_p = jnp.dot(pooled_p, old_head, preferred_element_type=jnp.float32)
    term_q = jnp.dot(pooled_q, new_head, preferred_element_type=jnp.float32)
    emb_p, query_part = (
        lax.psum_scatter(term_p, "mp", scatter_dimension=1, tiled=True),
        lax.psum_scatter(term_q, "mp", scatter_dimension=1, tiled=True),
    )
    refreshed = emb_p.astype(jnp.bfloat16)
    shard_count = lax.axis_size("section") * lax.axis_size("dp")
    request_count = q_count * k_count
    capacity = max(2, 2 * request_count // shard_count)
    flat_owner = neg_owner.reshape(-1)
    owner_hits = (flat_owner[:, None] == jnp.arange(shard_count, dtype=jnp.int32)[None, :]).astype(
        jnp.float32
    )
    request_order = jnp.arange(request_count, dtype=jnp.int32)
    earlier_rows = (request_order[:, None] > request_order[None, :]).astype(jnp.float32)
    seen_before = jnp.dot(earlier_rows, owner_hits, preferred_element_type=jnp.float32)
    slot_rank = jnp.sum(seen_before * owner_hits, axis=1).astype(jnp.int32)
    slot_index = flat_owner * capacity + slot_rank
    requests = (
        jnp.zeros((shard_count * capacity,), jnp.int32).at[slot_index].set(neg_row.reshape(-1))
    )
    requests = requests.reshape(shard_count, capacity)
    wanted_rows = lax.all_to_all(
        requests, ("section", "dp"), split_axis=0, concat_axis=0, tiled=True
    )
    found_rows = jnp.take(stale_index, wanted_rows.reshape(-1), axis=0)
    found_rows = found_rows.reshape(
        wanted_rows.shape[0], wanted_rows.shape[1], stale_index.shape[1]
    )
    fetched = lax.all_to_all(found_rows, ("section", "dp"), split_axis=0, concat_axis=0, tiled=True)
    negative = jnp.take(fetched.reshape(shard_count * capacity, -1), slot_index, axis=0)
    negative = negative.reshape(q_count, k_count, -1).astype(jnp.float32)
    positive_hits = (pos_slot[:, None] == jnp.arange(p_count, dtype=jnp.int32)[None, :]).astype(
        jnp.bfloat16
    )
    positive = jnp.dot(positive_hits, refreshed, preferred_element_type=jnp.float32)
    candidates = jnp.concatenate([positive[:, None, :], negative], axis=1)
    inner_part = jnp.einsum("qe,qje->qj", query_part, candidates, precision=lax.Precision.HIGHEST)
    cand_part = jnp.sum(candidates * candidates, axis=2)
    query_sq = jnp.sum(query_part * query_part, axis=1)
    inner, cand_sq, query_total = lax.psum((inner_part, cand_part, query_sq), "mp")
    cand_norm = jnp.sqrt(cand_sq + 1e-06)
    query_norm = jnp.sqrt(query_total + 1e-06)
    scores = inner / (cand_norm * query_norm[:, None] * TAU)
    exps = jnp.exp(scores)
    exp_total = jnp.sum(exps, axis=1)
    losses = jnp.log(exp_total) - scores[:, 0]
    first = (jnp.arange(k_count + 1) == 0).astype(jnp.float32)
    weights = (exps / exp_total[:, None] - first[None, :]) / (q_count * shard_count)
    direct = jnp.einsum(
        "qj,qje->qe",
        weights / (cand_norm * query_norm[:, None] * TAU),
        candidates,
        precision=lax.Precision.HIGHEST,
    )
    radial = jnp.sum(weights * scores, axis=1) / (query_norm * query_norm)
    query_grad = direct - radial[:, None] * query_part
    grad_whole = lax.all_gather(query_grad, "mp", axis=1, tiled=True)
    grad_term = jnp.dot(pooled_q.astype(jnp.float32).T, grad_whole, precision=lax.Precision.HIGHEST)
    grad_block = lax.psum_scatter(
        grad_term.astype(jnp.bfloat16), "dp", scatter_dimension=1, tiled=True
    )
    head_grad = lax.psum(grad_block, "section").astype(jnp.float32)
    return (refreshed, losses, head_grad)


def solution(mesh):
    placed = (
        P(("section", "dp"), None, "mp"),
        P(("section", "dp"), None, "mp"),
        P("mp"),
        P("dp", "mp"),
        P("dp", "mp"),
        P("mp", "dp"),
        P("mp", None),
        P("mp", None),
        P(("section", "dp"), "mp"),
        P(("section", "dp"), None),
        P(("section", "dp"), None),
        P(("section", "dp")),
    )
    return jax.shard_map(
        shards,
        mesh=mesh,
        in_specs=placed,
        out_specs=(P(("section", "dp"), "mp"), P(("section", "dp")), P("mp", "dp")),
        check_vma=False,
    )
```

profile of v0, /device:TPU:8, one launch (start us, length us, event | category | flops | bytes accessed | tf_op | source)
XLA Modules:
  0.0 769.5 jit_solution(10212196072936717279)
XLA Ops:
  7.2 1.7 pad_maximum_fusion
  11.0 0.8 reshape.151
  12.5 0.8 reshape.176
  14.3 0.8 all_to_all.9
  15.1 16.6 %all-to-all-start = ((s32[64,1,2]{2,1,0:T(1,128)}), s32[64,1,2]{2,1,0:T(1,128)S(1)}, u32[]{:S(2)}, u32[]{:S(2)}) async-start(s32[64,1,2]{2,1,0:T(1,128)} %bitcast.11), calls=%async_computation.1 | async-start | bytes 65536 | tf_op jit(solution)/shard_map/all_to_all | solution.py:88
  31.7 0.9 convert_reduce_fusion.1
  32.6 0.9 convert_reduce_fusion
  33.6 1.2 compare_and_fusion.1
  34.8 1.3 copy.33
  36.0 6.4 all-to-all-done
  44.8 0.8 broadcast_select_fusion
  45.5 6.2 all-to-all-start.1
  52.3 10.6 %all-gather = bf16[8,1,256]{2,1,0:T(2,128)(2,1)S(1)} all-gather(bf16[1,1,256]{2,1,0:T(2,128)(2,1)S(1)} %reshape.180), channel_id=1, replica_groups=mesh['section'=4,'dp'=16,'mp'=8] {'mp'}, dimensions={0}, use_global_device_ids=true | all-gather | bytes 4608 | tf_op jit(solution)/shard_map/all_gather | solution.py:41
  63.6 1.8 fusion
  65.4 96.5 %all-gather.9.cloned.1.call-done = bf16[2048,640]{1,0:T(8,128)(2,1)} async-done(((bf16[128,640]{1,0:T(8,128)(2,1)}), bf16[2048,640]{1,0:T(8,128)(2,1)}) %all-gather.9.cloned.1.call-update) | async-done | bytes 2621456 | tf_op jit(solution)/shard_map/all_gather | solution.py:47
  161.9 4.6 fusion.19
  166.5 105.6 %all-gather.11.cloned.1.call-done = bf16[2048,640]{1,0:T(8,128)(2,1)} async-done(((bf16[128,640]{1,0:T(8,128)(2,1)}), bf16[2048,640]{1,0:T(8,128)(2,1)}) %all-gather.11.cloned.1.call-update) | async-done | bytes 2621456 | tf_op jit(solution)/shard_map/all_gather | solution.py:50
  272.1 112.5 %all-gather.13.cloned.1.call-done = bf16[640,2048]{1,0:T(8,128)(2,1)} async-done(((bf16[640,128]{1,0:T(8,128)(2,1)}), bf16[640,2048]{1,0:T(8,128)(2,1)}) %all-gather.13.cloned.1.call-update) | async-done | bytes 2621456 | tf_op jit(solution)/shard_map/all_gather | solution.py:54
  384.6 6.4 fusion.12
  392.1 0.7 fusion.26
  392.8 29.8 %reduce-scatter.9.cloned.1.call-done = bf16[6,256]{1,0:T(8,128)(2,1)} async-done(((bf16[6,2048]{1,0:T(8,128)(2,1)}), bf16[6,256]{1,0:T(8,128)(2,1)}) %reduce-scatter.9.cloned.1.call-update) | async-done | bytes 3088 | tf_op jit(solution)/shard_map/reduce_scatter | solution.py:57
  423.3 2.0 convolution_bitcast_fusion
  425.4 1.1 convolution_bitcast_fusion.1
  426.6 33.9 %reduce-scatter.13.cloned.1.call-done = f32[96,2]{1,0:T(8,128)} async-done(((f32[768,2]{1,0:T(8,128)}), f32[96,2]{1,0:T(8,128)}) %reduce-scatter.13.cloned.1.call-update) | async-done | bytes 784
  460.5 0.9 copy.41
  461.6 36.6 %reduce-scatter.15.cloned.1.call-done = f32[96,4]{1,0:T(8,128)} async-done(((f32[768,4]{1,0:T(8,128)}), f32[96,4]{1,0:T(8,128)}) %reduce-scatter.15.cloned.1.call-update) | async-done | bytes 1552
  498.3 0.9 copy.43
  499.4 13.1 %all-reduce = (f32[4,9]{1,0:T(4,128)S(1)}, f32[4,9]{1,0:T(4,128)S(1)}, f32[4]{0:T(128)S(1)}) all-reduce(f32[4,9]{1,0:T(4,128)S(1)} %bitcast.70, f32[4,9]{1,0:T(4,128)S(1)} %fusion.24, f32[4]{0:T(128)S(1)} %multiply_reduce_fusion.1), channel_id=1, replica_groups=mesh['section'=4,'dp'=16,'mp'=8] {'mp'}, use_global_device_ids=true, to_apply=%region_10.11 | all-reduce | flops 76 | bytes 608 | tf_op jit(solution)/shard_map/psum | solution.py:106
  513.2 11.2 %all-gather.1 = f32[8,96,4]{1,2,0:T(4,128)S(1)} all-gather(f32[1,96,4]{1,2,0:T(4,128)S(1)} %subtract_bitcast_fusion), channel_id=1, replica_groups=mesh['section'=4,'dp'=16,'mp'=8] {'mp'}, dimensions={0}, use_global_device_ids=true | all-gather | bytes 13824 | tf_op jit(solution)/shard_map/all_gather | solution.py:123
  524.5 1.3 convolution_convert_fusion
  526.4 218.2 %reduce-scatter.11.cloned.1.call-done = bf16[256,48]{0,1:T(8,128)(2,1)} async-done(((bf16[256,768]{0,1:T(8,128)(2,1)}), bf16[256,48]{0,1:T(8,128)(2,1)}) %reduce-scatter.11.cloned.1.call-update) | async-done | bytes 24592 | tf_op jit(solution)/shard_map/reduce_scatter | solution.py:125
  744.6 17.3 %psum.31 = bf16[256,48]{0,1:T(8,128)(2,1)S(1)} all-reduce(bf16[256,48]{0,1:T(8,128)(2,1)} %reduce-scatter.11.cloned.1.call-done), channel_id=1, replica_groups=mesh['section'=4,'dp'=16,'mp'=8] {'section'}, use_global_device_ids=true, to_apply=%region_18.19 | all-reduce | flops 12288 | bytes 49152 | tf_op jit(solution)/shard_map/psum | solution.py:128
  (77 shorter events, 11.8 us)
Async XLA Ops:
  7.2 418.2 %copy-start = (bf16[256,768]{1,0:T(8,128)(2,1)S(1)}, bf16[256,768]{1,0:T(8,128)(2,1)}, u32[]{:S(2)}) copy-start(bf16[256,768]{1,0:T(8,128)(2,1)} %param.19) | copy-start | bytes 1179652
  7.2 45.1 %copy-start.5 = (bf16[256]{0:T(256)(128)(2,1)S(1)}, bf16[256]{0:T(256)(128)(2,1)}, u32[]{:S(2)}) copy-start(bf16[256]{0:T(256)(128)(2,1)} %param.14) | copy-start | bytes 1540
  7.2 56.4 %all-gather.7.cloned.1.call-start = ((), (), s32[]{:S(2)}) async-start(), calls=%async_computation.6 | async-start | bytes 1769472 | tf_op jit(solution)/shard_map/all_gather | solution.py:40
  8.9 153.0 %all-gather.9.cloned.1.call-start = ((), (), s32[]{:S(2)}) async-start(), calls=%async_computation.7 | async-start | bytes 2785280 | tf_op jit(solution)/shard_map/all_gather | solution.py:47
  9.7 262.4 %all-gather.11.cloned.1.call-start = ((), (), s32[]{:S(2)}) async-start(), calls=%async_computation.8 | async-start | bytes 2785280 | tf_op jit(solution)/shard_map/all_gather | solution.py:50
  10.4 374.2 %all-gather.13.cloned.1.call-start = ((), (), s32[]{:S(2)}) async-start(), calls=%async_computation.9 | async-start | bytes 2785280 | tf_op jit(solution)/shard_map/all_gather | solution.py:54
  15.1 27.4 %all-to-all-start = ((s32[64,1,2]{2,1,0:T(1,128)}), s32[64,1,2]{2,1,0:T(1,128)S(1)}, u32[]{:S(2)}, u32[]{:S(2)}) async-start(s32[64,1,2]{2,1,0:T(1,128)} %bitcast.11), calls=%async_computation.1 | async-start | bytes 65536 | tf_op jit(solution)/shard_map/all_to_all | solution.py:88
  45.5 17.4 %all-to-all-start.1 = ((bf16[64,2,96]{2,1,0:T(2,128)(2,1)}), bf16[64,2,96]{2,1,0:T(2,128)(2,1)S(1)}, u32[]{:S(2)}, u32[]{:S(2)}) async-start(bf16[64,2,96]{2,1,0:T(2,128)(2,1)} %broadcast_select_fusion), calls=%async_computation.2 | async-start | bytes 65536 | tf_op jit(solution)/shard_map/all_to_all | solution.py:95
  51.7 370.9 %reduce-scatter.9.cloned.1.call-start = ((), (), s32[]{:S(2)}) async-start(), calls=%async_computation.10 | async-start | bytes 36864 | tf_op jit(solution)/shard_map/reduce_scatter | solution.py:57
  62.9 209.2 %copy-start.1 = (f32[8,1,256]{2,1,0:T(1,128)}, f32[8,1,256]{2,1,0:T(1,128)S(1)}, u32[]{:S(2)}) copy-start(f32[8,1,256]{2,1,0:T(1,128)S(1)} %convert_element_type.85) | copy-start | bytes 24580
  65.4 101.1 %copy-start.2 = (f32[384]{0:T(512)}, f32[384]{0:T(512)S(1)}, u32[]{:S(2)}) copy-start(f32[384]{0:T(512)S(1)} %add_rsqrt_fusion) | copy-start | bytes 4612
  391.3 70.0 %copy-start.6 = (s32[4]{0:T(128)S(1)}, s32[4]{0:T(128)}, u32[]{:S(2)}) copy-start(s32[4]{0:T(128)} %param.23) | copy-start | bytes 52
  391.3 121.4 %copy-start.4 = (f32[9]{0:T(128)S(1)}, f32[9]{0:T(128)}, u32[]{:S(2)}) copy-start(f32[9]{0:T(128)} %compare_convert_fusion) | copy-start | bytes 112
  392.0 68.5 %reduce-scatter.13.cloned.1.call-start = ((), (), s32[]{:S(2)}) async-start(), calls=%async_computation.12 | async-start | bytes 442368
  425.4 72.9 %reduce-scatter.15.cloned.1.call-start = ((), (), s32[]{:S(2)}) async-start(), calls=%async_computation.13 | async-start | bytes 442368
  426.5 318.1 %reduce-scatter.11.cloned.1.call-start = ((), (), s32[]{:S(2)}) async-start(), calls=%async_computation.11 | async-start | bytes 417792 | tf_op jit(solution)/shard_map/reduce_scatter | solution.py:125
  461.3 301.3 %copy-start.3 = (bf16[2,96]{1,0:T(2,128)(2,1)}, bf16[2,96]{1,0:T(2,128)(2,1)S(1)}, u32[]{:S(2)}) copy-start(bf16[2,96]{1,0:T(2,128)(2,1)S(1)} %copy.41) | copy-start | bytes 1156
Sparse Core Ops, SparseCore 0:
  10.1 35.0 all-gather.6
  48.4 113.4 all-gather.8
  165.1 106.9 all-gather.10
  275.0 109.5 all-gather.12
  392.1 30.4 reduce-scatter.8
  425.5 34.9 reduce-scatter.12
  463.3 34.9 reduce-scatter.14
  525.9 218.6 reduce-scatter.10
where the time goes:
time: 771 us; the launch traced here: 769 us
  waiting for transfers between devices  642 us (83%)
  blocking collectives  52.3 us (7%)
  starting transfers between devices  23.1 us (3%)
  matrix products  16.2 us (2%)
  between operations  14.4 us (2%)
  other arithmetic  13.4 us (2%)
  local copies, waits for them, and re-layouts  8.51 us (1%)
    reduce_scatter x1, waiting for transfers between devices, shards(): lax.psum_scatter(grad_term.astype(jnp.bfloat16), 'dp', scatter_dimension=...  218 us
    all_gather x1, waiting for transfers between devices, shards(): lax.all_gather(w_down, 'dp', axis=1, tiled=True)  113 us
    all_gather x1, waiting for transfers between devices, shards(): lax.all_gather(w_up, 'dp', axis=0, tiled=True)  106 us
    all_gather x1, waiting for transfers between devices, shards(): lax.all_gather(w_gate, 'dp', axis=0, tiled=True)  96.5 us
    unnamed x10, waiting for transfers between devices  72.5 us
    reduce_scatter x1, waiting for transfers between devices, shards(): lax.psum_scatter(partial_value.astype(jnp.bfloat16), 'mp', scatter_dimens...  29.8 us
    psum x1, blocking collectives, shards(): head_grad = lax.psum(grad_block, 'section').astype(jnp.float32)  17.3 us
    all_to_all x1, starting transfers between devices, shards(): lax.all_to_all(requests, ('section', 'dp'), split_axis=0, concat_axis=0,...  16.6 us
  transfers between devices with their start and end apart: 10, of which 8 were waited for; matrix products, arithmetic and copies ran while one was open for 3% of the time, Pallas kernels for 0%

commit v1 on v0

v1 whole, which is shorter than its diff:
```python
import functools
import math

import jax
import jax.numpy as jnp
import numpy as np
from jax import lax
from jax.experimental import pallas as pl
from jax.experimental.pallas import tpu as pltpu
from jax.sharding import PartitionSpec as P

TAU = 0.02
MIB = 1024 * 1024


def params(mib=8):
    return pltpu.CompilerParams(vmem_limit_bytes=mib * MIB)


def in_hbm():
    return pl.BlockSpec(memory_space=pltpu.HBM)


def whole():
    return pl.BlockSpec(memory_space=pltpu.VMEM)


def gelu(v):
    c = math.sqrt(2.0 / math.pi)
    return 0.5 * v * (1.0 + jnp.tanh(c * (v + 0.044715 * (v * v * v))))


def mp_move(block, step, flip):
    n = lax.axis_size("mp") // 2
    perm = [(x * 2 + c, ((x + step) % n) * 2 + (c ^ flip)) for x in range(n) for c in range(2)]
    return lax.ppermute(block, "mp", perm)


def mate_move(block):
    return lax.ppermute(block, "section", [(s, s ^ 1) for s in range(lax.axis_size("section"))])


def half_move(block):
    sections, shards_n = lax.axis_size("section"), lax.axis_size("dp")
    turn = sections // 2 if (sections // 2) % 2 == 0 else 0
    perm = [
        (s * shards_n + d, ((s + turn) % sections) * shards_n + (d + shards_n // 2) % shards_n)
        for s in range(sections)
        for d in range(shards_n)
    ]
    return lax.ppermute(block, ("section", "dp"), perm)


def along_y(block):
    n = lax.axis_size("dp") // 2
    groups = [[h * n + y for y in range(n)] for h in range(2)]
    return lax.all_gather(block, "dp", axis=0, axis_index_groups=groups, tiled=True)


def x_ring(block, rows, wanted):
    low, high, wanted = lax.optimization_barrier((mp_move(block, 1, 0), mp_move(block, -1, 0), wanted))
    top, bottom = mp_move(low[:rows], 1, 0), mp_move(high[rows:], -1, 0)
    mine = jnp.concatenate([block, low, high, top, bottom], axis=0)
    return mine, mp_move(mine, 0, 1), wanted


def cut_kernel(gate_in, up_in, down_in, own, other, gate, up, down, sems):
    fetches = [
        pltpu.make_async_copy(source, target, sems.at[k])
        for k, (source, target) in enumerate(((gate_in, gate), (up_in, up), (down_in, down)))
    ]
    for fetch in fetches:
        fetch.start()
    units = gate.shape[1] // 2
    cut = units // 128 * 128
    gap = own.shape[1] - 3 * units
    own[:, 3 * units :] = jnp.zeros((own.shape[0], gap), own.dtype)
    other[:, :gap] = jnp.zeros((own.shape[0], gap), own.dtype)
    for fetch in fetches:
        fetch.wait()
    for half in range(2):

        @pl.when(lax.axis_index("section") % 2 == half)
        def _(first=half * units):
            turned = down[first : first + units, :].astype(jnp.float32).T.astype(jnp.bfloat16)
            own[:, 2 * units : 3 * units] = turned
            other[:, gap : gap + units] = turned
            for out, base in ((own, 0), (other, gap + units)):
                out[:, base : base + cut] = gate[:, first : first + cut]
                out[:, base + cut : base + units] = gate[:, first + cut : first + units]
                out[:, base + units : base + 2 * units - cut] = up[:, first + cut : first + units]
                out[:, base + 2 * units - cut : base + 2 * units] = up[:, first : first + cut]


def norm_kernel(nx, rows, near, far, out):
    step_rows = 32
    width = near.shape[1]
    x, c = lax.axis_index("mp") // 2, lax.axis_index("mp") % 2
    sides = []
    for ref, core in ((near, c), (far, 1 - c)):
        for k, step in enumerate((0, -1, 1, 2)):
            place = lax.rem(x + step + nx, nx) * 2 + core
            at = pl.ds(pl.multiple_of(place * width, width), width)
            sides.append((ref, k * (rows + 16), at))
    gains = [ref[first + rows : first + rows + 1, :].astype(jnp.float32) for ref, first, _ in sides]

    def body(i, carry):
        start = i * step_rows
        total = jnp.zeros((step_rows, width), jnp.float32)
        for ref, first, _ in sides:
            v = ref[pl.ds(pl.multiple_of(first + start, 16), step_rows), :].astype(jnp.float32)
            total = total + v * v
        scale = lax.rsqrt(jnp.sum(total, axis=1, keepdims=True) / (len(sides) * width) + 1e-06)
        target = pl.ds(pl.multiple_of(start, step_rows), step_rows)
        for (ref, first, at), gain in zip(sides, gains):
            v = ref[pl.ds(pl.multiple_of(first + start, 16), step_rows), :].astype(jnp.float32)
            out[target, at] = (v * scale * gain).astype(jnp.bfloat16)
        return carry

    lax.fori_loop(0, rows // step_rows, body, 0)


def marks(owner, shard_n):
    count = owner.shape[1]
    hit = lax.broadcasted_iota(jnp.int32, (shard_n, count), 0) == owner
    place = lax.broadcasted_iota(jnp.int32, (shard_n, count), 1).astype(jnp.float32)
    first = jnp.min(jnp.where(hit, place, 2.0 * count), axis=1, keepdims=True)
    last = jnp.max(jnp.where(hit, place, -1.0), axis=1, keepdims=True)
    return jnp.where(hit & (place == first), 1.0, 0.0), jnp.where(hit & (place == last) & (last > first), 1.0, 0.0)


def ask_kernel(owner, row, out):
    first, second = marks(owner[...], out.shape[0])
    wanted = row[...].astype(jnp.float32)
    one = jnp.sum(first * wanted, axis=1, keepdims=True)
    two = jnp.sum(second * wanted, axis=1, keepdims=True)
    lane = lax.broadcasted_iota(jnp.int32, out.shape, 1)
    out[...] = jnp.where(lane == 0, one, jnp.where(lane == 1, two, 0.0)).astype(jnp.int32)


def find_kernel(wanted, index, out):
    width, count = index.shape
    row = lax.broadcasted_iota(jnp.int32, (wanted.shape[0], count), 1)
    gap = jnp.zeros((wanted.shape[0], 128 - width), jnp.float32)
    for slot in range(2):
        hit = jnp.where(row == wanted[:, slot : slot + 1], 1.0, 0.0).astype(jnp.bfloat16)
        found = lax.dot_general(hit, index[...], (((1,), (1,)), ((), ())), preferred_element_type=jnp.float32)
        out[:, slot, :] = jnp.concatenate([found, gap], axis=1)


def hidden_kernel(units, normed, pool, weights, out, up_w, down_w, hidden, sems):
    h = lax.axis_index("dp") // (lax.axis_size("dp") // 2)
    rows = weights.shape[0]
    up_copies = [
        pltpu.make_async_copy(
            weights.at[:, pl.ds(4 * units * side, 2 * units)],
            up_w.at[pl.ds(pl.multiple_of((1 - h if side else h) * rows, rows), rows), :],
            sems.at[side],
        )
        for side in range(2)
    ]
    down_copy = pltpu.make_async_copy(weights.at[:, pl.ds(2 * units, 2 * units)], down_w, sems.at[2])
    for copy in up_copies + [down_copy]:
        copy.start()
    for copy in up_copies:
        copy.wait()
    cut = units // 128 * 128
    tail = units - cut
    both = jnp.dot(normed[...], up_w[...], preferred_element_type=jnp.float32)
    hidden[:, :cut] = (gelu(both[:, :cut]) * both[:, 2 * units - cut :]).astype(jnp.bfloat16)
    if tail:
        edge = both[:, cut : cut + 2 * tail]
        hidden[:, cut : cut + 2 * tail] = (gelu(edge) * pltpu.roll(edge, tail, 1)).astype(jnp.bfloat16)
    value = jnp.dot(pool[...], hidden[...], preferred_element_type=jnp.float32)[:, :units]
    high = value.astype(jnp.bfloat16).astype(jnp.float32)
    low = value - high
    both_parts = jnp.concatenate([high, low], axis=0)
    none = jnp.zeros_like(both_parts)
    own_rows = jnp.concatenate([both_parts, none], axis=1)
    other_rows = jnp.concatenate([none, both_parts], axis=1)
    sides = jnp.concatenate([own_rows, other_rows], axis=0).astype(jnp.bfloat16)
    down_copy.wait()
    total = lax.dot_general(sides, down_w[...], (((1,), (1,)), ((), ())), preferred_element_type=jnp.float32)
    mp_n, _, width = out.shape[0] // 2, out.shape[1], out.shape[2]
    for side in range(2):
        sums = total[side * 32 : side * 32 + 16] + total[side * 32 + 16 : side * 32 + 32]
        for mate in range(2):
            base = mate * mp_n + (1 - h if side else h) * (mp_n // 2)
            for k in range(mp_n // 2):
                out[base + k] = sums[mate * 8 : mate * 8 + 8, k * width : (k + 1) * width]


def head_kernel(p_count, lanes, parts, residual, old_head, new_head, owner, fetched, pooled_out, message, old, new, sems):
    fetches = [pltpu.make_async_copy(old_head, old, sems.at[0]), pltpu.make_async_copy(new_head, new, sems.at[1])]
    for fetch in fetches:
        fetch.start()
    total = residual[...]
    for k in range(parts.shape[0]):
        total = total + parts[k]
    pooled = total.astype(jnp.bfloat16)
    pooled_out[...] = pooled
    for fetch in fetches:
        fetch.wait()
    of_old = jnp.dot(pooled, old[...], preferred_element_type=jnp.float32)
    of_new = jnp.dot(pooled, new[...], preferred_element_type=jnp.float32)
    row = lax.broadcasted_iota(jnp.int32, of_old.shape, 0)
    term = jnp.where(row < p_count, of_old, of_new)
    gap = jnp.zeros((term.shape[0], 128 - lanes), jnp.float32)
    pieces = [
        jnp.concatenate([term[:, k * lanes : (k + 1) * lanes], gap], axis=1) for k in range(term.shape[1] // lanes)
    ]
    negatives = jnp.zeros((owner.shape[1], 128), jnp.float32)
    for slot, mark in enumerate(marks(owner[...], fetched.shape[0])):
        negatives = negatives + lax.dot_general(
            mark.astype(jnp.bfloat16),
            fetched[:, slot, :].astype(jnp.bfloat16),
            (((0,), (0,)), ((), ())),
            preferred_element_type=jnp.float32,
        )
    rows = jnp.concatenate(pieces + [negatives], axis=0).astype(jnp.bfloat16)
    for copy in range(message.shape[0]):
        message[copy] = rows


def loss_kernel(p_count, q_count, queries, slot, messages, pooled, fresh_out, loss_out, message, held):
    n = messages.shape[0]
    rows = messages[...].astype(jnp.float32)
    total = rows[0, : n * 8]
    for k in range(1, n):
        total = total + rows[k, : n * 8]
    emb = jnp.concatenate([total[a * 8 : (a + 1) * 8] for a in range(n)], axis=1)
    fresh = emb[:p_count].astype(jnp.bfloat16).astype(jnp.float32)
    held[:p_count] = fresh
    own = held[:, pl.ds(pl.multiple_of(lax.axis_index("mp") * 128, 128), 128)]
    fresh_out[...] = own[:p_count, : fresh_out.shape[1]].astype(jnp.bfloat16)
    k_count = (rows.shape[1] - n * 8) // q_count
    loss_rows, grad_rows = [], []
    for q in range(q_count):
        query = emb[p_count + q : p_count + q + 1]
        positive = fresh[0:1]
        for k in range(1, p_count):
            positive = jnp.where(slot[q] == k, fresh[k : k + 1], positive)
        tiles = [rows[a, n * 8 + q * k_count : n * 8 + (q + 1) * k_count] for a in range(n)]
        inner = jnp.zeros((k_count, 128), jnp.float32)
        square = inner
        for a in range(n):
            inner = inner + tiles[a] * query[:, a * 128 : (a + 1) * 128]
            square = square + tiles[a] * tiles[a]
        inner = jnp.sum(inner, axis=1, keepdims=True)
        square = jnp.sum(square, axis=1, keepdims=True)
        query_norm = jnp.sqrt(jnp.sum(query * query, axis=1, keepdims=True) + 1e-06)
        below = jnp.sqrt(square + 1e-06) * query_norm * TAU
        scores = inner / below
        below_p = jnp.sqrt(jnp.sum(positive * positive, axis=1, keepdims=True) + 1e-06) * query_norm * TAU
        score_p = jnp.sum(positive * query, axis=1, keepdims=True) / below_p
        exps, exp_p = jnp.exp(scores), jnp.exp(score_p)
        total = jnp.sum(exps, axis=0, keepdims=True) + exp_p
        loss_rows.append(jnp.log(total) - score_p)
        weights = exps / total / queries
        weight_p = (exp_p / total - 1.0) / queries
        radial = (jnp.sum(weights * scores, axis=0, keepdims=True) + weight_p * score_p) / (query_norm * query_norm)
        share = weights / below
        direct = jnp.concatenate([jnp.sum(share * tile, axis=0, keepdims=True) for tile in tiles], axis=1)
        grad_rows.append(direct + (weight_p / below_p) * positive - radial * query)
    losses = jnp.concatenate(loss_rows, axis=0)
    loss_out[...] = jnp.broadcast_to(losses, loss_out.shape)
    grads = jnp.concatenate(grad_rows, axis=0).astype(jnp.bfloat16)
    width = pooled.shape[1]
    features = pooled[...].astype(jnp.float32)[p_count : p_count + q_count].astype(jnp.bfloat16)
    columns = lax.axis_size("dp")
    for k in range(message.shape[0]):
        at = k % columns * n // columns * 128
        message[k, :, :width] = features
        message[k, :, width:] = grads[:, at : at + 128]


def grad_kernel(width, arrived, out):
    block = out.shape[0]
    both = lax.dot_general(
        arrived[:, width:], arrived[:, :width], (((0,), (0,)), ((), ())), preferred_element_type=jnp.float32
    )
    shared = lax.axis_size("dp") // lax.axis_size("mp")
    chosen = both[:block]
    for k in range(1, shared):
        chosen = jnp.where(lax.axis_index("dp") % shared == k, both[k * block : (k + 1) * block], chosen)
    out[...] = chosen


def shards(
    passage_tokens,
    query_tokens,
    norm_gain,
    w_gate,
    w_up,
    w_down,
    old_head,
    new_head,
    stale_index,
    neg_owner,
    neg_row,
    pos_slot,
):
    p_count, length, width = passage_tokens.shape
    q_count, q_length, _ = query_tokens.shape
    k_count = neg_owner.shape[1]
    embed = old_head.shape[1]
    sections = lax.axis_size("section")
    shard_count = sections * lax.axis_size("dp")
    mp_n = lax.axis_size("mp")
    features = width * mp_n
    f32, bf16 = jnp.float32, jnp.bfloat16

    units = w_gate.shape[1] // 2
    cut = units // 128 * 128
    wide = -(-3 * units // 128) * 128
    own, other = pl.pallas_call(
        cut_kernel,
        out_shape=[jax.ShapeDtypeStruct((w_gate.shape[0], wide), bf16)] * 2,
        in_specs=[in_hbm()] * 3,
        out_specs=[whole()] * 2,
        scratch_shapes=[pltpu.VMEM(w.shape, bf16) for w in (w_gate, w_up, w_down)] + [pltpu.SemaphoreType.DMA((3,))],
        compiler_params=params(56),
        name="cut",
    )(w_gate, w_up, w_down)
    other = half_move(other)

    rows = p_count * length + q_count * q_length
    gain_rows = jnp.broadcast_to(norm_gain[None, :], (16, width))
    tokens = jnp.concatenate([passage_tokens.reshape(-1, width), query_tokens.reshape(-1, width)], axis=0)
    other, mate_tokens = lax.optimization_barrier((other, mate_move(tokens)))

    edge = wide - 128
    merged = jnp.concatenate([own[:, :edge], own[:, edge:] + other[:, :128], other[:, 128:]], axis=1)
    weights = along_y(merged)

    flip = lax.axis_index("section") % 2 == 1
    tokens = jnp.concatenate(
        [jnp.where(flip, mate_tokens, tokens), jnp.where(flip, tokens, mate_tokens), gain_rows], axis=0
    )
    request_count = q_count * k_count
    owner = neg_owner.reshape(1, request_count)
    requests = pl.pallas_call(
        ask_kernel,
        out_shape=jax.ShapeDtypeStruct((shard_count, 128), jnp.int32),
        in_specs=[whole()] * 2,
        out_specs=whole(),
        compiler_params=params(),
        name="ask",
    )(owner, neg_row.reshape(1, request_count))
    wanted = lax.all_to_all(requests, ("section", "dp"), 0, 0, tiled=True)
    near, far, wanted = x_ring(tokens, rows, wanted)
    found = pl.pallas_call(
        find_kernel,
        out_shape=jax.ShapeDtypeStruct((shard_count, 2, 128), f32),
        in_specs=[whole()] * 2,
        out_specs=whole(),
        compiler_params=params(),
        name="find",
    )(wanted, stale_index.T)
    fetched = lax.all_to_all(found, ("section", "dp"), 0, 0, tiled=True)

    normed = pl.pallas_call(
        functools.partial(norm_kernel, mp_n // 2, 2 * rows),
        out_shape=jax.ShapeDtypeStruct((2 * rows, features), bf16),
        in_specs=[whole()] * 2,
        out_specs=whole(),
        compiler_params=params(16),
        name="norm",
    )(near, far)

    pool = np.zeros((16, 2 * rows), np.float32)
    for mate in range(2):
        base = mate * rows
        for k in range(p_count):
            pool[mate * 8 + k, base + k * length : base + (k + 1) * length] = 1.0 / length
        base += p_count * length
        for k in range(q_count):
            pool[mate * 8 + p_count + k, base + k * q_length : base + (k + 1) * q_length] = 1.0 / q_length
    padded = cut + 2 * (units - cut)
    parts = pl.pallas_call(
        functools.partial(hidden_kernel, units),
        out_shape=jax.ShapeDtypeStruct((2 * mp_n, 8, width), f32),
        in_specs=[whole(), whole(), in_hbm()],
        out_specs=whole(),
        scratch_shapes=[
            pltpu.VMEM((features, 2 * units), bf16),
            pltpu.VMEM((features // 2, 2 * units), bf16),
            pltpu.VMEM((2 * rows, padded), bf16),
            pltpu.SemaphoreType.DMA((3,)),
        ],
        compiler_params=params(52),
        name="hidden",
    )(normed, jnp.asarray(pool, bf16), weights)

    groups = [[s * mp_n + m for s in (p, p + 1) for m in range(mp_n)] for p in range(0, sections, 2)]
    parts = lax.all_to_all(
        parts, ("section", "mp"), split_axis=0, concat_axis=0, axis_index_groups=groups, tiled=True
    )
    residual = jnp.concatenate(
        [
            jnp.sum(passage_tokens.astype(f32), axis=1) / length,
            jnp.sum(query_tokens.astype(f32), axis=1) / q_length,
            jnp.zeros((8 - p_count - q_count, width), f32),
        ],
        axis=0,
    )
    own_width = embed // mp_n
    message_rows = 8 * mp_n + request_count
    pooled, message = pl.pallas_call(
        functools.partial(head_kernel, p_count, own_width),
        out_shape=[
            jax.ShapeDtypeStruct((8, width), bf16),
            jax.ShapeDtypeStruct((mp_n, message_rows, 128), bf16),
        ],
        in_specs=[whole()] * 2 + [in_hbm()] * 2 + [whole()] * 2,
        out_specs=[whole()] * 2,
        scratch_shapes=[
            pltpu.VMEM((width, embed), bf16),
            pltpu.VMEM((width, embed), bf16),
            pltpu.SemaphoreType.DMA((2,)),
        ],
        compiler_params=params(),
        name="head",
    )(parts, residual, old_head, new_head, owner, fetched)
    messages = lax.all_to_all(message, "mp", 0, 0, tiled=True)

    refreshed, losses, message = pl.pallas_call(
        functools.partial(loss_kernel, p_count, q_count, q_count * shard_count),
        out_shape=[
            jax.ShapeDtypeStruct((p_count, own_width), bf16),
            jax.ShapeDtypeStruct((q_count, 128), f32),
            jax.ShapeDtypeStruct((shard_count, q_count, width + 128), bf16),
        ],
        in_specs=[pl.BlockSpec(memory_space=pltpu.SMEM)] + [whole()] * 2,
        out_specs=[whole()] * 3,
        scratch_shapes=[pltpu.VMEM((8, 128 * mp_n), f32)],
        compiler_params=params(),
        name="loss",
    )(pos_slot, messages, pooled)

    arrived = lax.all_to_all(message, ("section", "dp"), 0, 0, tiled=True)
    head_grad = pl.pallas_call(
        functools.partial(grad_kernel, width),
        out_shape=jax.ShapeDtypeStruct((embed // lax.axis_size("dp"), width), f32),
        in_specs=[whole()],
        out_specs=whole(),
        compiler_params=params(),
        name="grad",
    )(arrived.reshape(-1, width + 128)).T
    return (refreshed, losses[:, 0], head_grad)


def solution(mesh):
    placed = (
        P(("section", "dp"), None, "mp"),
        P(("section", "dp"), None, "mp"),
        P("mp"),
        P("dp", "mp"),
        P("dp", "mp"),
        P("mp", "dp"),
        P("mp", None),
        P("mp", None),
        P(("section", "dp"), "mp"),
        P(("section", "dp"), None),
        P(("section", "dp"), None),
        P(("section", "dp")),
    )
    return jax.shard_map(
        shards,
        mesh=mesh,
        in_specs=placed,
        out_specs=(P(("section", "dp"), "mp"), P(("section", "dp")), P("mp", "dp")),
        check_vma=False,
    )
```

time: 771 us -> 155 us (0.20)
  waiting for transfers between devices: 642 us -> 41.1 us
  blocking collectives: 52.3 us -> 9.23 us
  starting transfers between devices: 23.1 us -> 64 us
  Pallas kernels: 0 us -> 18.7 us
  matrix products: 16.2 us -> 0 us
  other arithmetic: 13.4 us -> 2.82 us
    all_gather x4 -> x1, waiting for transfers between devices: 315 us -> 0.01 us  [along_y(): lax.all_gather(block, 'dp', axis=0, axis_index_groups=groups, tiled=True)]
    reduce_scatter x2 -> x0, waiting for transfers between devices: 248 us -> none  [the longest x1 218 us: shards(): lax.psum_scatter(grad_term.astype(jnp.bfloat16), 'dp', scatter_dimension=...]
    unnamed x10 -> x1, waiting for transfers between devices: 72.5 us -> 0.02 us
    ppermute x0 -> x7, starting transfers between devices: none -> 30.6 us  [the longest x5 16.2 us: mp_move(): return lax.ppermute(block, 'mp', perm)]
    psum x2 -> x0, blocking collectives: 30.4 us -> none  [the longest x1 17.3 us: shards(): head_grad = lax.psum(grad_block, 'section').astype(jnp.float32)]
    all_to_all x2 -> x4, waiting for transfers between devices: 6.4 us -> 29.5 us  [the longest x1 12 us: shards(): arrived = lax.all_to_all(message, ('section', 'dp'), 0, 0, tiled=True)]
    all_gather x2 -> x0, blocking collectives: 21.8 us -> none  [the longest x1 11.2 us: shards(): grad_whole = lax.all_gather(query_grad, 'mp', axis=1, tiled=True)]
    pallas_call x0 -> x8, Pallas kernels: none -> 18.7 us  [the longest x1 8.41 us: shards(): pl.pallas_call(functools.partial(hidden_kernel, units), out_shape=jax.Sha...]
  transfers between devices with their start and end apart: 10 -> 12, of which waited for: 8 -> 6; matrix products, arithmetic and copies ran while one was open for 3% -> 2% of each run, Pallas kernels for 0% -> 9%
where the time goes in v1:
time: 155 us; the launch traced here: 154 us
  starting transfers between devices  64 us (41%)
  waiting for transfers between devices  41.1 us (27%)
  Pallas kernels  18.7 us (12%)
  between operations  14.4 us (9%)
  blocking collectives  9.23 us (6%)
  local copies, waits for them, and re-layouts  3.73 us (2%)
  other arithmetic  2.82 us (2%)
    ppermute x5, starting transfers between devices, mp_move(): return lax.ppermute(block, 'mp', perm)  16.2 us
    all_to_all x1, waiting for transfers between devices, shards(): arrived = lax.all_to_all(message, ('section', 'dp'), 0, 0, tiled=True)  12 us
    all_to_all x1, starting transfers between devices, shards(): arrived = lax.all_to_all(message, ('section', 'dp'), 0, 0, tiled=True)  11.7 us
    all_to_all x1, waiting for transfers between devices, shards(): wanted = lax.all_to_all(requests, ('section', 'dp'), 0, 0, tiled=True)  11 us
    ppermute x1, starting transfers between devices, half_move(): return lax.ppermute(block, ('section', 'dp'), perm)  10.9 us
    all_to_all x1, starting transfers between devices, shards(): wanted = lax.all_to_all(requests, ('section', 'dp'), 0, 0, tiled=True)  10 us
    all_to_all x1, blocking collectives, shards(): messages = lax.all_to_all(message, 'mp', 0, 0, tiled=True)  9.23 us
    ppermute x1, waiting for transfers between devices, mate_move(): lax.ppermute(block, 'section', [(s, s ^ 1) for s in range(lax.axis_size('...  8.41 us
  transfers between devices with their start and end apart: 12, of which 6 were waited for; matrix products, arithmetic and copies ran while one was open for 2% of the time, Pallas kernels for 9%

profile of v1, /device:TPU:8, one launch (start us, length us, event | category | flops | bytes accessed | tf_op | source)
XLA Modules:
  0.0 153.9 jit_solution(4192314336331381348)
XLA Ops:
  7.2 2.1 %cut.1 = (bf16[128,1024]{1,0:T(8,128)(2,1)}, bf16[128,1024]{1,0:T(8,128)(2,1)}) custom-call(bf16[128,640]{1,0:T(8,128)(2,1)} %gate_in.1, bf16[128,640]{1,0:T(8,128)(2,1)} %up_in.1, bf16[640,128]{1,0:T(8,128)(2,1)} %down_in.1), custom_call_target="tpu_custom_call" | custom-call | tf_op jit(solution)/shard_map/cut/pallas_call | solution.py:316
  9.4 10.9 %collective-permute-start = (bf16[128,1024]{1,0:T(8,128)(2,1)}, bf16[128,1024]{1,0:T(8,128)(2,1)S(1)}, u32[]{:S(2)}, u32[]{:S(2)}) collective-permute-start(bf16[128,1024]{1,0:T(8,128)(2,1)} %get-tuple-element.15), channel_id=1, source_target_pairs={{0,320},{8,328},{16,336},{24,344},{32,352},{40,360},{48,368},{56,3... | collective-permute-start | bytes 786440 | tf_op jit(solution)/shard_map/ppermute | solution.py:51
  20.3 1.0 pad_maximum_fusion.2
  21.3 3.5 %collective-permute-start.1 = (bf16[384,256]{1,0:T(8,128)(2,1)S(1)}, bf16[384,256]{1,0:T(8,128)(2,1)S(1)}, u32[]{:S(2)}, u32[]{:S(2)}) collective-permute-start(bf16[384,256]{1,0:T(8,128)(2,1)S(1)} %pad_maximum_fusion.2), channel_id=1, source_target_pairs={{0,128},{128,0},{256,384},{384,256},{1,129},{129,1},{257,385},{385... | collective-permute-start | bytes 589832 | tf_op jit(solution)/shard_map/ppermute | solution.py:40
  24.8 1.0 slice.23
  25.8 8.4 %collective-permute-done.1 = bf16[384,256]{1,0:T(8,128)(2,1)S(1)} collective-permute-done((bf16[384,256]{1,0:T(8,128)(2,1)S(1)}, bf16[384,256]{1,0:T(8,128)(2,1)S(1)}, u32[]{:S(2)}, u32[]{:S(2)}) %collective-permute-start.1) | collective-permute-done | bytes 196640 | tf_op jit(solution)/shard_map/ppermute | solution.py:40
  34.2 0.8 slice_add_fusion
  35.0 0.8 pad_maximum_fusion
  36.0 3.4 %collective-permute-start.2 = (bf16[784,256]{1,0:T(8,128)(2,1)S(1)}, bf16[784,256]{1,0:T(8,128)(2,1)S(1)}, u32[]{:S(2)}, u32[]{:S(2)}) collective-permute-start(bf16[784,256]{1,0:T(8,128)(2,1)S(1)} %pad_maximum_fusion.1), channel_id=1, source_target_pairs={{0,2},{1,3},{2,4},{3,5},{4,6},{5,7},{6,0},{7,1},{8,10},{9,11},{10,... | collective-permute-start | bytes 1204232 | tf_op jit(solution)/shard_map/ppermute | solution.py:36
  39.5 3.7 %collective-permute-start.3 = (bf16[784,256]{1,0:T(8,128)(2,1)S(1)}, bf16[784,256]{1,0:T(8,128)(2,1)S(1)}, u32[]{:S(2)}, u32[]{:S(2)}) collective-permute-start(bf16[784,256]{1,0:T(8,128)(2,1)S(1)} %pad_maximum_fusion.1), channel_id=1, source_target_pairs={{0,6},{1,7},{2,0},{3,1},{4,2},{5,3},{6,4},{7,5},{8,14},{9,15},{10,... | collective-permute-start | bytes 1204232 | tf_op jit(solution)/shard_map/ppermute | solution.py:36
  43.3 0.8 ask.1
  44.1 10.0 %all-to-all-start = ((s32[64,1,128]{2,1,0:T(1,128)}), s32[64,1,128]{2,1,0:T(1,128)S(1)}, u32[]{:S(2)}, u32[]{:S(2)}) async-start(s32[64,1,128]{2,1,0:T(1,128)} %bitcast.3), calls=%async_computation | async-start | bytes 65536 | tf_op jit(solution)/shard_map/all_to_all | solution.py:350
  54.1 11.0 %all-to-all-done = s32[64,1,128]{2,1,0:T(1,128)S(1)} async-done(((s32[64,1,128]{2,1,0:T(1,128)}), s32[64,1,128]{2,1,0:T(1,128)S(1)}, u32[]{:S(2)}, u32[]{:S(2)}) %all-to-all-start) | async-done | bytes 32800 | tf_op jit(solution)/shard_map/all_to_all | solution.py:350
  65.2 2.3 %collective-permute-start.4 = (bf16[384,256]{1,0:T(8,128)(2,1)S(1)}, bf16[384,256]{1,0:T(8,128)(2,1)S(1)}, u32[]{:S(2)}, u32[]{:S(2)}) collective-permute-start(bf16[384,256]{1,0:T(8,128)(2,1)S(1)} %slice.21), channel_id=1, source_target_pairs={{0,2},{1,3},{2,4},{3,5},{4,6},{5,7},{6,0},{7,1},{8,10},{9,11},{10,... | collective-permute-start | bytes 589832 | tf_op jit(solution)/shard_map/ppermute | solution.py:36
  67.5 4.9 %collective-permute-start.5 = (bf16[400,256]{1,0:T(8,128)(2,1)S(1)}, bf16[400,256]{1,0:T(8,128)(2,1)S(1)}, u32[]{:S(2)}, u32[]{:S(2)}) collective-permute-start(bf16[400,256]{1,0:T(8,128)(2,1)S(1)} %slice.22), channel_id=1, source_target_pairs={{0,6},{1,7},{2,0},{3,1},{4,2},{5,3},{6,4},{7,5},{8,14},{9,15},{10,... | collective-permute-start | bytes 614408 | tf_op jit(solution)/shard_map/ppermute | solution.py:36
  72.5 1.6 %collective-permute-done.4 = bf16[384,256]{1,0:T(8,128)(2,1)S(1)} collective-permute-done((bf16[384,256]{1,0:T(8,128)(2,1)S(1)}, bf16[384,256]{1,0:T(8,128)(2,1)S(1)}, u32[]{:S(2)}, u32[]{:S(2)}) %collective-permute-start.4) | collective-permute-done | bytes 196640 | tf_op jit(solution)/shard_map/ppermute | solution.py:36
  74.1 1.6 %collective-permute-done.5 = bf16[400,256]{1,0:T(8,128)(2,1)S(1)} collective-permute-done((bf16[400,256]{1,0:T(8,128)(2,1)S(1)}, bf16[400,256]{1,0:T(8,128)(2,1)S(1)}, u32[]{:S(2)}, u32[]{:S(2)}) %collective-permute-start.5) | collective-permute-done | bytes 204832 | tf_op jit(solution)/shard_map/ppermute | solution.py:36
  75.7 1.9 %collective-permute-start.6 = (bf16[3136,256]{1,0:T(8,128)(2,1)S(1)}, bf16[3136,256]{1,0:T(8,128)(2,1)S(1)}, u32[]{:S(2)}, u32[]{:S(2)}) collective-permute-start(bf16[3136,256]{1,0:T(8,128)(2,1)S(1)} %constant_dynamic-update-slice_fusion.near), channel_id=1, source_target_pairs={{0,1},{1,0},{2,3},{3,2},{4,5},{5,4},{6,7},{7,6},{8,9},{9,8},{10,11... | collective-permute-start | bytes 4816904 | tf_op jit(solution)/shard_map/ppermute | solution.py:36
  77.6 1.1 find.1
  78.7 5.5 %all-to-all-start.2 = ((f32[64,2,128]{2,1,0:T(2,128)}), f32[64,2,128]{2,1,0:T(2,128)S(1)}, u32[]{:S(2)}, u32[]{:S(2)}) async-start(f32[64,2,128]{2,1,0:T(2,128)} %find.1), calls=%async_computation.2 | async-start | bytes 131072 | tf_op jit(solution)/shard_map/all_to_all | solution.py:360
  84.2 3.1 %norm.1.normed = bf16[768,2048]{1,0:T(8,128)(2,1)S(1)} custom-call(bf16[3136,256]{1,0:T(8,128)(2,1)S(1)} %constant_dynamic-update-slice_fusion.near, bf16[3136,256]{1,0:T(8,128)(2,1)S(1)} %collective-permute-done.6.far), custom_call_target="tpu_custom_call" | custom-call | tf_op jit(solution)/shard_map/norm/pallas_call | solution.py:362
  87.4 1.7 %copy-done = bf16[768,2048]{1,0:T(8,128)(2,1)} copy-done((bf16[768,2048]{1,0:T(8,128)(2,1)}, bf16[768,2048]{1,0:T(8,128)(2,1)S(1)}, u32[]{:S(2)}) %copy-start) | copy-done | bytes 3145752
  89.1 8.4 %hidden.1 = f32[16,8,256]{2,1,0:T(8,128)} custom-call(bf16[768,2048]{1,0:T(8,128)(2,1)} %copy-done, bf16[16,768]{1,0:T(8,128)(2,1)S(1)} %copy-done.4, bf16[1024,1920]{1,0:T(8,128)(2,1)} %all-gather.2.cloned.1.call-done.weights), custom_call_target="tpu_custom_call" | custom-call | tf_op jit(solution)/shard_map/hidden/pallas_call | solution.py:380
  97.5 6.1 %all-to-all-start.1 = ((f32[16,8,256]{2,1,0:T(8,128)}), f32[16,8,256]{2,1,0:T(8,128)S(1)}, u32[]{:S(2)}, u32[]{:S(2)}) async-start(f32[16,8,256]{2,1,0:T(8,128)} %hidden.1), calls=%async_computation.1 | async-start | bytes 262144 | tf_op jit(solution)/shard_map/all_to_all | solution.py:396
  103.8 6.5 %all-to-all-done.1.parts = f32[16,8,256]{2,1,0:T(8,128)S(1)} async-done(((f32[16,8,256]{2,1,0:T(8,128)}), f32[16,8,256]{2,1,0:T(8,128)S(1)}, u32[]{:S(2)}, u32[]{:S(2)}) %all-to-all-start.1) | async-done | bytes 131104 | tf_op jit(solution)/shard_map/all_to_all | solution.py:396
  110.3 0.7 head.1
  111.0 9.2 %all_to_all.32.messages = bf16[8,96,128]{2,1,0:T(8,128)(2,1)S(1)} all-to-all(bf16[8,96,128]{2,1,0:T(8,128)(2,1)S(1)} %get-tuple-element.22), channel_id=1, replica_groups=mesh['section'=4,'dp'=16,'mp'=8] {'mp'}, dimensions={0} | all-to-all | bytes 393216 | tf_op jit(solution)/shard_map/all_to_all | solution.py:425
  120.3 1.6 %loss.1 = (bf16[2,96]{1,0:T(2,128)(2,1)}, f32[4,128]{1,0:T(4,128)S(1)}, bf16[64,4,384]{2,1,0:T(4,128)(2,1)}) custom-call(s32[4]{0:T(128)S(1)} %copy-done.5, bf16[8,96,128]{2,1,0:T(8,128)(2,1)S(1)} %all_to_all.32.messages, bf16[8,256]{1,0:T(8,128)(2,1)S(1)} %get-tuple-element.23.pooled), custom_call_target="tpu_custom_call" | custom-call | tf_op jit(solution)/shard_map/loss/pallas_call | solution.py:427
  121.8 11.7 %all-to-all-start.4 = ((bf16[64,4,384]{2,1,0:T(4,128)(2,1)}), bf16[64,4,384]{2,1,0:T(4,128)(2,1)S(1)}, u32[]{:S(2)}, u32[]{:S(2)}) async-start(bf16[64,4,384]{2,1,0:T(4,128)(2,1)} %get-tuple-element.26), calls=%async_computation.4 | async-start | bytes 393216 | tf_op jit(solution)/shard_map/all_to_all | solution.py:441
  133.6 0.6 slice_reduce_fusion
  134.2 12.0 %all-to-all-done.4 = bf16[64,4,384]{2,1,0:T(4,128)(2,1)S(1)} async-done(((bf16[64,4,384]{2,1,0:T(4,128)(2,1)}), bf16[64,4,384]{2,1,0:T(4,128)(2,1)S(1)}, u32[]{:S(2)}, u32[]{:S(2)}) %all-to-all-start.4) | async-done | bytes 196640 | tf_op jit(solution)/shard_map/all_to_all | solution.py:441
  146.2 0.8 grad.1
  (51 shorter events, 0.8 us)
Async XLA Ops:
  7.2 28.7 %copy-start.6 = (bf16[2,128,256]{2,1,0:T(8,128)(2,1)S(1)}, bf16[2,128,256]{2,1,0:T(8,128)(2,1)}, u32[]{:S(2)}) copy-start(bf16[2,128,256]{2,1,0:T(8,128)(2,1)} %param.13) | copy-start | bytes 393220
  7.2 28.7 %copy-start.7 = (bf16[4,32,256]{2,1,0:T(8,128)(2,1)S(1)}, bf16[4,32,256]{2,1,0:T(8,128)(2,1)}, u32[]{:S(2)}) copy-start(bf16[4,32,256]{2,1,0:T(8,128)(2,1)} %param.14) | copy-start | bytes 196612
  7.2 81.9 %all-gather.2.cloned.1.call-start = ((), (), s32[]{:S(2)}) async-start(), calls=%async_computation.5 | async-start | bytes 4423680 | tf_op jit(solution)/shard_map/all_gather | solution.py:57
  9.4 24.8 %collective-permute-start = (bf16[128,1024]{1,0:T(8,128)(2,1)}, bf16[128,1024]{1,0:T(8,128)(2,1)S(1)}, u32[]{:S(2)}, u32[]{:S(2)}) collective-permute-start(bf16[128,1024]{1,0:T(8,128)(2,1)} %get-tuple-element.15), channel_id=1, source_target_pairs={{0,320},{8,328},{16,336},{24,344},{32,352},{40,360},{48,368},{56,3... | collective-permute-start | bytes 786440 | tf_op jit(solution)/shard_map/ppermute | solution.py:51
  21.3 12.9 %collective-permute-start.1 = (bf16[384,256]{1,0:T(8,128)(2,1)S(1)}, bf16[384,256]{1,0:T(8,128)(2,1)S(1)}, u32[]{:S(2)}, u32[]{:S(2)}) collective-permute-start(bf16[384,256]{1,0:T(8,128)(2,1)S(1)} %pad_maximum_fusion.2), channel_id=1, source_target_pairs={{0,128},{128,0},{256,384},{384,256},{1,129},{129,1},{257,385},{385... | collective-permute-start | bytes 589832 | tf_op jit(solution)/shard_map/ppermute | solution.py:40
  35.0 1.0 copy-start.8
  35.8 7.3 %copy-start.9 = (s32[4,8]{1,0:T(4,128)S(1)}, s32[4,8]{1,0:T(4,128)}, u32[]{:S(2)}) copy-start(s32[4,8]{1,0:T(4,128)} %param.22) | copy-start | bytes 388
  35.8 7.4 %copy-start.10 = (s32[4,8]{1,0:T(4,128)S(1)}, s32[4,8]{1,0:T(4,128)}, u32[]{:S(2)}) copy-start(s32[4,8]{1,0:T(4,128)} %param.23) | copy-start | bytes 388
  36.0 29.1 %collective-permute-start.2 = (bf16[784,256]{1,0:T(8,128)(2,1)S(1)}, bf16[784,256]{1,0:T(8,128)(2,1)S(1)}, u32[]{:S(2)}, u32[]{:S(2)}) collective-permute-start(bf16[784,256]{1,0:T(8,128)(2,1)S(1)} %pad_maximum_fusion.1), channel_id=1, source_target_pairs={{0,2},{1,3},{2,4},{3,5},{4,6},{5,7},{6,0},{7,1},{8,10},{9,11},{10,... | collective-permute-start | bytes 1204232 | tf_op jit(solution)/shard_map/ppermute | solution.py:36
  39.5 25.7 %collective-permute-start.3 = (bf16[784,256]{1,0:T(8,128)(2,1)S(1)}, bf16[784,256]{1,0:T(8,128)(2,1)S(1)}, u32[]{:S(2)}, u32[]{:S(2)}) collective-permute-start(bf16[784,256]{1,0:T(8,128)(2,1)S(1)} %pad_maximum_fusion.1), channel_id=1, source_target_pairs={{0,6},{1,7},{2,0},{3,1},{4,2},{5,3},{6,4},{7,5},{8,14},{9,15},{10,... | collective-permute-start | bytes 1204232 | tf_op jit(solution)/shard_map/ppermute | solution.py:36
  44.1 21.0 %all-to-all-start = ((s32[64,1,128]{2,1,0:T(1,128)}), s32[64,1,128]{2,1,0:T(1,128)S(1)}, u32[]{:S(2)}, u32[]{:S(2)}) async-start(s32[64,1,128]{2,1,0:T(1,128)} %bitcast.3), calls=%async_computation | async-start | bytes 65536 | tf_op jit(solution)/shard_map/all_to_all | solution.py:350
  65.1 12.5 %copy-start.3 = (bf16[2048,96]{0,1:T(8,128)(2,1)S(1)}, bf16[2048,96]{0,1:T(8,128)(2,1)}, u32[]{:S(2)}) copy-start(bf16[2048,96]{0,1:T(8,128)(2,1)} %param.21) | copy-start | bytes 1179652
  65.2 8.9 %collective-permute-start.4 = (bf16[384,256]{1,0:T(8,128)(2,1)S(1)}, bf16[384,256]{1,0:T(8,128)(2,1)S(1)}, u32[]{:S(2)}, u32[]{:S(2)}) collective-permute-start(bf16[384,256]{1,0:T(8,128)(2,1)S(1)} %slice.21), channel_id=1, source_target_pairs={{0,2},{1,3},{2,4},{3,5},{4,6},{5,7},{6,0},{7,1},{8,10},{9,11},{10,... | collective-permute-start | bytes 589832 | tf_op jit(solution)/shard_map/ppermute | solution.py:36
  67.5 8.1 %collective-permute-start.5 = (bf16[400,256]{1,0:T(8,128)(2,1)S(1)}, bf16[400,256]{1,0:T(8,128)(2,1)S(1)}, u32[]{:S(2)}, u32[]{:S(2)}) collective-permute-start(bf16[400,256]{1,0:T(8,128)(2,1)S(1)} %slice.22), channel_id=1, source_target_pairs={{0,6},{1,7},{2,0},{3,1},{4,2},{5,3},{6,4},{7,5},{8,14},{9,15},{10,... | collective-permute-start | bytes 614408 | tf_op jit(solution)/shard_map/ppermute | solution.py:36
  75.7 8.6 %collective-permute-start.6 = (bf16[3136,256]{1,0:T(8,128)(2,1)S(1)}, bf16[3136,256]{1,0:T(8,128)(2,1)S(1)}, u32[]{:S(2)}, u32[]{:S(2)}) collective-permute-start(bf16[3136,256]{1,0:T(8,128)(2,1)S(1)} %constant_dynamic-update-slice_fusion.near), channel_id=1, source_target_pairs={{0,1},{1,0},{2,3},{3,2},{4,5},{5,4},{6,7},{7,6},{8,9},{9,8},{10,11... | collective-permute-start | bytes 4816904 | tf_op jit(solution)/shard_map/ppermute | solution.py:36
  78.7 18.8 %all-to-all-start.2 = ((f32[64,2,128]{2,1,0:T(2,128)}), f32[64,2,128]{2,1,0:T(2,128)S(1)}, u32[]{:S(2)}, u32[]{:S(2)}) async-start(f32[64,2,128]{2,1,0:T(2,128)} %find.1), calls=%async_computation.2 | async-start | bytes 131072 | tf_op jit(solution)/shard_map/all_to_all | solution.py:360
  84.2 4.8 %copy-start.4 = (bf16[16,768]{1,0:T(8,128)(2,1)S(1)}, bf16[16,768]{1,0:T(8,128)(2,1)}, u32[]{:S(2)}) copy-start(bf16[16,768]{1,0:T(8,128)(2,1)} %constant.31.clone.pool) | copy-start | bytes 73732
  87.4 1.7 %copy-start = (bf16[768,2048]{1,0:T(8,128)(2,1)}, bf16[768,2048]{1,0:T(8,128)(2,1)S(1)}, u32[]{:S(2)}) copy-start(bf16[768,2048]{1,0:T(8,128)(2,1)S(1)} %norm.1.normed) | copy-start | bytes 9437188
  89.1 21.3 %copy-start.1 = (bf16[256,768]{1,0:T(8,128)(2,1)S(1)}, bf16[256,768]{1,0:T(8,128)(2,1)}, u32[]{:S(2)}) copy-start(bf16[256,768]{1,0:T(8,128)(2,1)} %old_head.1) | copy-start | bytes 1179652
  89.1 21.3 %copy-start.2 = (bf16[256,768]{1,0:T(8,128)(2,1)S(1)}, bf16[256,768]{1,0:T(8,128)(2,1)}, u32[]{:S(2)}) copy-start(bf16[256,768]{1,0:T(8,128)(2,1)} %new_head.1) | copy-start | bytes 1179652
  97.5 22.8 %copy-start.5 = (s32[4]{0:T(128)S(1)}, s32[4]{0:T(128)}, u32[]{:S(2)}) copy-start(s32[4]{0:T(128)} %slot.1) | copy-start | bytes 52
  97.5 12.8 %all-to-all-start.1 = ((f32[16,8,256]{2,1,0:T(8,128)}), f32[16,8,256]{2,1,0:T(8,128)S(1)}, u32[]{:S(2)}, u32[]{:S(2)}) async-start(f32[16,8,256]{2,1,0:T(8,128)} %hidden.1), calls=%async_computation.1 | async-start | bytes 262144 | tf_op jit(solution)/shard_map/all_to_all | solution.py:396
  121.8 24.3 %all-to-all-start.4 = ((bf16[64,4,384]{2,1,0:T(4,128)(2,1)}), bf16[64,4,384]{2,1,0:T(4,128)(2,1)S(1)}, u32[]{:S(2)}, u32[]{:S(2)}) async-start(bf16[64,4,384]{2,1,0:T(4,128)(2,1)} %get-tuple-element.26), calls=%async_computation.4 | async-start | bytes 393216 | tf_op jit(solution)/shard_map/all_to_all | solution.py:441
Sparse Core Ops, SparseCore 0:
  36.0 52.8 all-gather.1

commit v2 on v1

--- a/solution.py
+++ b/solution.py
@@ -57,10 +57,10 @@
     return lax.all_gather(block, "dp", axis=0, axis_index_groups=groups, tiled=True)
 
 
-def x_ring(block, rows, wanted):
-    low, high, wanted = lax.optimization_barrier((mp_move(block, 1, 0), mp_move(block, -1, 0), wanted))
-    top, bottom = mp_move(low[:rows], 1, 0), mp_move(high[rows:], -1, 0)
-    mine = jnp.concatenate([block, low, high, top, bottom], axis=0)
+def x_blocks(block, wanted):
+    others = [mp_move(block, step, 0) for step in (1, -1, 2)]
+    others, wanted = lax.optimization_barrier((others, wanted))
+    mine = jnp.concatenate([block] + others, axis=0)
     return mine, mp_move(mine, 0, 1), wanted
 
 
@@ -92,6 +92,13 @@
                 out[:, base + 2 * units - cut : base + 2 * units] = up[:, first : first + cut]
 
 
+def merge_kernel(own, other, out):
+    edge = own.shape[1] - 128
+    out[:, :edge] = own[:, :edge]
+    out[:, edge : edge + 128] = own[:, edge:] + other[:, :128]
+    out[:, edge + 128 :] = other[:, 128:]
+
+
 def norm_kernel(nx, rows, near, far, out):
     step_rows = 32
     width = near.shape[1]
@@ -151,22 +158,35 @@
 def hidden_kernel(units, normed, pool, weights, out, up_w, down_w, hidden, sems):
     h = lax.axis_index("dp") // (lax.axis_size("dp") // 2)
     rows = weights.shape[0]
-    up_copies = [
-        pltpu.make_async_copy(
-            weights.at[:, pl.ds(4 * units * side, 2 * units)],
-            up_w.at[pl.ds(pl.multiple_of((1 - h if side else h) * rows, rows), rows), :],
-            sems.at[side],
+    parts = 4
+    piece = rows // parts
+    copies = []
+    for side, target in ((0, up_w), (2, up_w), (1, down_w)):
+        base = rows if side == 2 else 0
+        copies.append(
+            [
+                pltpu.make_async_copy(
+                    weights.at[pl.ds(k * piece, piece), pl.ds(2 * units * side, 2 * units)],
+                    target.at[pl.ds(base + k * piece, piece), :],
+                    sems.at[side * parts + k],
+                )
+                for k in range(parts)
+            ]
         )
-        for side in range(2)
-    ]
-    down_copy = pltpu.make_async_copy(weights.at[:, pl.ds(2 * units, 2 * units)], down_w, sems.at[2])
-    for copy in up_copies + [down_copy]:
-        copy.start()
-    for copy in up_copies:
-        copy.wait()
+    for group in copies:
+        for copy in group:
+            copy.start()
+    both = None
+    for side in range(2):
+        for copy in copies[side]:
+            copy.wait()
+        columns = pl.ds(pl.multiple_of((1 - h if side else h) * rows, rows), rows)
+        term = jnp.dot(
+            normed[:, columns], up_w[side * rows : (side + 1) * rows, :], preferred_element_type=jnp.float32
+        )
+        both = term if both is None else both + term
     cut = units // 128 * 128
     tail = units - cut
-    both = jnp.dot(normed[...], up_w[...], preferred_element_type=jnp.float32)
     hidden[:, :cut] = (gelu(both[:, :cut]) * both[:, 2 * units - cut :]).astype(jnp.bfloat16)
     if tail:
         edge = both[:, cut : cut + 2 * tail]
@@ -179,7 +199,8 @@
     own_rows = jnp.concatenate([both_parts, none], axis=1)
     other_rows = jnp.concatenate([none, both_parts], axis=1)
     sides = jnp.concatenate([own_rows, other_rows], axis=0).astype(jnp.bfloat16)
-    down_copy.wait()
+    for copy in copies[2]:
+        copy.wait()
     total = lax.dot_general(sides, down_w[...], (((1,), (1,)), ((), ())), preferred_element_type=jnp.float32)
     mp_n, _, width = out.shape[0] // 2, out.shape[1], out.shape[2]
     for side in range(2):
@@ -327,16 +348,6 @@
     rows = p_count * length + q_count * q_length
     gain_rows = jnp.broadcast_to(norm_gain[None, :], (16, width))
     tokens = jnp.concatenate([passage_tokens.reshape(-1, width), query_tokens.reshape(-1, width)], axis=0)
-    other, mate_tokens = lax.optimization_barrier((other, mate_move(tokens)))
-
-    edge = wide - 128
-    merged = jnp.concatenate([own[:, :edge], own[:, edge:] + other[:, :128], other[:, 128:]], axis=1)
-    weights = along_y(merged)
-
-    flip = lax.axis_index("section") % 2 == 1
-    tokens = jnp.concatenate(
-        [jnp.where(flip, mate_tokens, tokens), jnp.where(flip, tokens, mate_tokens), gain_rows], axis=0
-    )
     request_count = q_count * k_count
     owner = neg_owner.reshape(1, request_count)
     requests = pl.pallas_call(
@@ -347,8 +358,24 @@
         compiler_params=params(),
         name="ask",
     )(owner, neg_row.reshape(1, request_count))
+
+    other, mate_tokens, requests = lax.optimization_barrier((other, mate_move(tokens), requests))
+    merged = pl.pallas_call(
+        merge_kernel,
+        out_shape=jax.ShapeDtypeStruct((w_gate.shape[0], 6 * units), bf16),
+        in_specs=[whole()] * 2,
+        out_specs=whole(),
+        compiler_params=params(),
+        name="merge",
+    )(own, other)
+    weights = along_y(merged)
+
+    flip = lax.axis_index("section") % 2 == 1
+    tokens = jnp.concatenate(
+        [jnp.where(flip, mate_tokens, tokens), jnp.where(flip, tokens, mate_tokens), gain_rows], axis=0
+    )
     wanted = lax.all_to_all(requests, ("section", "dp"), 0, 0, tiled=True)
-    near, far, wanted = x_ring(tokens, rows, wanted)
+    near, far, wanted = x_blocks(tokens, wanted)
     found = pl.pallas_call(
         find_kernel,
         out_shape=jax.ShapeDtypeStruct((shard_count, 2, 128), f32),
@@ -386,7 +413,7 @@
             pltpu.VMEM((features, 2 * units), bf16),
             pltpu.VMEM((features // 2, 2 * units), bf16),
             pltpu.VMEM((2 * rows, padded), bf16),
-            pltpu.SemaphoreType.DMA((3,)),
+            pltpu.SemaphoreType.DMA((12,)),
         ],
         compiler_params=params(52),
         name="hidden",

time: 155 us -> 154 us (level)
  starting transfers between devices: 64 us -> 59.7 us
  local copies, waits for them, and re-layouts: 3.73 us -> 7.03 us
  other arithmetic: 2.82 us -> 1.24 us
    all_gather x1, waiting for transfers between devices: 0.01 us -> 6 us  [along_y(): lax.all_gather(block, 'dp', axis=0, axis_index_groups=groups, tiled=True)]
    ppermute x5 -> x4, starting transfers between devices: 16.2 us -> 12.7 us  [mp_move(): return lax.ppermute(block, 'mp', perm)]
    ppermute x5 -> x4, waiting for transfers between devices: 3.17 us -> 0.01 us  [mp_move(): return lax.ppermute(block, 'mp', perm)]
    unnamed x26 -> x23, local copies, waits for them, and re-layouts: 1.78 us -> 3.72 us
  transfers between devices with their start and end apart: 12 -> 11, of which waited for: 6 -> 5; matrix products, arithmetic and copies ran while one was open for 2% -> 3% of each run, Pallas kernels for 9% -> 9%
where the time goes in v2:
time: 154 us
  starting transfers between devices  59.7 us (39%)
  waiting for transfers between devices  42.5 us (28%)
  Pallas kernels  19.5 us (13%)
  between operations  14.3 us (9%)
  blocking collectives  9.23 us (6%)
  local copies, waits for them, and re-layouts  7.03 us (5%)
    ppermute x4, starting transfers between devices, mp_move(): return lax.ppermute(block, 'mp', perm)  12.7 us
    all_to_all x1, waiting for transfers between devices, shards(): arrived = lax.all_to_all(message, ('section', 'dp'), 0, 0, tiled=True)  12 us
    all_to_all x1, starting transfers between devices, shards(): arrived = lax.all_to_all(message, ('section', 'dp'), 0, 0, tiled=True)  11.6 us
    all_to_all x1, waiting for transfers between devices, shards(): wanted = lax.all_to_all(requests, ('section', 'dp'), 0, 0, tiled=True)  11 us
    ppermute x1, starting transfers between devices, half_move(): return lax.ppermute(block, ('section', 'dp'), perm)  10.9 us
    all_to_all x1, starting transfers between devices, shards(): wanted = lax.all_to_all(requests, ('section', 'dp'), 0, 0, tiled=True)  10 us
    all_to_all x1, blocking collectives, shards(): messages = lax.all_to_all(message, 'mp', 0, 0, tiled=True)  9.23 us
    pallas_call x1, Pallas kernels, shards(): pl.pallas_call(functools.partial(hidden_kernel, units), out_shape=jax.Sha...  8.43 us
  transfers between devices with their start and end apart: 11, of which 5 were waited for; matrix products, arithmetic and copies ran while one was open for 3% of the time, Pallas kernels for 9%

profile of v2, /device:TPU:8, one launch (start us, length us, event | category | flops | bytes accessed | tf_op | source)
XLA Modules:
  0.0 153.6 jit_solution(609639113777476902)
XLA Ops:
  7.2 2.1 %cut.1 = (bf16[128,1024]{1,0:T(8,128)(2,1)}, bf16[128,1024]{1,0:T(8,128)(2,1)}) custom-call(bf16[128,640]{1,0:T(8,128)(2,1)} %gate_in.1, bf16[128,640]{1,0:T(8,128)(2,1)} %up_in.1, bf16[640,128]{1,0:T(8,128)(2,1)} %down_in.1), custom_call_target="tpu_custom_call" | custom-call | tf_op jit(solution)/shard_map/cut/pallas_call | solution.py:337
  9.4 10.9 %collective-permute-start = (bf16[128,1024]{1,0:T(8,128)(2,1)}, bf16[128,1024]{1,0:T(8,128)(2,1)S(1)}, u32[]{:S(2)}, u32[]{:S(2)}) collective-permute-start(bf16[128,1024]{1,0:T(8,128)(2,1)} %get-tuple-element.17), channel_id=1, source_target_pairs={{0,320},{8,328},{16,336},{24,344},{32,352},{40,360},{48,368},{56,3... | collective-permute-start | bytes 786440 | tf_op jit(solution)/shard_map/ppermute | solution.py:51
  20.3 1.0 pad_maximum_fusion.1
  21.3 3.5 %collective-permute-start.1 = (bf16[384,256]{1,0:T(8,128)(2,1)S(1)}, bf16[384,256]{1,0:T(8,128)(2,1)S(1)}, u32[]{:S(2)}, u32[]{:S(2)}) collective-permute-start(bf16[384,256]{1,0:T(8,128)(2,1)S(1)} %pad_maximum_fusion.1), channel_id=1, source_target_pairs={{0,128},{128,0},{256,384},{384,256},{1,129},{129,1},{257,385},{385... | collective-permute-start | bytes 589832 | tf_op jit(solution)/shard_map/ppermute | solution.py:40
  24.8 0.8 reshape.26.owner
  25.6 0.8 reshape.27.row
  26.4 0.8 ask.1
  27.2 7.0 %collective-permute-done.1 = bf16[384,256]{1,0:T(8,128)(2,1)S(1)} collective-permute-done((bf16[384,256]{1,0:T(8,128)(2,1)S(1)}, bf16[384,256]{1,0:T(8,128)(2,1)S(1)}, u32[]{:S(2)}, u32[]{:S(2)}) %collective-permute-start.1) | collective-permute-done | bytes 196640 | tf_op jit(solution)/shard_map/ppermute | solution.py:40
  34.2 0.9 copy-done.4
  35.2 0.8 merge.1
  36.2 3.4 %collective-permute-start.2 = (bf16[784,256]{1,0:T(8,128)(2,1)S(1)}, bf16[784,256]{1,0:T(8,128)(2,1)S(1)}, u32[]{:S(2)}, u32[]{:S(2)}) collective-permute-start(bf16[784,256]{1,0:T(8,128)(2,1)S(1)} %pad_maximum_fusion), channel_id=1, source_target_pairs={{0,2},{1,3},{2,4},{3,5},{4,6},{5,7},{6,0},{7,1},{8,10},{9,11},{10,... | collective-permute-start | bytes 1204232 | tf_op jit(solution)/shard_map/ppermute | solution.py:36
  39.6 3.7 %collective-permute-start.3 = (bf16[784,256]{1,0:T(8,128)(2,1)S(1)}, bf16[784,256]{1,0:T(8,128)(2,1)S(1)}, u32[]{:S(2)}, u32[]{:S(2)}) collective-permute-start(bf16[784,256]{1,0:T(8,128)(2,1)S(1)} %pad_maximum_fusion), channel_id=1, source_target_pairs={{0,6},{1,7},{2,0},{3,1},{4,2},{5,3},{6,4},{7,5},{8,14},{9,15},{10,... | collective-permute-start | bytes 1204232 | tf_op jit(solution)/shard_map/ppermute | solution.py:36
  43.3 3.7 %collective-permute-start.4 = (bf16[784,256]{1,0:T(8,128)(2,1)S(1)}, bf16[784,256]{1,0:T(8,128)(2,1)}, u32[]{:S(2)}, u32[]{:S(2)}) collective-permute-start(bf16[784,256]{1,0:T(8,128)(2,1)S(1)} %pad_maximum_fusion), channel_id=1, source_target_pairs={{0,4},{1,5},{2,6},{3,7},{4,0},{5,1},{6,2},{7,3},{8,12},{9,13},{10,... | collective-permute-start | bytes 1204232 | tf_op jit(solution)/shard_map/ppermute | solution.py:36
  47.0 10.0 %all-to-all-start = ((s32[64,1,128]{2,1,0:T(1,128)}), s32[64,1,128]{2,1,0:T(1,128)S(1)}, u32[]{:S(2)}, u32[]{:S(2)}) async-start(s32[64,1,128]{2,1,0:T(1,128)} %bitcast.3), calls=%async_computation | async-start | bytes 65536 | tf_op jit(solution)/shard_map/all_to_all | solution.py:377
  57.0 11.0 %all-to-all-done = s32[64,1,128]{2,1,0:T(1,128)S(1)} async-done(((s32[64,1,128]{2,1,0:T(1,128)}), s32[64,1,128]{2,1,0:T(1,128)S(1)}, u32[]{:S(2)}, u32[]{:S(2)}) %all-to-all-start) | async-done | bytes 32800 | tf_op jit(solution)/shard_map/all_to_all | solution.py:377
  68.1 1.0 constant_dynamic-update-slice_fusion.near
  69.1 1.9 %collective-permute-start.5 = (bf16[3136,256]{1,0:T(8,128)(2,1)S(1)}, bf16[3136,256]{1,0:T(8,128)(2,1)S(1)}, u32[]{:S(2)}, u32[]{:S(2)}) collective-permute-start(bf16[3136,256]{1,0:T(8,128)(2,1)S(1)} %constant_dynamic-update-slice_fusion.near), channel_id=1, source_target_pairs={{0,1},{1,0},{2,3},{3,2},{4,5},{5,4},{6,7},{7,6},{8,9},{9,8},{10,11... | collective-permute-start | bytes 4816904 | tf_op jit(solution)/shard_map/ppermute | solution.py:36
  71.1 1.0 copy-done.3
  72.1 1.1 find.1
  73.2 5.5 %all-to-all-start.2 = ((f32[64,2,128]{2,1,0:T(2,128)}), f32[64,2,128]{2,1,0:T(2,128)S(1)}, u32[]{:S(2)}, u32[]{:S(2)}) async-start(f32[64,2,128]{2,1,0:T(2,128)} %find.1), calls=%async_computation.2 | async-start | bytes 131072 | tf_op jit(solution)/shard_map/all_to_all | solution.py:387
  78.7 3.1 %norm.1.normed = bf16[768,2048]{1,0:T(8,128)(2,1)S(1)} custom-call(bf16[3136,256]{1,0:T(8,128)(2,1)S(1)} %constant_dynamic-update-slice_fusion.near, bf16[3136,256]{1,0:T(8,128)(2,1)S(1)} %collective-permute-done.5.far), custom_call_target="tpu_custom_call" | custom-call | tf_op jit(solution)/shard_map/norm/pallas_call | solution.py:389
  81.9 1.7 %copy-done = bf16[768,2048]{1,0:T(8,128)(2,1)} copy-done((bf16[768,2048]{1,0:T(8,128)(2,1)}, bf16[768,2048]{1,0:T(8,128)(2,1)S(1)}, u32[]{:S(2)}) %copy-start) | copy-done | bytes 3145752
  83.6 6.0 %all-gather.2.cloned.1.call-done.weights = bf16[1024,1920]{1,0:T(8,128)(2,1)} async-done(((bf16[128,1920]{1,0:T(8,128)(2,1)}), bf16[1024,1920]{1,0:T(8,128)(2,1)}) %all-gather.2.cloned.1.call-update) | async-done | bytes 3932176 | tf_op jit(solution)/shard_map/all_gather | solution.py:57
  89.6 8.4 %hidden.1 = f32[16,8,256]{2,1,0:T(8,128)} custom-call(bf16[768,2048]{1,0:T(8,128)(2,1)} %copy-done, bf16[16,768]{1,0:T(8,128)(2,1)S(1)} %copy-done.5, bf16[1024,1920]{1,0:T(8,128)(2,1)} %all-gather.2.cloned.1.call-done.weights), custom_call_target="tpu_custom_call" | custom-call | tf_op jit(solution)/shard_map/hidden/pallas_call | solution.py:407
  98.0 5.5 %all-to-all-start.1 = ((f32[16,8,256]{2,1,0:T(8,128)}), f32[16,8,256]{2,1,0:T(8,128)S(1)}, u32[]{:S(2)}, u32[]{:S(2)}) async-start(f32[16,8,256]{2,1,0:T(8,128)} %hidden.1), calls=%async_computation.1 | async-start | bytes 262144 | tf_op jit(solution)/shard_map/all_to_all | solution.py:423
  103.7 6.5 %all-to-all-done.1.parts = f32[16,8,256]{2,1,0:T(8,128)S(1)} async-done(((f32[16,8,256]{2,1,0:T(8,128)}), f32[16,8,256]{2,1,0:T(8,128)S(1)}, u32[]{:S(2)}, u32[]{:S(2)}) %all-to-all-start.1) | async-done | bytes 131104 | tf_op jit(solution)/shard_map/all_to_all | solution.py:423
  110.2 0.7 head.1
  110.9 9.2 %all_to_all.32.messages = bf16[8,96,128]{2,1,0:T(8,128)(2,1)S(1)} all-to-all(bf16[8,96,128]{2,1,0:T(8,128)(2,1)S(1)} %get-tuple-element.26), channel_id=1, replica_groups=mesh['section'=4,'dp'=16,'mp'=8] {'mp'}, dimensions={0} | all-to-all | bytes 393216 | tf_op jit(solution)/shard_map/all_to_all | solution.py:452
  120.1 1.6 %loss.1 = (bf16[2,96]{1,0:T(2,128)(2,1)}, f32[4,128]{1,0:T(4,128)S(1)}, bf16[64,4,384]{2,1,0:T(4,128)(2,1)}) custom-call(s32[4]{0:T(128)S(1)} %copy-done.6, bf16[8,96,128]{2,1,0:T(8,128)(2,1)S(1)} %all_to_all.32.messages, bf16[8,256]{1,0:T(8,128)(2,1)S(1)} %get-tuple-element.27.pooled), custom_call_target="tpu_custom_call" | custom-call | tf_op jit(solution)/shard_map/loss/pallas_call | solution.py:454
  121.7 11.6 %all-to-all-start.4 = ((bf16[64,4,384]{2,1,0:T(4,128)(2,1)}), bf16[64,4,384]{2,1,0:T(4,128)(2,1)S(1)}, u32[]{:S(2)}, u32[]{:S(2)}) async-start(bf16[64,4,384]{2,1,0:T(4,128)(2,1)} %get-tuple-element.30), calls=%async_computation.4 | async-start | bytes 393216 | tf_op jit(solution)/shard_map/all_to_all | solution.py:468
  133.9 12.0 %all-to-all-done.4 = bf16[64,4,384]{2,1,0:T(4,128)(2,1)S(1)} async-done(((bf16[64,4,384]{2,1,0:T(4,128)(2,1)}), bf16[64,4,384]{2,1,0:T(4,128)(2,1)S(1)}, u32[]{:S(2)}, u32[]{:S(2)}) %all-to-all-start.4) | async-done | bytes 196640 | tf_op jit(solution)/shard_map/all_to_all | solution.py:468
  145.9 0.8 grad.1
  (41 shorter events, 1.2 us)
Async XLA Ops:
  7.2 28.8 %copy-start.7 = (bf16[2,128,256]{2,1,0:T(8,128)(2,1)S(1)}, bf16[2,128,256]{2,1,0:T(8,128)(2,1)}, u32[]{:S(2)}) copy-start(bf16[2,128,256]{2,1,0:T(8,128)(2,1)} %param.13) | copy-start | bytes 393220
  7.2 28.8 %copy-start.8 = (bf16[4,32,256]{2,1,0:T(8,128)(2,1)S(1)}, bf16[4,32,256]{2,1,0:T(8,128)(2,1)}, u32[]{:S(2)}) copy-start(bf16[4,32,256]{2,1,0:T(8,128)(2,1)} %param.14) | copy-start | bytes 196612
  7.2 82.4 %all-gather.2.cloned.1.call-start = ((), (), s32[]{:S(2)}) async-start(), calls=%async_computation.5 | async-start | bytes 4423680 | tf_op jit(solution)/shard_map/all_gather | solution.py:57
  9.4 24.8 %collective-permute-start = (bf16[128,1024]{1,0:T(8,128)(2,1)}, bf16[128,1024]{1,0:T(8,128)(2,1)S(1)}, u32[]{:S(2)}, u32[]{:S(2)}) collective-permute-start(bf16[128,1024]{1,0:T(8,128)(2,1)} %get-tuple-element.17), channel_id=1, source_target_pairs={{0,320},{8,328},{16,336},{24,344},{32,352},{40,360},{48,368},{56,3... | collective-permute-start | bytes 786440 | tf_op jit(solution)/shard_map/ppermute | solution.py:51
  21.3 14.8 %copy-start.9 = (bf16[256]{0:T(256)(128)(2,1)S(1)}, bf16[256]{0:T(256)(128)(2,1)}, u32[]{:S(2)}) copy-start(bf16[256]{0:T(256)(128)(2,1)} %param.15) | copy-start | bytes 1540
  21.3 12.9 %collective-permute-start.1 = (bf16[384,256]{1,0:T(8,128)(2,1)S(1)}, bf16[384,256]{1,0:T(8,128)(2,1)S(1)}, u32[]{:S(2)}, u32[]{:S(2)}) collective-permute-start(bf16[384,256]{1,0:T(8,128)(2,1)S(1)} %pad_maximum_fusion.1), channel_id=1, source_target_pairs={{0,128},{128,0},{256,384},{384,256},{1,129},{129,1},{257,385},{385... | collective-permute-start | bytes 589832 | tf_op jit(solution)/shard_map/ppermute | solution.py:40
  34.2 1.0 copy-start.4
  36.2 31.8 %collective-permute-start.2 = (bf16[784,256]{1,0:T(8,128)(2,1)S(1)}, bf16[784,256]{1,0:T(8,128)(2,1)S(1)}, u32[]{:S(2)}, u32[]{:S(2)}) collective-permute-start(bf16[784,256]{1,0:T(8,128)(2,1)S(1)} %pad_maximum_fusion), channel_id=1, source_target_pairs={{0,2},{1,3},{2,4},{3,5},{4,6},{5,7},{6,0},{7,1},{8,10},{9,11},{10,... | collective-permute-start | bytes 1204232 | tf_op jit(solution)/shard_map/ppermute | solution.py:36
  39.6 28.4 %collective-permute-start.3 = (bf16[784,256]{1,0:T(8,128)(2,1)S(1)}, bf16[784,256]{1,0:T(8,128)(2,1)S(1)}, u32[]{:S(2)}, u32[]{:S(2)}) collective-permute-start(bf16[784,256]{1,0:T(8,128)(2,1)S(1)} %pad_maximum_fusion), channel_id=1, source_target_pairs={{0,6},{1,7},{2,0},{3,1},{4,2},{5,3},{6,4},{7,5},{8,14},{9,15},{10,... | collective-permute-start | bytes 1204232 | tf_op jit(solution)/shard_map/ppermute | solution.py:36
  43.3 24.8 %collective-permute-start.4 = (bf16[784,256]{1,0:T(8,128)(2,1)S(1)}, bf16[784,256]{1,0:T(8,128)(2,1)}, u32[]{:S(2)}, u32[]{:S(2)}) collective-permute-start(bf16[784,256]{1,0:T(8,128)(2,1)S(1)} %pad_maximum_fusion), channel_id=1, source_target_pairs={{0,4},{1,5},{2,6},{3,7},{4,0},{5,1},{6,2},{7,3},{8,12},{9,13},{10,... | collective-permute-start | bytes 1204232 | tf_op jit(solution)/shard_map/ppermute | solution.py:36
  47.0 21.0 %all-to-all-start = ((s32[64,1,128]{2,1,0:T(1,128)}), s32[64,1,128]{2,1,0:T(1,128)S(1)}, u32[]{:S(2)}, u32[]{:S(2)}) async-start(s32[64,1,128]{2,1,0:T(1,128)} %bitcast.3), calls=%async_computation | async-start | bytes 65536 | tf_op jit(solution)/shard_map/all_to_all | solution.py:377
  69.1 9.6 %collective-permute-start.5 = (bf16[3136,256]{1,0:T(8,128)(2,1)S(1)}, bf16[3136,256]{1,0:T(8,128)(2,1)S(1)}, u32[]{:S(2)}, u32[]{:S(2)}) collective-permute-start(bf16[3136,256]{1,0:T(8,128)(2,1)S(1)} %constant_dynamic-update-slice_fusion.near), channel_id=1, source_target_pairs={{0,1},{1,0},{2,3},{3,2},{4,5},{5,4},{6,7},{7,6},{8,9},{9,8},{10,11... | collective-permute-start | bytes 4816904 | tf_op jit(solution)/shard_map/ppermute | solution.py:36
  71.1 1.0 copy-start.3
  73.2 24.8 %all-to-all-start.2 = ((f32[64,2,128]{2,1,0:T(2,128)}), f32[64,2,128]{2,1,0:T(2,128)S(1)}, u32[]{:S(2)}, u32[]{:S(2)}) async-start(f32[64,2,128]{2,1,0:T(2,128)} %find.1), calls=%async_computation.2 | async-start | bytes 131072 | tf_op jit(solution)/shard_map/all_to_all | solution.py:387
  78.7 10.9 %copy-start.5 = (bf16[16,768]{1,0:T(8,128)(2,1)S(1)}, bf16[16,768]{1,0:T(8,128)(2,1)}, u32[]{:S(2)}) copy-start(bf16[16,768]{1,0:T(8,128)(2,1)} %constant.31.clone.pool) | copy-start | bytes 73732
  81.9 1.7 %copy-start = (bf16[768,2048]{1,0:T(8,128)(2,1)}, bf16[768,2048]{1,0:T(8,128)(2,1)S(1)}, u32[]{:S(2)}) copy-start(bf16[768,2048]{1,0:T(8,128)(2,1)S(1)} %norm.1.normed) | copy-start | bytes 9437188
  83.6 26.6 %copy-start.1 = (bf16[256,768]{1,0:T(8,128)(2,1)S(1)}, bf16[256,768]{1,0:T(8,128)(2,1)}, u32[]{:S(2)}) copy-start(bf16[256,768]{1,0:T(8,128)(2,1)} %old_head.1) | copy-start | bytes 1179652
  83.6 26.6 %copy-start.2 = (bf16[256,768]{1,0:T(8,128)(2,1)S(1)}, bf16[256,768]{1,0:T(8,128)(2,1)}, u32[]{:S(2)}) copy-start(bf16[256,768]{1,0:T(8,128)(2,1)} %new_head.1) | copy-start | bytes 1179652
  98.0 22.1 %copy-start.6 = (s32[4]{0:T(128)S(1)}, s32[4]{0:T(128)}, u32[]{:S(2)}) copy-start(s32[4]{0:T(128)} %slot.1) | copy-start | bytes 52
  98.0 12.2 %all-to-all-start.1 = ((f32[16,8,256]{2,1,0:T(8,128)}), f32[16,8,256]{2,1,0:T(8,128)S(1)}, u32[]{:S(2)}, u32[]{:S(2)}) async-start(f32[16,8,256]{2,1,0:T(8,128)} %hidden.1), calls=%async_computation.1 | async-start | bytes 262144 | tf_op jit(solution)/shard_map/all_to_all | solution.py:423
  121.7 24.2 %all-to-all-start.4 = ((bf16[64,4,384]{2,1,0:T(4,128)(2,1)}), bf16[64,4,384]{2,1,0:T(4,128)(2,1)S(1)}, u32[]{:S(2)}, u32[]{:S(2)}) async-start(bf16[64,4,384]{2,1,0:T(4,128)(2,1)} %get-tuple-element.30), calls=%async_computation.4 | async-start | bytes 393216 | tf_op jit(solution)/shard_map/all_to_all | solution.py:468
Sparse Core Ops, SparseCore 0:
  36.1 53.4 all-gather.1

commit v3 on v2

--- a/solution.py
+++ b/solution.py
@@ -57,10 +57,10 @@
     return lax.all_gather(block, "dp", axis=0, axis_index_groups=groups, tiled=True)
 
 
-def x_blocks(block, wanted):
-    others = [mp_move(block, step, 0) for step in (1, -1, 2)]
-    others, wanted = lax.optimization_barrier((others, wanted))
-    mine = jnp.concatenate([block] + others, axis=0)
+def spread(block, low, high, wanted):
+    mine = jnp.concatenate([block, low, high, mp_move(block, 2, 0)], axis=0)
+    mate, wanted = lax.optimization_barrier((mate_move(mine), wanted))
+    mine = jnp.concatenate([mine, mate], axis=0)
     return mine, mp_move(mine, 0, 1), wanted
 
 
@@ -92,17 +92,11 @@
                 out[:, base + 2 * units - cut : base + 2 * units] = up[:, first : first + cut]
 
 
-def merge_kernel(own, other, out):
-    edge = own.shape[1] - 128
-    out[:, :edge] = own[:, :edge]
-    out[:, edge : edge + 128] = own[:, edge:] + other[:, :128]
-    out[:, edge + 128 :] = other[:, 128:]
-
-
 def norm_kernel(nx, rows, near, far, out):
     step_rows = 32
     width = near.shape[1]
     x, c = lax.axis_index("mp") // 2, lax.axis_index("mp") % 2
+    parity = lax.axis_index("section") % 2
     sides = []
     for ref, core in ((near, c), (far, 1 - c)):
         for k, step in enumerate((0, -1, 1, 2)):
@@ -110,21 +104,24 @@
             at = pl.ds(pl.multiple_of(place * width, width), width)
             sides.append((ref, k * (rows + 16), at))
     gains = [ref[first + rows : first + rows + 1, :].astype(jnp.float32) for ref, first, _ in sides]
-
-    def body(i, carry):
-        start = i * step_rows
-        total = jnp.zeros((step_rows, width), jnp.float32)
-        for ref, first, _ in sides:
-            v = ref[pl.ds(pl.multiple_of(first + start, 16), step_rows), :].astype(jnp.float32)
-            total = total + v * v
-        scale = lax.rsqrt(jnp.sum(total, axis=1, keepdims=True) / (len(sides) * width) + 1e-06)
-        target = pl.ds(pl.multiple_of(start, step_rows), step_rows)
-        for (ref, first, at), gain in zip(sides, gains):
-            v = ref[pl.ds(pl.multiple_of(first + start, 16), step_rows), :].astype(jnp.float32)
-            out[target, at] = (v * scale * gain).astype(jnp.bfloat16)
-        return carry
-
-    lax.fori_loop(0, rows // step_rows, body, 0)
+    for mate in range(2):
+        base = mate * 4 * (rows + 16)
+        target_base = (1 - parity if mate else parity) * rows
+
+        def body(i, carry, base=base, target_base=target_base):
+            start = i * step_rows
+            total = jnp.zeros((step_rows, width), jnp.float32)
+            for ref, first, _ in sides:
+                v = ref[pl.ds(pl.multiple_of(base + first + start, 16), step_rows), :].astype(jnp.float32)
+                total = total + v * v
+            scale = lax.rsqrt(jnp.sum(total, axis=1, keepdims=True) / (len(sides) * width) + 1e-06)
+            target = pl.ds(pl.multiple_of(target_base + start, step_rows), step_rows)
+            for (ref, first, at), gain in zip(sides, gains):
+                v = ref[pl.ds(pl.multiple_of(base + first + start, 16), step_rows), :].astype(jnp.float32)
+                out[target, at] = (v * scale * gain).astype(jnp.bfloat16)
+            return carry
+
+        lax.fori_loop(0, rows // step_rows, body, 0)
 
 
 def marks(owner, shard_n):
@@ -176,21 +173,25 @@
     for group in copies:
         for copy in group:
             copy.start()
-    both = None
-    for side in range(2):
-        for copy in copies[side]:
-            copy.wait()
-        columns = pl.ds(pl.multiple_of((1 - h if side else h) * rows, rows), rows)
-        term = jnp.dot(
-            normed[:, columns], up_w[side * rows : (side + 1) * rows, :], preferred_element_type=jnp.float32
-        )
-        both = term if both is None else both + term
     cut = units // 128 * 128
     tail = units - cut
-    hidden[:, :cut] = (gelu(both[:, :cut]) * both[:, 2 * units - cut :]).astype(jnp.bfloat16)
-    if tail:
-        edge = both[:, cut : cut + 2 * tail]
-        hidden[:, cut : cut + 2 * tail] = (gelu(edge) * pltpu.roll(edge, tail, 1)).astype(jnp.bfloat16)
+    tokens = normed.shape[0] // 2
+    for part in range(2):
+        at = slice(part * tokens, (part + 1) * tokens)
+        both = None
+        for side in range(2):
+            if part == 0:
+                for copy in copies[side]:
+                    copy.wait()
+            columns = pl.ds(pl.multiple_of((1 - h if side else h) * rows, rows), rows)
+            term = jnp.dot(
+                normed[at, columns], up_w[side * rows : (side + 1) * rows, :], preferred_element_type=jnp.float32
+            )
+            both = term if both is None else both + term
+        hidden[at, :cut] = (gelu(both[:, :cut]) * both[:, 2 * units - cut :]).astype(jnp.bfloat16)
+        if tail:
+            edge = both[:, cut : cut + 2 * tail]
+            hidden[at, cut : cut + 2 * tail] = (gelu(edge) * pltpu.roll(edge, tail, 1)).astype(jnp.bfloat16)
     value = jnp.dot(pool[...], hidden[...], preferred_element_type=jnp.float32)[:, :units]
     high = value.astype(jnp.bfloat16).astype(jnp.float32)
     low = value - high
@@ -347,7 +348,9 @@
 
     rows = p_count * length + q_count * q_length
     gain_rows = jnp.broadcast_to(norm_gain[None, :], (16, width))
-    tokens = jnp.concatenate([passage_tokens.reshape(-1, width), query_tokens.reshape(-1, width)], axis=0)
+    tokens = jnp.concatenate(
+        [passage_tokens.reshape(-1, width), query_tokens.reshape(-1, width), gain_rows], axis=0
+    )
     request_count = q_count * k_count
     owner = neg_owner.reshape(1, request_count)
     requests = pl.pallas_call(
@@ -359,23 +362,13 @@
         name="ask",
     )(owner, neg_row.reshape(1, request_count))
 
-    other, mate_tokens, requests = lax.optimization_barrier((other, mate_move(tokens), requests))
-    merged = pl.pallas_call(
-        merge_kernel,
-        out_shape=jax.ShapeDtypeStruct((w_gate.shape[0], 6 * units), bf16),
-        in_specs=[whole()] * 2,
-        out_specs=whole(),
-        compiler_params=params(),
-        name="merge",
-    )(own, other)
-    weights = along_y(merged)
-
-    flip = lax.axis_index("section") % 2 == 1
-    tokens = jnp.concatenate(
-        [jnp.where(flip, mate_tokens, tokens), jnp.where(flip, tokens, mate_tokens), gain_rows], axis=0
-    )
+    low, high = mp_move(tokens, 1, 0), mp_move(tokens, -1, 0)
+    other, requests, low, high = lax.optimization_barrier((other, requests, low, high))
+    gap = 6 * units - wide
+    weights = along_y(jnp.pad(own, ((0, 0), (0, gap))) + jnp.pad(other, ((0, 0), (gap, 0))))
+
     wanted = lax.all_to_all(requests, ("section", "dp"), 0, 0, tiled=True)
-    near, far, wanted = x_blocks(tokens, wanted)
+    near, far, wanted = spread(tokens, low, high, wanted)
     found = pl.pallas_call(
         find_kernel,
         out_shape=jax.ShapeDtypeStruct((shard_count, 2, 128), f32),
@@ -387,7 +380,7 @@
     fetched = lax.all_to_all(found, ("section", "dp"), 0, 0, tiled=True)
 
     normed = pl.pallas_call(
-        functools.partial(norm_kernel, mp_n // 2, 2 * rows),
+        functools.partial(norm_kernel, mp_n // 2, rows),
         out_shape=jax.ShapeDtypeStruct((2 * rows, features), bf16),
         in_specs=[whole()] * 2,
         out_specs=whole(),

time: 154 us -> 153 us (level)
  blocking collectives: 9.23 us -> 31.5 us
  waiting for transfers between devices: 42.5 us -> 28.7 us
  starting transfers between devices: 59.7 us -> 52.9 us
  local copies, waits for them, and re-layouts: 7.03 us -> 4.83 us
  Pallas kernels: 19.5 us -> 17.4 us
  other arithmetic: 1.24 us -> 2.86 us
    all_to_all x0 -> x1, blocking collectives: none -> 22.2 us  [shards(): wanted = lax.all_to_all(requests, ('section', 'dp'), 0, 0, tiled=True)]
    all_to_all x1 -> x0, waiting for transfers between devices: 11 us -> none  [shards(): wanted = lax.all_to_all(requests, ('section', 'dp'), 0, 0, tiled=True)]
    all_to_all x1 -> x0, starting transfers between devices: 10 us -> none  [shards(): wanted = lax.all_to_all(requests, ('section', 'dp'), 0, 0, tiled=True)]
    ppermute x4, waiting for transfers between devices: 0.01 us -> 7.1 us  [mp_move(): return lax.ppermute(block, 'mp', perm)]
    ppermute x1, waiting for transfers between devices: 7.05 us -> 0.01 us  [mate_move(): lax.ppermute(block, 'section', [(s, s ^ 1) for s in range(lax.axis_size('...]
    all_gather x1, waiting for transfers between devices: 6 us -> 3.12 us  [along_y(): lax.all_gather(block, 'dp', axis=0, axis_index_groups=groups, tiled=True)]
    all_to_all x1, starting transfers between devices: 5.45 us -> 7.71 us  [shards(): fetched = lax.all_to_all(found, ('section', 'dp'), 0, 0, tiled=True)]
    unnamed x23, local copies, waits for them, and re-layouts: 3.72 us -> 1.8 us
  transfers between devices with their start and end apart: 11 -> 10, of which waited for: 5 -> 6; matrix products, arithmetic and copies ran while one was open for 3% -> 3% of each run, Pallas kernels for 9% -> 8%
where the time goes in v3:
time: 153 us
  starting transfers between devices  52.9 us (35%)
  blocking collectives  31.5 us (21%)
  waiting for transfers between devices  28.7 us (19%)
  Pallas kernels  17.4 us (11%)
  between operations  14.3 us (9%)
  local copies, waits for them, and re-layouts  4.83 us (3%)
  other arithmetic  2.86 us (2%)
    all_to_all x1, blocking collectives, shards(): wanted = lax.all_to_all(requests, ('section', 'dp'), 0, 0, tiled=True)  22.2 us
    ppermute x4, starting transfers between devices, mp_move(): return lax.ppermute(block, 'mp', perm)  13.6 us
    all_to_all x1, waiting for transfers between devices, shards(): arrived = lax.all_to_all(message, ('section', 'dp'), 0, 0, tiled=True)  12 us
    all_to_all x1, starting transfers between devices, shards(): arrived = lax.all_to_all(message, ('section', 'dp'), 0, 0, tiled=True)  11.6 us
    ppermute x1, starting transfers between devices, half_move(): return lax.ppermute(block, ('section', 'dp'), perm)  10.9 us
    all_to_all x1, blocking collectives, shards(): messages = lax.all_to_all(message, 'mp', 0, 0, tiled=True)  9.23 us
    pallas_call x1, Pallas kernels, shards(): pl.pallas_call(functools.partial(hidden_kernel, units), out_shape=jax.Sha...  7.74 us
    all_to_all x1, starting transfers between devices, shards(): fetched = lax.all_to_all(found, ('section', 'dp'), 0, 0, tiled=True)  7.71 us
  transfers between devices with their start and end apart: 10, of which 6 were waited for; matrix products, arithmetic and copies ran while one was open for 3% of the time, Pallas kernels for 8%

profile of v3, /device:TPU:8, one launch (start us, length us, event | category | flops | bytes accessed | tf_op | source)
XLA Modules:
  0.0 152.5 jit_solution(13743550420888692905)
XLA Ops:
  7.2 2.1 %cut.1 = (bf16[128,1024]{1,0:T(8,128)(2,1)}, bf16[128,1024]{1,0:T(8,128)(2,1)}) custom-call(bf16[128,640]{1,0:T(8,128)(2,1)} %gate_in.1, bf16[128,640]{1,0:T(8,128)(2,1)} %up_in.1, bf16[640,128]{1,0:T(8,128)(2,1)} %down_in.1), custom_call_target="tpu_custom_call" | custom-call | tf_op jit(solution)/shard_map/cut/pallas_call | solution.py:338
  9.4 10.9 %collective-permute-start = (bf16[128,1024]{1,0:T(8,128)(2,1)}, bf16[128,1024]{1,0:T(8,128)(2,1)S(1)}, u32[]{:S(2)}, u32[]{:S(2)}) collective-permute-start(bf16[128,1024]{1,0:T(8,128)(2,1)} %get-tuple-element.16), channel_id=1, source_target_pairs={{0,320},{8,328},{16,336},{24,344},{32,352},{40,360},{48,368},{56,3... | collective-permute-start | bytes 786440 | tf_op jit(solution)/shard_map/ppermute | solution.py:51
  20.3 0.7 broadcast_in_dim.4
  21.0 1.0 pad_maximum_fusion
  22.0 3.4 %collective-permute-start.1 = (bf16[400,256]{1,0:T(8,128)(2,1)S(1)}, bf16[400,256]{1,0:T(8,128)(2,1)S(1)}, u32[]{:S(2)}, u32[]{:S(2)}) collective-permute-start(bf16[400,256]{1,0:T(8,128)(2,1)S(1)} %pad_maximum_fusion), channel_id=1, source_target_pairs={{0,2},{1,3},{2,4},{3,5},{4,6},{5,7},{6,0},{7,1},{8,10},{9,11},{10,... | collective-permute-start | bytes 614408 | tf_op jit(solution)/shard_map/ppermute | solution.py:36
  25.4 3.7 %collective-permute-start.2 = (bf16[400,256]{1,0:T(8,128)(2,1)S(1)}, bf16[400,256]{1,0:T(8,128)(2,1)S(1)}, u32[]{:S(2)}, u32[]{:S(2)}) collective-permute-start(bf16[400,256]{1,0:T(8,128)(2,1)S(1)} %pad_maximum_fusion), channel_id=1, source_target_pairs={{0,6},{1,7},{2,0},{3,1},{4,2},{5,3},{6,4},{7,5},{8,14},{9,15},{10,... | collective-permute-start | bytes 614408 | tf_op jit(solution)/shard_map/ppermute | solution.py:36
  29.0 0.8 reshape.26.owner
  29.8 0.8 reshape.27.row
  30.6 0.2 ask.1
  30.8 0.9 collective-permute-done.1
  31.6 1.9 %collective-permute-done.2 = bf16[400,256]{1,0:T(8,128)(2,1)S(1)} collective-permute-done((bf16[400,256]{1,0:T(8,128)(2,1)S(1)}, bf16[400,256]{1,0:T(8,128)(2,1)S(1)}, u32[]{:S(2)}, u32[]{:S(2)}) %collective-permute-start.2) | collective-permute-done | bytes 204832 | tf_op jit(solution)/shard_map/ppermute | solution.py:36
  33.5 1.8 %pad_add_fusion = bf16[128,1920]{1,0:T(8,128)(2,1)} fusion(bf16[128,1024]{1,0:T(8,128)(2,1)S(1)} %collective-permute-done, bf16[128,1024]{1,0:T(8,128)(2,1)} %get-tuple-element.21), kind=kLoop, calls=%fused_computation | loop fusion | flops 983040 | bytes 1015808 | tf_op jit(solution)/shard_map/add | solution.py:368
  35.3 4.6 %collective-permute-start.3 = (bf16[400,256]{1,0:T(8,128)(2,1)S(1)}, bf16[400,256]{1,0:T(8,128)(2,1)S(1)}, u32[]{:S(2)}, u32[]{:S(2)}) collective-permute-start(bf16[400,256]{1,0:T(8,128)(2,1)S(1)} %pad_maximum_fusion), channel_id=1, source_target_pairs={{0,4},{1,5},{2,6},{3,7},{4,0},{5,1},{6,2},{7,3},{8,12},{9,13},{10,... | collective-permute-start | bytes 614408 | tf_op jit(solution)/shard_map/ppermute | solution.py:36
  40.1 4.3 %collective-permute-done.3 = bf16[400,256]{1,0:T(8,128)(2,1)S(1)} collective-permute-done((bf16[400,256]{1,0:T(8,128)(2,1)S(1)}, bf16[400,256]{1,0:T(8,128)(2,1)S(1)}, u32[]{:S(2)}, u32[]{:S(2)}) %collective-permute-start.3) | collective-permute-done | bytes 204832 | tf_op jit(solution)/shard_map/ppermute | solution.py:36
  44.5 3.6 %collective-permute-start.4 = (bf16[1600,256]{1,0:T(8,128)(2,1)S(1)}, bf16[1600,256]{1,0:T(8,128)(2,1)S(1)}, u32[]{:S(2)}, u32[]{:S(2)}) collective-permute-start(bf16[1600,256]{1,0:T(8,128)(2,1)S(1)} %get-tuple-element.29), channel_id=1, source_target_pairs={{0,128},{128,0},{256,384},{384,256},{1,129},{129,1},{257,385},{385... | collective-permute-start | bytes 2457608 | tf_op jit(solution)/shard_map/ppermute | solution.py:40
  48.1 22.2 %all_to_all.32 = s32[64,1,128]{2,1,0:T(1,128)S(1)} all-to-all(s32[64,1,128]{2,1,0:T(1,128)S(1)} %bitcast.9), channel_id=1, replica_groups=mesh['section'=4,'dp'=16,'mp'=8] {'section','dp'}, dimensions={0} | all-to-all | bytes 65536 | tf_op jit(solution)/shard_map/all_to_all | solution.py:370
  70.3 1.9 %collective-permute-start.5 = (bf16[3200,256]{1,0:T(8,128)(2,1)S(1)}, bf16[3200,256]{1,0:T(8,128)(2,1)S(1)}, u32[]{:S(2)}, u32[]{:S(2)}) collective-permute-start(bf16[3200,256]{1,0:T(8,128)(2,1)S(1)} %constant_dynamic-update-slice_fusion.6.near), channel_id=1, source_target_pairs={{0,1},{1,0},{2,3},{3,2},{4,5},{5,4},{6,7},{7,6},{8,9},{9,8},{10,11... | collective-permute-start | bytes 4915208 | tf_op jit(solution)/shard_map/ppermute | solution.py:36
  72.3 1.1 find.1
  73.4 7.7 %all-to-all-start.2 = ((f32[64,2,128]{2,1,0:T(2,128)}), f32[64,2,128]{2,1,0:T(2,128)S(1)}, u32[]{:S(2)}, u32[]{:S(2)}) async-start(f32[64,2,128]{2,1,0:T(2,128)} %find.1), calls=%async_computation.2 | async-start | bytes 131072 | tf_op jit(solution)/shard_map/all_to_all | solution.py:380
  81.2 3.2 %norm.1.normed = bf16[768,2048]{1,0:T(8,128)(2,1)S(1)} custom-call(bf16[3200,256]{1,0:T(8,128)(2,1)S(1)} %constant_dynamic-update-slice_fusion.6.near, bf16[3200,256]{1,0:T(8,128)(2,1)S(1)} %collective-permute-done.5.far), custom_call_target="tpu_custom_call" | custom-call | tf_op jit(solution)/shard_map/norm/pallas_call | solution.py:382
  84.4 1.7 %copy-done = bf16[768,2048]{1,0:T(8,128)(2,1)} copy-done((bf16[768,2048]{1,0:T(8,128)(2,1)}, bf16[768,2048]{1,0:T(8,128)(2,1)S(1)}, u32[]{:S(2)}) %copy-start) | copy-done | bytes 3145752
  86.0 3.1 %all-gather.2.cloned.1.call-done.weights = bf16[1024,1920]{1,0:T(8,128)(2,1)} async-done(((bf16[128,1920]{1,0:T(8,128)(2,1)}), bf16[1024,1920]{1,0:T(8,128)(2,1)}) %all-gather.2.cloned.1.call-update) | async-done | bytes 3932176 | tf_op jit(solution)/shard_map/all_gather | solution.py:57
  89.2 7.7 %hidden.1 = f32[16,8,256]{2,1,0:T(8,128)} custom-call(bf16[768,2048]{1,0:T(8,128)(2,1)} %copy-done, bf16[16,768]{1,0:T(8,128)(2,1)S(1)} %copy-done.4, bf16[1024,1920]{1,0:T(8,128)(2,1)} %all-gather.2.cloned.1.call-done.weights), custom_call_target="tpu_custom_call" | custom-call | tf_op jit(solution)/shard_map/hidden/pallas_call | solution.py:400
  96.9 5.4 %all-to-all-start.1 = ((f32[16,8,256]{2,1,0:T(8,128)}), f32[16,8,256]{2,1,0:T(8,128)S(1)}, u32[]{:S(2)}, u32[]{:S(2)}) async-start(f32[16,8,256]{2,1,0:T(8,128)} %hidden.1), calls=%async_computation.1 | async-start | bytes 262144 | tf_op jit(solution)/shard_map/all_to_all | solution.py:416
  102.5 6.5 %all-to-all-done.1.parts = f32[16,8,256]{2,1,0:T(8,128)S(1)} async-done(((f32[16,8,256]{2,1,0:T(8,128)}), f32[16,8,256]{2,1,0:T(8,128)S(1)}, u32[]{:S(2)}, u32[]{:S(2)}) %all-to-all-start.1) | async-done | bytes 131104 | tf_op jit(solution)/shard_map/all_to_all | solution.py:416
  109.1 0.7 head.1
  109.8 9.2 %all_to_all.33.messages = bf16[8,96,128]{2,1,0:T(8,128)(2,1)S(1)} all-to-all(bf16[8,96,128]{2,1,0:T(8,128)(2,1)S(1)} %get-tuple-element.24), channel_id=1, replica_groups=mesh['section'=4,'dp'=16,'mp'=8] {'mp'}, dimensions={0} | all-to-all | bytes 393216 | tf_op jit(solution)/shard_map/all_to_all | solution.py:445
  119.0 1.6 %loss.1 = (bf16[2,96]{1,0:T(2,128)(2,1)}, f32[4,128]{1,0:T(4,128)S(1)}, bf16[64,4,384]{2,1,0:T(4,128)(2,1)}) custom-call(s32[4]{0:T(128)S(1)} %copy-done.5, bf16[8,96,128]{2,1,0:T(8,128)(2,1)S(1)} %all_to_all.33.messages, bf16[8,256]{1,0:T(8,128)(2,1)S(1)} %get-tuple-element.25.pooled), custom_call_target="tpu_custom_call" | custom-call | tf_op jit(solution)/shard_map/loss/pallas_call | solution.py:447
  120.6 11.6 %all-to-all-start.4 = ((bf16[64,4,384]{2,1,0:T(4,128)(2,1)}), bf16[64,4,384]{2,1,0:T(4,128)(2,1)S(1)}, u32[]{:S(2)}, u32[]{:S(2)}) async-start(bf16[64,4,384]{2,1,0:T(4,128)(2,1)} %get-tuple-element.28), calls=%async_computation.4 | async-start | bytes 393216 | tf_op jit(solution)/shard_map/all_to_all | solution.py:461
  132.2 0.6 slice_reduce_fusion
  132.9 12.0 %all-to-all-done.4 = bf16[64,4,384]{2,1,0:T(4,128)(2,1)S(1)} async-done(((bf16[64,4,384]{2,1,0:T(4,128)(2,1)}), bf16[64,4,384]{2,1,0:T(4,128)(2,1)S(1)}, u32[]{:S(2)}, u32[]{:S(2)}) %all-to-all-start.4) | async-done | bytes 196640 | tf_op jit(solution)/shard_map/all_to_all | solution.py:461
  144.9 0.8 grad.1
  (38 shorter events, 0.6 us)
Async XLA Ops:
  7.2 32.8 %copy-start.6 = (bf16[2,128,256]{2,1,0:T(8,128)(2,1)S(1)}, bf16[2,128,256]{2,1,0:T(8,128)(2,1)}, u32[]{:S(2)}) copy-start(bf16[2,128,256]{2,1,0:T(8,128)(2,1)} %param.13) | copy-start | bytes 393220
  7.2 32.8 %copy-start.7 = (bf16[4,32,256]{2,1,0:T(8,128)(2,1)S(1)}, bf16[4,32,256]{2,1,0:T(8,128)(2,1)}, u32[]{:S(2)}) copy-start(bf16[4,32,256]{2,1,0:T(8,128)(2,1)} %param.14) | copy-start | bytes 196612
  7.2 32.8 %copy-start.8 = (bf16[256]{0:T(256)(128)(2,1)S(1)}, bf16[256]{0:T(256)(128)(2,1)}, u32[]{:S(2)}) copy-start(bf16[256]{0:T(256)(128)(2,1)} %param.15) | copy-start | bytes 1540
  7.2 82.0 %all-gather.2.cloned.1.call-start = ((), (), s32[]{:S(2)}) async-start(), calls=%async_computation.5 | async-start | bytes 4423680 | tf_op jit(solution)/shard_map/all_gather | solution.py:57
  9.4 24.1 %collective-permute-start = (bf16[128,1024]{1,0:T(8,128)(2,1)}, bf16[128,1024]{1,0:T(8,128)(2,1)S(1)}, u32[]{:S(2)}, u32[]{:S(2)}) collective-permute-start(bf16[128,1024]{1,0:T(8,128)(2,1)} %get-tuple-element.16), channel_id=1, source_target_pairs={{0,320},{8,328},{16,336},{24,344},{32,352},{40,360},{48,368},{56,3... | collective-permute-start | bytes 786440 | tf_op jit(solution)/shard_map/ppermute | solution.py:51
  22.0 9.6 %collective-permute-start.1 = (bf16[400,256]{1,0:T(8,128)(2,1)S(1)}, bf16[400,256]{1,0:T(8,128)(2,1)S(1)}, u32[]{:S(2)}, u32[]{:S(2)}) collective-permute-start(bf16[400,256]{1,0:T(8,128)(2,1)S(1)} %pad_maximum_fusion), channel_id=1, source_target_pairs={{0,2},{1,3},{2,4},{3,5},{4,6},{5,7},{6,0},{7,1},{8,10},{9,11},{10,... | collective-permute-start | bytes 614408 | tf_op jit(solution)/shard_map/ppermute | solution.py:36
  25.4 8.2 %collective-permute-start.2 = (bf16[400,256]{1,0:T(8,128)(2,1)S(1)}, bf16[400,256]{1,0:T(8,128)(2,1)S(1)}, u32[]{:S(2)}, u32[]{:S(2)}) collective-permute-start(bf16[400,256]{1,0:T(8,128)(2,1)S(1)} %pad_maximum_fusion), channel_id=1, source_target_pairs={{0,6},{1,7},{2,0},{3,1},{4,2},{5,3},{6,4},{7,5},{8,14},{9,15},{10,... | collective-permute-start | bytes 614408 | tf_op jit(solution)/shard_map/ppermute | solution.py:36
  35.3 9.2 %collective-permute-start.3 = (bf16[400,256]{1,0:T(8,128)(2,1)S(1)}, bf16[400,256]{1,0:T(8,128)(2,1)S(1)}, u32[]{:S(2)}, u32[]{:S(2)}) collective-permute-start(bf16[400,256]{1,0:T(8,128)(2,1)S(1)} %pad_maximum_fusion), channel_id=1, source_target_pairs={{0,4},{1,5},{2,6},{3,7},{4,0},{5,1},{6,2},{7,3},{8,12},{9,13},{10,... | collective-permute-start | bytes 614408 | tf_op jit(solution)/shard_map/ppermute | solution.py:36
  40.1 32.2 %copy-start.3 = (bf16[2048,96]{0,1:T(8,128)(2,1)S(1)}, bf16[2048,96]{0,1:T(8,128)(2,1)}, u32[]{:S(2)}) copy-start(bf16[2048,96]{0,1:T(8,128)(2,1)} %param.21) | copy-start | bytes 1179652
  44.5 25.8 %collective-permute-start.4 = (bf16[1600,256]{1,0:T(8,128)(2,1)S(1)}, bf16[1600,256]{1,0:T(8,128)(2,1)S(1)}, u32[]{:S(2)}, u32[]{:S(2)}) collective-permute-start(bf16[1600,256]{1,0:T(8,128)(2,1)S(1)} %get-tuple-element.29), channel_id=1, source_target_pairs={{0,128},{128,0},{256,384},{384,256},{1,129},{129,1},{257,385},{385... | collective-permute-start | bytes 2457608 | tf_op jit(solution)/shard_map/ppermute | solution.py:40
  70.3 10.8 %collective-permute-start.5 = (bf16[3200,256]{1,0:T(8,128)(2,1)S(1)}, bf16[3200,256]{1,0:T(8,128)(2,1)S(1)}, u32[]{:S(2)}, u32[]{:S(2)}) collective-permute-start(bf16[3200,256]{1,0:T(8,128)(2,1)S(1)} %constant_dynamic-update-slice_fusion.6.near), channel_id=1, source_target_pairs={{0,1},{1,0},{2,3},{3,2},{4,5},{5,4},{6,7},{7,6},{8,9},{9,8},{10,11... | collective-permute-start | bytes 4915208 | tf_op jit(solution)/shard_map/ppermute | solution.py:36
  73.4 23.5 %all-to-all-start.2 = ((f32[64,2,128]{2,1,0:T(2,128)}), f32[64,2,128]{2,1,0:T(2,128)S(1)}, u32[]{:S(2)}, u32[]{:S(2)}) async-start(f32[64,2,128]{2,1,0:T(2,128)} %find.1), calls=%async_computation.2 | async-start | bytes 131072 | tf_op jit(solution)/shard_map/all_to_all | solution.py:380
  81.2 8.0 %copy-start.4 = (bf16[16,768]{1,0:T(8,128)(2,1)S(1)}, bf16[16,768]{1,0:T(8,128)(2,1)}, u32[]{:S(2)}) copy-start(bf16[16,768]{1,0:T(8,128)(2,1)} %constant.14.clone.pool) | copy-start | bytes 73732
  84.4 1.7 %copy-start = (bf16[768,2048]{1,0:T(8,128)(2,1)}, bf16[768,2048]{1,0:T(8,128)(2,1)S(1)}, u32[]{:S(2)}) copy-start(bf16[768,2048]{1,0:T(8,128)(2,1)S(1)} %norm.1.normed) | copy-start | bytes 9437188
  86.0 23.0 %copy-start.1 = (bf16[256,768]{1,0:T(8,128)(2,1)S(1)}, bf16[256,768]{1,0:T(8,128)(2,1)}, u32[]{:S(2)}) copy-start(bf16[256,768]{1,0:T(8,128)(2,1)} %old_head.1) | copy-start | bytes 1179652
  86.0 23.0 %copy-start.2 = (bf16[256,768]{1,0:T(8,128)(2,1)S(1)}, bf16[256,768]{1,0:T(8,128)(2,1)}, u32[]{:S(2)}) copy-start(bf16[256,768]{1,0:T(8,128)(2,1)} %new_head.1) | copy-start | bytes 1179652
  96.9 22.1 %copy-start.5 = (s32[4]{0:T(128)S(1)}, s32[4]{0:T(128)}, u32[]{:S(2)}) copy-start(s32[4]{0:T(128)} %slot.1) | copy-start | bytes 52
  96.9 12.1 %all-to-all-start.1 = ((f32[16,8,256]{2,1,0:T(8,128)}), f32[16,8,256]{2,1,0:T(8,128)S(1)}, u32[]{:S(2)}, u32[]{:S(2)}) async-start(f32[16,8,256]{2,1,0:T(8,128)} %hidden.1), calls=%async_computation.1 | async-start | bytes 262144 | tf_op jit(solution)/shard_map/all_to_all | solution.py:416
  120.6 24.2 %all-to-all-start.4 = ((bf16[64,4,384]{2,1,0:T(4,128)(2,1)}), bf16[64,4,384]{2,1,0:T(4,128)(2,1)S(1)}, u32[]{:S(2)}, u32[]{:S(2)}) async-start(bf16[64,4,384]{2,1,0:T(4,128)(2,1)} %get-tuple-element.28), calls=%async_computation.4 | async-start | bytes 393216 | tf_op jit(solution)/shard_map/all_to_all | solution.py:461
Sparse Core Ops, SparseCore 0:
  35.4 53.6 all-gather.1

commit v4 on v3

--- a/solution.py
+++ b/solution.py
@@ -73,8 +73,8 @@
         fetch.start()
     units = gate.shape[1] // 2
     cut = units // 128 * 128
-    gap = own.shape[1] - 3 * units
-    own[:, 3 * units :] = jnp.zeros((own.shape[0], gap), own.dtype)
+    gap = other.shape[1] - 3 * units
+    own[:, 3 * units :] = jnp.zeros((own.shape[0], own.shape[1] - 3 * units), own.dtype)
     other[:, :gap] = jnp.zeros((own.shape[0], gap), own.dtype)
     for fetch in fetches:
         fetch.wait()
@@ -337,7 +337,7 @@
     wide = -(-3 * units // 128) * 128
     own, other = pl.pallas_call(
         cut_kernel,
-        out_shape=[jax.ShapeDtypeStruct((w_gate.shape[0], wide), bf16)] * 2,
+        out_shape=[jax.ShapeDtypeStruct((w_gate.shape[0], lanes), bf16) for lanes in (6 * units, wide)],
         in_specs=[in_hbm()] * 3,
         out_specs=[whole()] * 2,
         scratch_shapes=[pltpu.VMEM(w.shape, bf16) for w in (w_gate, w_up, w_down)] + [pltpu.SemaphoreType.DMA((3,))],
@@ -363,9 +363,9 @@
     )(owner, neg_row.reshape(1, request_count))
 
     low, high = mp_move(tokens, 1, 0), mp_move(tokens, -1, 0)
-    other, requests, low, high = lax.optimization_barrier((other, requests, low, high))
-    gap = 6 * units - wide
-    weights = along_y(jnp.pad(own, ((0, 0), (0, gap))) + jnp.pad(other, ((0, 0), (gap, 0))))
+    other, requests, low = lax.optimization_barrier((other, requests, low))
+    edge = 6 * units - wide
+    weights = along_y(lax.dynamic_update_slice(own, own[:, edge:] + other, (0, edge)))
 
     wanted = lax.all_to_all(requests, ("section", "dp"), 0, 0, tiled=True)
     near, far, wanted = spread(tokens, low, high, wanted)

time: 153 us -> 156 us (1.020)
    ppermute x4, waiting for transfers between devices: 7.1 us -> 10.8 us  [mp_move(): return lax.ppermute(block, 'mp', perm)]
    all_gather x1, waiting for transfers between devices: 3.12 us -> 0.01 us  [along_y(): lax.all_gather(block, 'dp', axis=0, axis_index_groups=groups, tiled=True)]
    add x1 -> x0, other arithmetic: 1.76 us -> none  [shards(): jnp.pad(own, ((0, 0), (0, gap))) + jnp.pad(other, ((0, 0), (gap, 0)))]
    dynamic_update_slice x0 -> x1, other arithmetic: none -> 1.72 us  [shards(): lax.dynamic_update_slice(own, own[:, edge:] + other, (0, edge))]
where the time goes in v4:
time: 156 us; the launch traced here: 155 us
  starting transfers between devices  54.4 us (35%)
  blocking collectives  31.5 us (20%)
  waiting for transfers between devices  29.5 us (19%)
  Pallas kernels  17.6 us (11%)
  between operations  14.3 us (9%)
  local copies, waits for them, and re-layouts  4.83 us (3%)
  other arithmetic  2.82 us (2%)
    all_to_all x1, blocking collectives, shards(): wanted = lax.all_to_all(requests, ('section', 'dp'), 0, 0, tiled=True)  22.2 us
    ppermute x4, starting transfers between devices, mp_move(): return lax.ppermute(block, 'mp', perm)  12.7 us
    all_to_all x1, waiting for transfers between devices, shards(): arrived = lax.all_to_all(message, ('section', 'dp'), 0, 0, tiled=True)  12 us
    all_to_all x1, starting transfers between devices, shards(): arrived = lax.all_to_all(message, ('section', 'dp'), 0, 0, tiled=True)  11.7 us
    ppermute x1, starting transfers between devices, half_move(): return lax.ppermute(block, ('section', 'dp'), perm)  10.9 us
    ppermute x4, waiting for transfers between devices, mp_move(): return lax.ppermute(block, 'mp', perm)  10.8 us
    all_to_all x1, blocking collectives, shards(): messages = lax.all_to_all(message, 'mp', 0, 0, tiled=True)  9.23 us
    all_to_all x1, starting transfers between devices, shards(): fetched = lax.all_to_all(found, ('section', 'dp'), 0, 0, tiled=True)  8.89 us
  transfers between devices with their start and end apart: 10, of which 6 were waited for; matrix products, arithmetic and copies ran while one was open for 3% of the time, Pallas kernels for 8%

profile of v4, /device:TPU:8, one launch (start us, length us, event | category | flops | bytes accessed | tf_op | source)
XLA Modules:
  0.0 154.9 jit_solution(17638848790673729402)
XLA Ops:
  7.2 2.2 %cut.1 = (bf16[128,1920]{1,0:T(8,128)(2,1)}, bf16[128,1024]{1,0:T(8,128)(2,1)}) custom-call(bf16[128,640]{1,0:T(8,128)(2,1)} %gate_in.1, bf16[128,640]{1,0:T(8,128)(2,1)} %up_in.1, bf16[640,128]{1,0:T(8,128)(2,1)} %down_in.1), custom_call_target="tpu_custom_call" | custom-call | tf_op jit(solution)/shard_map/cut/pallas_call | solution.py:338
  9.5 10.9 %collective-permute-start = (bf16[128,1024]{1,0:T(8,128)(2,1)}, bf16[128,1024]{1,0:T(8,128)(2,1)S(1)}, u32[]{:S(2)}, u32[]{:S(2)}) collective-permute-start(bf16[128,1024]{1,0:T(8,128)(2,1)} %get-tuple-element.15), channel_id=1, source_target_pairs={{0,320},{8,328},{16,336},{24,344},{32,352},{40,360},{48,368},{56,3... | collective-permute-start | bytes 786440 | tf_op jit(solution)/shard_map/ppermute | solution.py:51
  20.4 0.7 broadcast_in_dim.4
  21.1 1.0 pad_maximum_fusion
  22.0 3.4 %collective-permute-start.1 = (bf16[400,256]{1,0:T(8,128)(2,1)S(1)}, bf16[400,256]{1,0:T(8,128)(2,1)S(1)}, u32[]{:S(2)}, u32[]{:S(2)}) collective-permute-start(bf16[400,256]{1,0:T(8,128)(2,1)S(1)} %pad_maximum_fusion), channel_id=1, source_target_pairs={{0,2},{1,3},{2,4},{3,5},{4,6},{5,7},{6,0},{7,1},{8,10},{9,11},{10,... | collective-permute-start | bytes 614408 | tf_op jit(solution)/shard_map/ppermute | solution.py:36
  25.4 0.8 reshape.26.owner
  26.2 0.8 reshape.27.row
  27.0 0.2 ask.1
  27.2 4.5 %collective-permute-done.1 = bf16[400,256]{1,0:T(8,128)(2,1)S(1)} collective-permute-done((bf16[400,256]{1,0:T(8,128)(2,1)S(1)}, bf16[400,256]{1,0:T(8,128)(2,1)S(1)}, u32[]{:S(2)}, u32[]{:S(2)}) %collective-permute-start.1) | collective-permute-done | bytes 204832 | tf_op jit(solution)/shard_map/ppermute | solution.py:36
  31.7 0.2 collective-permute-done
  31.9 1.7 %add_dynamic-update-slice_fusion = bf16[128,1920]{1,0:T(8,128)(2,1)} fusion(bf16[128,1920]{1,0:T(8,128)(2,1)} %get-tuple-element.19, bf16[128,1024]{1,0:T(8,128)(2,1)S(1)} %collective-permute-done), kind=kLoop, calls=%fused_computation.1 | loop fusion | flops 524288 | bytes 786432 | tf_op jit(solution)/shard_map/dynamic_update_slice | solution.py:368
  33.6 4.7 %collective-permute-start.2 = (bf16[400,256]{1,0:T(8,128)(2,1)S(1)}, bf16[400,256]{1,0:T(8,128)(2,1)S(1)}, u32[]{:S(2)}, u32[]{:S(2)}) collective-permute-start(bf16[400,256]{1,0:T(8,128)(2,1)S(1)} %pad_maximum_fusion), channel_id=1, source_target_pairs={{0,6},{1,7},{2,0},{3,1},{4,2},{5,3},{6,4},{7,5},{8,14},{9,15},{10,... | collective-permute-start | bytes 614408 | tf_op jit(solution)/shard_map/ppermute | solution.py:36
  38.3 2.7 %collective-permute-start.3 = (bf16[400,256]{1,0:T(8,128)(2,1)S(1)}, bf16[400,256]{1,0:T(8,128)(2,1)S(1)}, u32[]{:S(2)}, u32[]{:S(2)}) collective-permute-start(bf16[400,256]{1,0:T(8,128)(2,1)S(1)} %pad_maximum_fusion), channel_id=1, source_target_pairs={{0,4},{1,5},{2,6},{3,7},{4,0},{5,1},{6,2},{7,3},{8,12},{9,13},{10,... | collective-permute-start | bytes 614408 | tf_op jit(solution)/shard_map/ppermute | solution.py:36
  41.2 5.0 %collective-permute-done.2 = bf16[400,256]{1,0:T(8,128)(2,1)S(1)} collective-permute-done((bf16[400,256]{1,0:T(8,128)(2,1)S(1)}, bf16[400,256]{1,0:T(8,128)(2,1)S(1)}, u32[]{:S(2)}, u32[]{:S(2)}) %collective-permute-start.2) | collective-permute-done | bytes 204832 | tf_op jit(solution)/shard_map/ppermute | solution.py:36
  46.2 1.2 collective-permute-done.3
  47.5 5.0 %collective-permute-start.4 = (bf16[1600,256]{1,0:T(8,128)(2,1)S(1)}, bf16[1600,256]{1,0:T(8,128)(2,1)S(1)}, u32[]{:S(2)}, u32[]{:S(2)}) collective-permute-start(bf16[1600,256]{1,0:T(8,128)(2,1)S(1)} %get-tuple-element.27), channel_id=1, source_target_pairs={{0,128},{128,0},{256,384},{384,256},{1,129},{129,1},{257,385},{385... | collective-permute-start | bytes 2457608 | tf_op jit(solution)/shard_map/ppermute | solution.py:40
  52.5 22.2 %all_to_all.32 = s32[64,1,128]{2,1,0:T(1,128)S(1)} all-to-all(s32[64,1,128]{2,1,0:T(1,128)S(1)} %bitcast.9), channel_id=1, replica_groups=mesh['section'=4,'dp'=16,'mp'=8] {'section','dp'}, dimensions={0} | all-to-all | bytes 65536 | tf_op jit(solution)/shard_map/all_to_all | solution.py:370
  74.8 1.9 %collective-permute-start.5 = (bf16[3200,256]{1,0:T(8,128)(2,1)S(1)}, bf16[3200,256]{1,0:T(8,128)(2,1)S(1)}, u32[]{:S(2)}, u32[]{:S(2)}) collective-permute-start(bf16[3200,256]{1,0:T(8,128)(2,1)S(1)} %constant_dynamic-update-slice_fusion.6.near), channel_id=1, source_target_pairs={{0,1},{1,0},{2,3},{3,2},{4,5},{5,4},{6,7},{7,6},{8,9},{9,8},{10,11... | collective-permute-start | bytes 4915208 | tf_op jit(solution)/shard_map/ppermute | solution.py:36
  76.7 1.1 find.1
  77.8 8.9 %all-to-all-start.2 = ((f32[64,2,128]{2,1,0:T(2,128)}), f32[64,2,128]{2,1,0:T(2,128)S(1)}, u32[]{:S(2)}, u32[]{:S(2)}) async-start(f32[64,2,128]{2,1,0:T(2,128)} %find.1), calls=%async_computation.2 | async-start | bytes 131072 | tf_op jit(solution)/shard_map/all_to_all | solution.py:380
  86.8 3.2 %norm.1.normed = bf16[768,2048]{1,0:T(8,128)(2,1)S(1)} custom-call(bf16[3200,256]{1,0:T(8,128)(2,1)S(1)} %constant_dynamic-update-slice_fusion.6.near, bf16[3200,256]{1,0:T(8,128)(2,1)S(1)} %collective-permute-done.5.far), custom_call_target="tpu_custom_call" | custom-call | tf_op jit(solution)/shard_map/norm/pallas_call | solution.py:382
  90.0 1.7 %copy-done = bf16[768,2048]{1,0:T(8,128)(2,1)} copy-done((bf16[768,2048]{1,0:T(8,128)(2,1)}, bf16[768,2048]{1,0:T(8,128)(2,1)S(1)}, u32[]{:S(2)}) %copy-start) | copy-done | bytes 3145752
  91.7 7.8 %hidden.1 = f32[16,8,256]{2,1,0:T(8,128)} custom-call(bf16[768,2048]{1,0:T(8,128)(2,1)} %copy-done, bf16[16,768]{1,0:T(8,128)(2,1)S(1)} %copy-done.4, bf16[1024,1920]{1,0:T(8,128)(2,1)} %all-gather.2.cloned.1.call-done.weights), custom_call_target="tpu_custom_call" | custom-call | tf_op jit(solution)/shard_map/hidden/pallas_call | solution.py:400
  99.5 5.1 %all-to-all-start.1 = ((f32[16,8,256]{2,1,0:T(8,128)}), f32[16,8,256]{2,1,0:T(8,128)S(1)}, u32[]{:S(2)}, u32[]{:S(2)}) async-start(f32[16,8,256]{2,1,0:T(8,128)} %hidden.1), calls=%async_computation.1 | async-start | bytes 262144 | tf_op jit(solution)/shard_map/all_to_all | solution.py:416
  104.8 6.5 %all-to-all-done.1.parts = f32[16,8,256]{2,1,0:T(8,128)S(1)} async-done(((f32[16,8,256]{2,1,0:T(8,128)}), f32[16,8,256]{2,1,0:T(8,128)S(1)}, u32[]{:S(2)}, u32[]{:S(2)}) %all-to-all-start.1) | async-done | bytes 131104 | tf_op jit(solution)/shard_map/all_to_all | solution.py:416
  111.3 0.7 head.1
  112.0 9.2 %all_to_all.33.messages = bf16[8,96,128]{2,1,0:T(8,128)(2,1)S(1)} all-to-all(bf16[8,96,128]{2,1,0:T(8,128)(2,1)S(1)} %get-tuple-element.22), channel_id=1, replica_groups=mesh['section'=4,'dp'=16,'mp'=8] {'mp'}, dimensions={0} | all-to-all | bytes 393216 | tf_op jit(solution)/shard_map/all_to_all | solution.py:445
  121.3 1.6 %loss.1 = (bf16[2,96]{1,0:T(2,128)(2,1)}, f32[4,128]{1,0:T(4,128)S(1)}, bf16[64,4,384]{2,1,0:T(4,128)(2,1)}) custom-call(s32[4]{0:T(128)S(1)} %copy-done.5, bf16[8,96,128]{2,1,0:T(8,128)(2,1)S(1)} %all_to_all.33.messages, bf16[8,256]{1,0:T(8,128)(2,1)S(1)} %get-tuple-element.23.pooled), custom_call_target="tpu_custom_call" | custom-call | tf_op jit(solution)/shard_map/loss/pallas_call | solution.py:447
  122.9 11.7 %all-to-all-start.4 = ((bf16[64,4,384]{2,1,0:T(4,128)(2,1)}), bf16[64,4,384]{2,1,0:T(4,128)(2,1)S(1)}, u32[]{:S(2)}, u32[]{:S(2)}) async-start(bf16[64,4,384]{2,1,0:T(4,128)(2,1)} %get-tuple-element.26), calls=%async_computation.4 | async-start | bytes 393216 | tf_op jit(solution)/shard_map/all_to_all | solution.py:461
  134.6 0.6 slice_reduce_fusion
  135.2 12.0 %all-to-all-done.4 = bf16[64,4,384]{2,1,0:T(4,128)(2,1)S(1)} async-done(((bf16[64,4,384]{2,1,0:T(4,128)(2,1)}), bf16[64,4,384]{2,1,0:T(4,128)(2,1)S(1)}, u32[]{:S(2)}, u32[]{:S(2)}) %all-to-all-start.4) | async-done | bytes 196640 | tf_op jit(solution)/shard_map/all_to_all | solution.py:461
  147.3 0.8 grad.1
  (38 shorter events, 0.6 us)
Async XLA Ops:
  7.2 33.9 %copy-start.6 = (bf16[2,128,256]{2,1,0:T(8,128)(2,1)S(1)}, bf16[2,128,256]{2,1,0:T(8,128)(2,1)}, u32[]{:S(2)}) copy-start(bf16[2,128,256]{2,1,0:T(8,128)(2,1)} %param.13) | copy-start | bytes 393220
  7.2 33.9 %copy-start.7 = (bf16[4,32,256]{2,1,0:T(8,128)(2,1)S(1)}, bf16[4,32,256]{2,1,0:T(8,128)(2,1)}, u32[]{:S(2)}) copy-start(bf16[4,32,256]{2,1,0:T(8,128)(2,1)} %param.14) | copy-start | bytes 196612
  7.2 33.9 %copy-start.8 = (bf16[256]{0:T(256)(128)(2,1)S(1)}, bf16[256]{0:T(256)(128)(2,1)}, u32[]{:S(2)}) copy-start(bf16[256]{0:T(256)(128)(2,1)} %param.15) | copy-start | bytes 1540
  7.2 84.5 %all-gather.2.cloned.1.call-start = ((), (), s32[]{:S(2)}) async-start(), calls=%async_computation.5 | async-start | bytes 4423680 | tf_op jit(solution)/shard_map/all_gather | solution.py:57
  9.5 22.4 %collective-permute-start = (bf16[128,1024]{1,0:T(8,128)(2,1)}, bf16[128,1024]{1,0:T(8,128)(2,1)S(1)}, u32[]{:S(2)}, u32[]{:S(2)}) collective-permute-start(bf16[128,1024]{1,0:T(8,128)(2,1)} %get-tuple-element.15), channel_id=1, source_target_pairs={{0,320},{8,328},{16,336},{24,344},{32,352},{40,360},{48,368},{56,3... | collective-permute-start | bytes 786440 | tf_op jit(solution)/shard_map/ppermute | solution.py:51
  22.0 9.6 %collective-permute-start.1 = (bf16[400,256]{1,0:T(8,128)(2,1)S(1)}, bf16[400,256]{1,0:T(8,128)(2,1)S(1)}, u32[]{:S(2)}, u32[]{:S(2)}) collective-permute-start(bf16[400,256]{1,0:T(8,128)(2,1)S(1)} %pad_maximum_fusion), channel_id=1, source_target_pairs={{0,2},{1,3},{2,4},{3,5},{4,6},{5,7},{6,0},{7,1},{8,10},{9,11},{10,... | collective-permute-start | bytes 614408 | tf_op jit(solution)/shard_map/ppermute | solution.py:36
  33.6 12.6 %collective-permute-start.2 = (bf16[400,256]{1,0:T(8,128)(2,1)S(1)}, bf16[400,256]{1,0:T(8,128)(2,1)S(1)}, u32[]{:S(2)}, u32[]{:S(2)}) collective-permute-start(bf16[400,256]{1,0:T(8,128)(2,1)S(1)} %pad_maximum_fusion), channel_id=1, source_target_pairs={{0,6},{1,7},{2,0},{3,1},{4,2},{5,3},{6,4},{7,5},{8,14},{9,15},{10,... | collective-permute-start | bytes 614408 | tf_op jit(solution)/shard_map/ppermute | solution.py:36
  38.3 9.2 %collective-permute-start.3 = (bf16[400,256]{1,0:T(8,128)(2,1)S(1)}, bf16[400,256]{1,0:T(8,128)(2,1)S(1)}, u32[]{:S(2)}, u32[]{:S(2)}) collective-permute-start(bf16[400,256]{1,0:T(8,128)(2,1)S(1)} %pad_maximum_fusion), channel_id=1, source_target_pairs={{0,4},{1,5},{2,6},{3,7},{4,0},{5,1},{6,2},{7,3},{8,12},{9,13},{10,... | collective-permute-start | bytes 614408 | tf_op jit(solution)/shard_map/ppermute | solution.py:36
  41.2 35.6 %copy-start.3 = (bf16[2048,96]{0,1:T(8,128)(2,1)S(1)}, bf16[2048,96]{0,1:T(8,128)(2,1)}, u32[]{:S(2)}) copy-start(bf16[2048,96]{0,1:T(8,128)(2,1)} %param.21) | copy-start | bytes 1179652
  47.5 27.2 %collective-permute-start.4 = (bf16[1600,256]{1,0:T(8,128)(2,1)S(1)}, bf16[1600,256]{1,0:T(8,128)(2,1)S(1)}, u32[]{:S(2)}, u32[]{:S(2)}) collective-permute-start(bf16[1600,256]{1,0:T(8,128)(2,1)S(1)} %get-tuple-element.27), channel_id=1, source_target_pairs={{0,128},{128,0},{256,384},{384,256},{1,129},{129,1},{257,385},{385... | collective-permute-start | bytes 2457608 | tf_op jit(solution)/shard_map/ppermute | solution.py:40
  74.8 12.0 %collective-permute-start.5 = (bf16[3200,256]{1,0:T(8,128)(2,1)S(1)}, bf16[3200,256]{1,0:T(8,128)(2,1)S(1)}, u32[]{:S(2)}, u32[]{:S(2)}) collective-permute-start(bf16[3200,256]{1,0:T(8,128)(2,1)S(1)} %constant_dynamic-update-slice_fusion.6.near), channel_id=1, source_target_pairs={{0,1},{1,0},{2,3},{3,2},{4,5},{5,4},{6,7},{7,6},{8,9},{9,8},{10,11... | collective-permute-start | bytes 4915208 | tf_op jit(solution)/shard_map/ppermute | solution.py:36
  77.8 21.7 %all-to-all-start.2 = ((f32[64,2,128]{2,1,0:T(2,128)}), f32[64,2,128]{2,1,0:T(2,128)S(1)}, u32[]{:S(2)}, u32[]{:S(2)}) async-start(f32[64,2,128]{2,1,0:T(2,128)} %find.1), calls=%async_computation.2 | async-start | bytes 131072 | tf_op jit(solution)/shard_map/all_to_all | solution.py:380
  86.8 4.9 %copy-start.4 = (bf16[16,768]{1,0:T(8,128)(2,1)S(1)}, bf16[16,768]{1,0:T(8,128)(2,1)}, u32[]{:S(2)}) copy-start(bf16[16,768]{1,0:T(8,128)(2,1)} %constant.15.clone.pool) | copy-start | bytes 73732
  90.0 1.7 %copy-start = (bf16[768,2048]{1,0:T(8,128)(2,1)}, bf16[768,2048]{1,0:T(8,128)(2,1)S(1)}, u32[]{:S(2)}) copy-start(bf16[768,2048]{1,0:T(8,128)(2,1)S(1)} %norm.1.normed) | copy-start | bytes 9437188
  91.6 19.7 %copy-start.1 = (bf16[256,768]{1,0:T(8,128)(2,1)S(1)}, bf16[256,768]{1,0:T(8,128)(2,1)}, u32[]{:S(2)}) copy-start(bf16[256,768]{1,0:T(8,128)(2,1)} %old_head.1) | copy-start | bytes 1179652
  91.7 19.7 %copy-start.2 = (bf16[256,768]{1,0:T(8,128)(2,1)S(1)}, bf16[256,768]{1,0:T(8,128)(2,1)}, u32[]{:S(2)}) copy-start(bf16[256,768]{1,0:T(8,128)(2,1)} %new_head.1) | copy-start | bytes 1179652
  99.5 21.8 %copy-start.5 = (s32[4]{0:T(128)S(1)}, s32[4]{0:T(128)}, u32[]{:S(2)}) copy-start(s32[4]{0:T(128)} %slot.1) | copy-start | bytes 52
  99.5 11.8 %all-to-all-start.1 = ((f32[16,8,256]{2,1,0:T(8,128)}), f32[16,8,256]{2,1,0:T(8,128)S(1)}, u32[]{:S(2)}, u32[]{:S(2)}) async-start(f32[16,8,256]{2,1,0:T(8,128)} %hidden.1), calls=%async_computation.1 | async-start | bytes 262144 | tf_op jit(solution)/shard_map/all_to_all | solution.py:416
  122.9 24.3 %all-to-all-start.4 = ((bf16[64,4,384]{2,1,0:T(4,128)(2,1)}), bf16[64,4,384]{2,1,0:T(4,128)(2,1)S(1)}, u32[]{:S(2)}, u32[]{:S(2)}) async-start(bf16[64,4,384]{2,1,0:T(4,128)(2,1)} %get-tuple-element.26), calls=%async_computation.4 | async-start | bytes 393216 | tf_op jit(solution)/shard_map/all_to_all | solution.py:461
Sparse Core Ops, SparseCore 0:
  33.8 53.9 all-gather.1

commit v5 on v3

--- a/solution.py
+++ b/solution.py
@@ -64,13 +64,24 @@
     return mine, mp_move(mine, 0, 1), wanted
 
 
-def cut_kernel(gate_in, up_in, down_in, own, other, gate, up, down, sems):
+def cut_kernel(gate_in, up_in, down_in, passages, queries, gain, own, other, tokens, gate, up, down, sems):
+    split = passages.shape[0]
+    rows = split + queries.shape[0]
     fetches = [
         pltpu.make_async_copy(source, target, sems.at[k])
-        for k, (source, target) in enumerate(((gate_in, gate), (up_in, up), (down_in, down)))
+        for k, (source, target) in enumerate(
+            (
+                (gate_in, gate),
+                (up_in, up),
+                (down_in, down),
+                (passages, tokens.at[pl.ds(0, split), :]),
+                (queries, tokens.at[pl.ds(split, rows - split), :]),
+            )
+        )
     ]
     for fetch in fetches:
         fetch.start()
+    tokens[rows:, :] = jnp.broadcast_to(gain[...], (tokens.shape[0] - rows, tokens.shape[1]))
     units = gate.shape[1] // 2
     cut = units // 128 * 128
     gap = own.shape[1] - 3 * units
@@ -335,22 +346,26 @@
     units = w_gate.shape[1] // 2
     cut = units // 128 * 128
     wide = -(-3 * units // 128) * 128
-    own, other = pl.pallas_call(
+    rows = p_count * length + q_count * q_length
+    own, other, tokens = pl.pallas_call(
         cut_kernel,
-        out_shape=[jax.ShapeDtypeStruct((w_gate.shape[0], wide), bf16)] * 2,
-        in_specs=[in_hbm()] * 3,
-        out_specs=[whole()] * 2,
-        scratch_shapes=[pltpu.VMEM(w.shape, bf16) for w in (w_gate, w_up, w_down)] + [pltpu.SemaphoreType.DMA((3,))],
+        out_shape=[jax.ShapeDtypeStruct((w_gate.shape[0], wide), bf16)] * 2
+        + [jax.ShapeDtypeStruct((rows + 16, width), bf16)],
+        in_specs=[in_hbm()] * 5 + [whole()],
+        out_specs=[whole()] * 3,
+        scratch_shapes=[pltpu.VMEM(w.shape, bf16) for w in (w_gate, w_up, w_down)] + [pltpu.SemaphoreType.DMA((5,))],
         compiler_params=params(56),
         name="cut",
-    )(w_gate, w_up, w_down)
+    )(
+        w_gate,
+        w_up,
+        w_down,
+        passage_tokens.reshape(-1, width),
+        query_tokens.reshape(-1, width),
+        norm_gain[None, :],
+    )
     other = half_move(other)
 
-    rows = p_count * length + q_count * q_length
-    gain_rows = jnp.broadcast_to(norm_gain[None, :], (16, width))
-    tokens = jnp.concatenate(
-        [passage_tokens.reshape(-1, width), query_tokens.reshape(-1, width), gain_rows], axis=0
-    )
     request_count = q_count * k_count
     owner = neg_owner.reshape(1, request_count)
     requests = pl.pallas_call(

time: 153 us -> 157 us (1.026)
  blocking collectives: 31.5 us -> 9.23 us
  starting transfers between devices: 52.9 us -> 67.3 us
  waiting for transfers between devices: 28.7 us -> 36.5 us
    all_to_all x1 -> x0, blocking collectives: 22.2 us -> none  [shards(): wanted = lax.all_to_all(requests, ('section', 'dp'), 0, 0, tiled=True)]
    all_to_all x0 -> x1, starting transfers between devices: none -> 11.4 us  [shards(): wanted = lax.all_to_all(requests, ('section', 'dp'), 0, 0, tiled=True)]
    all_to_all x0 -> x1, waiting for transfers between devices: none -> 10.9 us  [shards(): wanted = lax.all_to_all(requests, ('section', 'dp'), 0, 0, tiled=True)]
    all_gather x1, waiting for transfers between devices: 3.12 us -> 0.01 us  [along_y(): lax.all_gather(block, 'dp', axis=0, axis_index_groups=groups, tiled=True)]
  transfers between devices with their start and end apart: 10 -> 11, of which waited for: 6 -> 6; matrix products, arithmetic and copies ran while one was open for 3% -> 3% of each run, Pallas kernels for 8% -> 8%
where the time goes in v5:
time: 157 us; the launch traced here: 156 us
  starting transfers between devices  67.3 us (43%)
  waiting for transfers between devices  36.5 us (23%)
  Pallas kernels  18.9 us (12%)
  between operations  14.3 us (9%)
  blocking collectives  9.23 us (6%)
  local copies, waits for them, and re-layouts  6.31 us (4%)
  other arithmetic  3.69 us (2%)
    ppermute x4, starting transfers between devices, mp_move(): return lax.ppermute(block, 'mp', perm)  13.6 us
    all_to_all x1, waiting for transfers between devices, shards(): arrived = lax.all_to_all(message, ('section', 'dp'), 0, 0, tiled=True)  12 us
    all_to_all x1, starting transfers between devices, shards(): arrived = lax.all_to_all(message, ('section', 'dp'), 0, 0, tiled=True)  11.7 us
    all_to_all x1, starting transfers between devices, shards(): wanted = lax.all_to_all(requests, ('section', 'dp'), 0, 0, tiled=True)  11.4 us
    ppermute x1, starting transfers between devices, half_move(): return lax.ppermute(block, ('section', 'dp'), perm)  11.1 us
    all_to_all x1, waiting for transfers between devices, shards(): wanted = lax.all_to_all(requests, ('section', 'dp'), 0, 0, tiled=True)  10.9 us
    all_to_all x1, blocking collectives, shards(): messages = lax.all_to_all(message, 'mp', 0, 0, tiled=True)  9.23 us
    all_to_all x1, starting transfers between devices, shards(): fetched = lax.all_to_all(found, ('section', 'dp'), 0, 0, tiled=True)  9.23 us
  transfers between devices with their start and end apart: 11, of which 6 were waited for; matrix products, arithmetic and copies ran while one was open for 3% of the time, Pallas kernels for 8%

profile of v5, /device:TPU:8, one launch (start us, length us, event | category | flops | bytes accessed | tf_op | source)
XLA Modules:
  0.0 156.2 jit_solution(12706219510328770071)
XLA Ops:
  7.2 1.2 broadcast_in_dim.6.gain
  8.4 2.9 %cut.1 = (bf16[128,1024]{1,0:T(8,128)(2,1)}, bf16[128,1024]{1,0:T(8,128)(2,1)}, bf16[400,256]{1,0:T(8,128)(2,1)}) custom-call(bf16[128,640]{1,0:T(8,128)(2,1)} %gate_in.1, bf16[128,640]{1,0:T(8,128)(2,1)} %up_in.1, bf16[640,128]{1,0:T(8,128)(2,1)} %down_in.1, bf16[256,256]{1,0:T(8,128)(2,1)} %bitcast.10, bf16[128,256]{1,0:T(8,128)(2,1)} %bitcast.11, ...), custom_call_target="tpu_custom_call" | custom-call | tf_op jit(solution)/shard_map/cut/pallas_call | solution.py:350
  11.4 11.1 %collective-permute-start = (bf16[128,1024]{1,0:T(8,128)(2,1)}, bf16[128,1024]{1,0:T(8,128)(2,1)S(1)}, u32[]{:S(2)}, u32[]{:S(2)}) collective-permute-start(bf16[128,1024]{1,0:T(8,128)(2,1)} %get-tuple-element.18), channel_id=1, source_target_pairs={{0,320},{8,328},{16,336},{24,344},{32,352},{40,360},{48,368},{56,3... | collective-permute-start | bytes 786440 | tf_op jit(solution)/shard_map/ppermute | solution.py:51
  22.4 3.4 %collective-permute-start.1 = (bf16[400,256]{1,0:T(8,128)(2,1)}, bf16[400,256]{1,0:T(8,128)(2,1)S(1)}, u32[]{:S(2)}, u32[]{:S(2)}) collective-permute-start(bf16[400,256]{1,0:T(8,128)(2,1)} %get-tuple-element.17), channel_id=1, source_target_pairs={{0,2},{1,3},{2,4},{3,5},{4,6},{5,7},{6,0},{7,1},{8,10},{9,11},{10,... | collective-permute-start | bytes 614408 | tf_op jit(solution)/shard_map/ppermute | solution.py:36
  25.8 3.7 %collective-permute-start.2 = (bf16[400,256]{1,0:T(8,128)(2,1)}, bf16[400,256]{1,0:T(8,128)(2,1)S(1)}, u32[]{:S(2)}, u32[]{:S(2)}) collective-permute-start(bf16[400,256]{1,0:T(8,128)(2,1)} %get-tuple-element.17), channel_id=1, source_target_pairs={{0,6},{1,7},{2,0},{3,1},{4,2},{5,3},{6,4},{7,5},{8,14},{9,15},{10,... | collective-permute-start | bytes 614408 | tf_op jit(solution)/shard_map/ppermute | solution.py:36
  29.5 0.8 reshape.25.owner
  30.3 0.8 reshape.26.row
  31.0 0.8 ask.1
  32.3 1.9 %collective-permute-done.2 = bf16[400,256]{1,0:T(8,128)(2,1)S(1)} collective-permute-done((bf16[400,256]{1,0:T(8,128)(2,1)}, bf16[400,256]{1,0:T(8,128)(2,1)S(1)}, u32[]{:S(2)}, u32[]{:S(2)}) %collective-permute-start.2) | collective-permute-done | bytes 204832 | tf_op jit(solution)/shard_map/ppermute | solution.py:36
  34.2 1.8 %pad_add_fusion = bf16[128,1920]{1,0:T(8,128)(2,1)} fusion(bf16[128,1024]{1,0:T(8,128)(2,1)S(1)} %collective-permute-done, bf16[128,1024]{1,0:T(8,128)(2,1)} %get-tuple-element.23), kind=kLoop, calls=%fused_computation.1 | loop fusion | flops 983040 | bytes 1015808 | tf_op jit(solution)/shard_map/add | solution.py:383
  36.0 4.6 %collective-permute-start.3 = (bf16[400,256]{1,0:T(8,128)(2,1)}, bf16[400,256]{1,0:T(8,128)(2,1)S(1)}, u32[]{:S(2)}, u32[]{:S(2)}) collective-permute-start(bf16[400,256]{1,0:T(8,128)(2,1)} %get-tuple-element.17), channel_id=1, source_target_pairs={{0,4},{1,5},{2,6},{3,7},{4,0},{5,1},{6,2},{7,3},{8,12},{9,13},{10,... | collective-permute-start | bytes 614408 | tf_op jit(solution)/shard_map/ppermute | solution.py:36
  40.6 4.7 %collective-permute-done.3 = bf16[400,256]{1,0:T(8,128)(2,1)S(1)} collective-permute-done((bf16[400,256]{1,0:T(8,128)(2,1)}, bf16[400,256]{1,0:T(8,128)(2,1)S(1)}, u32[]{:S(2)}, u32[]{:S(2)}) %collective-permute-start.3) | collective-permute-done | bytes 204832 | tf_op jit(solution)/shard_map/ppermute | solution.py:36
  45.4 0.9 pad_maximum_fusion
  46.3 5.0 %collective-permute-start.4 = (bf16[1600,256]{1,0:T(8,128)(2,1)}, bf16[1600,256]{1,0:T(8,128)(2,1)S(1)}, u32[]{:S(2)}, u32[]{:S(2)}) collective-permute-start(bf16[1600,256]{1,0:T(8,128)(2,1)} %pad_maximum_fusion), channel_id=1, source_target_pairs={{0,128},{128,0},{256,384},{384,256},{1,129},{129,1},{257,385},{385... | collective-permute-start | bytes 2457608 | tf_op jit(solution)/shard_map/ppermute | solution.py:40
  51.3 11.4 %all-to-all-start = ((s32[64,1,128]{2,1,0:T(1,128)}), s32[64,1,128]{2,1,0:T(1,128)S(1)}, u32[]{:S(2)}, u32[]{:S(2)}) async-start(s32[64,1,128]{2,1,0:T(1,128)} %bitcast.3), calls=%async_computation | async-start | bytes 65536 | tf_op jit(solution)/shard_map/all_to_all | solution.py:385
  62.8 10.9 %all-to-all-done = s32[64,1,128]{2,1,0:T(1,128)S(1)} async-done(((s32[64,1,128]{2,1,0:T(1,128)}), s32[64,1,128]{2,1,0:T(1,128)S(1)}, u32[]{:S(2)}, u32[]{:S(2)}) %all-to-all-start) | async-done | bytes 32800 | tf_op jit(solution)/shard_map/all_to_all | solution.py:385
  73.7 1.9 %collective-permute-start.5 = (bf16[3200,256]{1,0:T(8,128)(2,1)S(1)}, bf16[3200,256]{1,0:T(8,128)(2,1)S(1)}, u32[]{:S(2)}, u32[]{:S(2)}) collective-permute-start(bf16[3200,256]{1,0:T(8,128)(2,1)S(1)} %constant_dynamic-update-slice_fusion.near), channel_id=1, source_target_pairs={{0,1},{1,0},{2,3},{3,2},{4,5},{5,4},{6,7},{7,6},{8,9},{9,8},{10,11... | collective-permute-start | bytes 4915208 | tf_op jit(solution)/shard_map/ppermute | solution.py:36
  75.7 0.9 convert_reduce_fusion.1
  76.5 1.0 copy-done.3
  77.5 1.1 find.1
  78.6 9.2 %all-to-all-start.2 = ((f32[64,2,128]{2,1,0:T(2,128)}), f32[64,2,128]{2,1,0:T(2,128)S(1)}, u32[]{:S(2)}, u32[]{:S(2)}) async-start(f32[64,2,128]{2,1,0:T(2,128)} %find.1), calls=%async_computation.2 | async-start | bytes 131072 | tf_op jit(solution)/shard_map/all_to_all | solution.py:395
  87.9 3.2 %norm.1.normed = bf16[768,2048]{1,0:T(8,128)(2,1)S(1)} custom-call(bf16[3200,256]{1,0:T(8,128)(2,1)S(1)} %constant_dynamic-update-slice_fusion.near, bf16[3200,256]{1,0:T(8,128)(2,1)S(1)} %collective-permute-done.5.far), custom_call_target="tpu_custom_call" | custom-call | tf_op jit(solution)/shard_map/norm/pallas_call | solution.py:397
  91.1 1.7 %copy-done = bf16[768,2048]{1,0:T(8,128)(2,1)} copy-done((bf16[768,2048]{1,0:T(8,128)(2,1)}, bf16[768,2048]{1,0:T(8,128)(2,1)S(1)}, u32[]{:S(2)}) %copy-start) | copy-done | bytes 3145752
  92.8 7.8 %hidden.1 = f32[16,8,256]{2,1,0:T(8,128)} custom-call(bf16[768,2048]{1,0:T(8,128)(2,1)} %copy-done, bf16[16,768]{1,0:T(8,128)(2,1)S(1)} %copy-done.4, bf16[1024,1920]{1,0:T(8,128)(2,1)} %all-gather.2.cloned.1.call-done.weights), custom_call_target="tpu_custom_call" | custom-call | tf_op jit(solution)/shard_map/hidden/pallas_call | solution.py:415
  100.6 5.3 %all-to-all-start.1 = ((f32[16,8,256]{2,1,0:T(8,128)}), f32[16,8,256]{2,1,0:T(8,128)S(1)}, u32[]{:S(2)}, u32[]{:S(2)}) async-start(f32[16,8,256]{2,1,0:T(8,128)} %hidden.1), calls=%async_computation.1 | async-start | bytes 262144 | tf_op jit(solution)/shard_map/all_to_all | solution.py:431
  106.2 6.5 %all-to-all-done.1.parts = f32[16,8,256]{2,1,0:T(8,128)S(1)} async-done(((f32[16,8,256]{2,1,0:T(8,128)}), f32[16,8,256]{2,1,0:T(8,128)S(1)}, u32[]{:S(2)}, u32[]{:S(2)}) %all-to-all-start.1) | async-done | bytes 131104 | tf_op jit(solution)/shard_map/all_to_all | solution.py:431
  112.7 0.7 head.1
  113.4 9.2 %all_to_all.32.messages = bf16[8,96,128]{2,1,0:T(8,128)(2,1)S(1)} all-to-all(bf16[8,96,128]{2,1,0:T(8,128)(2,1)S(1)} %get-tuple-element.26), channel_id=1, replica_groups=mesh['section'=4,'dp'=16,'mp'=8] {'mp'}, dimensions={0} | all-to-all | bytes 393216 | tf_op jit(solution)/shard_map/all_to_all | solution.py:460
  122.6 1.6 %loss.1 = (bf16[2,96]{1,0:T(2,128)(2,1)}, f32[4,128]{1,0:T(4,128)S(1)}, bf16[64,4,384]{2,1,0:T(4,128)(2,1)}) custom-call(s32[4]{0:T(128)S(1)} %copy-done.5, bf16[8,96,128]{2,1,0:T(8,128)(2,1)S(1)} %all_to_all.32.messages, bf16[8,256]{1,0:T(8,128)(2,1)S(1)} %get-tuple-element.27.pooled), custom_call_target="tpu_custom_call" | custom-call | tf_op jit(solution)/shard_map/loss/pallas_call | solution.py:462
  124.2 11.7 %all-to-all-start.4 = ((bf16[64,4,384]{2,1,0:T(4,128)(2,1)}), bf16[64,4,384]{2,1,0:T(4,128)(2,1)S(1)}, u32[]{:S(2)}, u32[]{:S(2)}) async-start(bf16[64,4,384]{2,1,0:T(4,128)(2,1)} %get-tuple-element.30), calls=%async_computation.4 | async-start | bytes 393216 | tf_op jit(solution)/shard_map/all_to_all | solution.py:476
  136.6 12.0 %all-to-all-done.4 = bf16[64,4,384]{2,1,0:T(4,128)(2,1)S(1)} async-done(((bf16[64,4,384]{2,1,0:T(4,128)(2,1)}), bf16[64,4,384]{2,1,0:T(4,128)(2,1)S(1)}, u32[]{:S(2)}, u32[]{:S(2)}) %all-to-all-start.4) | async-done | bytes 196640 | tf_op jit(solution)/shard_map/all_to_all | solution.py:476
  148.6 0.8 grad.1
  (35 shorter events, 1.5 us)
Async XLA Ops:
  7.2 85.6 %all-gather.2.cloned.1.call-start = ((), (), s32[]{:S(2)}) async-start(), calls=%async_computation.5 | async-start | bytes 4423680 | tf_op jit(solution)/shard_map/all_gather | solution.py:57
  11.3 34.0 %copy-start.6 = (bf16[400,256]{1,0:T(8,128)(2,1)S(1)}, bf16[400,256]{1,0:T(8,128)(2,1)}, u32[]{:S(2)}) copy-start(bf16[400,256]{1,0:T(8,128)(2,1)} %get-tuple-element.17) | copy-start | bytes 614404
  11.4 22.8 %collective-permute-start = (bf16[128,1024]{1,0:T(8,128)(2,1)}, bf16[128,1024]{1,0:T(8,128)(2,1)S(1)}, u32[]{:S(2)}, u32[]{:S(2)}) collective-permute-start(bf16[128,1024]{1,0:T(8,128)(2,1)} %get-tuple-element.18), channel_id=1, source_target_pairs={{0,320},{8,328},{16,336},{24,344},{32,352},{40,360},{48,368},{56,3... | collective-permute-start | bytes 786440 | tf_op jit(solution)/shard_map/ppermute | solution.py:51
  22.4 9.9 %collective-permute-start.1 = (bf16[400,256]{1,0:T(8,128)(2,1)}, bf16[400,256]{1,0:T(8,128)(2,1)S(1)}, u32[]{:S(2)}, u32[]{:S(2)}) collective-permute-start(bf16[400,256]{1,0:T(8,128)(2,1)} %get-tuple-element.17), channel_id=1, source_target_pairs={{0,2},{1,3},{2,4},{3,5},{4,6},{5,7},{6,0},{7,1},{8,10},{9,11},{10,... | collective-permute-start | bytes 614408 | tf_op jit(solution)/shard_map/ppermute | solution.py:36
  25.8 8.4 %collective-permute-start.2 = (bf16[400,256]{1,0:T(8,128)(2,1)}, bf16[400,256]{1,0:T(8,128)(2,1)S(1)}, u32[]{:S(2)}, u32[]{:S(2)}) collective-permute-start(bf16[400,256]{1,0:T(8,128)(2,1)} %get-tuple-element.17), channel_id=1, source_target_pairs={{0,6},{1,7},{2,0},{3,1},{4,2},{5,3},{6,4},{7,5},{8,14},{9,15},{10,... | collective-permute-start | bytes 614408 | tf_op jit(solution)/shard_map/ppermute | solution.py:36
  36.0 9.4 %collective-permute-start.3 = (bf16[400,256]{1,0:T(8,128)(2,1)}, bf16[400,256]{1,0:T(8,128)(2,1)S(1)}, u32[]{:S(2)}, u32[]{:S(2)}) collective-permute-start(bf16[400,256]{1,0:T(8,128)(2,1)} %get-tuple-element.17), channel_id=1, source_target_pairs={{0,4},{1,5},{2,6},{3,7},{4,0},{5,1},{6,2},{7,3},{8,12},{9,13},{10,... | collective-permute-start | bytes 614408 | tf_op jit(solution)/shard_map/ppermute | solution.py:36
  46.3 27.4 %collective-permute-start.4 = (bf16[1600,256]{1,0:T(8,128)(2,1)}, bf16[1600,256]{1,0:T(8,128)(2,1)S(1)}, u32[]{:S(2)}, u32[]{:S(2)}) collective-permute-start(bf16[1600,256]{1,0:T(8,128)(2,1)} %pad_maximum_fusion), channel_id=1, source_target_pairs={{0,128},{128,0},{256,384},{384,256},{1,129},{129,1},{257,385},{385... | collective-permute-start | bytes 2457608 | tf_op jit(solution)/shard_map/ppermute | solution.py:40
  51.3 22.4 %all-to-all-start = ((s32[64,1,128]{2,1,0:T(1,128)}), s32[64,1,128]{2,1,0:T(1,128)S(1)}, u32[]{:S(2)}, u32[]{:S(2)}) async-start(s32[64,1,128]{2,1,0:T(1,128)} %bitcast.3), calls=%async_computation | async-start | bytes 65536 | tf_op jit(solution)/shard_map/all_to_all | solution.py:385
  62.7 25.2 %copy-start.7 = (bf16[2,128,256]{2,1,0:T(8,128)(2,1)S(1)}, bf16[2,128,256]{2,1,0:T(8,128)(2,1)}, u32[]{:S(2)}) copy-start(bf16[2,128,256]{2,1,0:T(8,128)(2,1)} %param.13) | copy-start | bytes 393220
  73.7 14.2 %collective-permute-start.5 = (bf16[3200,256]{1,0:T(8,128)(2,1)S(1)}, bf16[3200,256]{1,0:T(8,128)(2,1)S(1)}, u32[]{:S(2)}, u32[]{:S(2)}) collective-permute-start(bf16[3200,256]{1,0:T(8,128)(2,1)S(1)} %constant_dynamic-update-slice_fusion.near), channel_id=1, source_target_pairs={{0,1},{1,0},{2,3},{3,2},{4,5},{5,4},{6,7},{7,6},{8,9},{9,8},{10,11... | collective-permute-start | bytes 4915208 | tf_op jit(solution)/shard_map/ppermute | solution.py:36
  76.5 1.0 copy-start.3
  78.6 22.0 %all-to-all-start.2 = ((f32[64,2,128]{2,1,0:T(2,128)}), f32[64,2,128]{2,1,0:T(2,128)S(1)}, u32[]{:S(2)}, u32[]{:S(2)}) async-start(f32[64,2,128]{2,1,0:T(2,128)} %find.1), calls=%async_computation.2 | async-start | bytes 131072 | tf_op jit(solution)/shard_map/all_to_all | solution.py:395
  87.9 4.9 %copy-start.4 = (bf16[16,768]{1,0:T(8,128)(2,1)S(1)}, bf16[16,768]{1,0:T(8,128)(2,1)}, u32[]{:S(2)}) copy-start(bf16[16,768]{1,0:T(8,128)(2,1)} %constant.14.clone.pool) | copy-start | bytes 73732
  91.1 1.7 %copy-start = (bf16[768,2048]{1,0:T(8,128)(2,1)}, bf16[768,2048]{1,0:T(8,128)(2,1)S(1)}, u32[]{:S(2)}) copy-start(bf16[768,2048]{1,0:T(8,128)(2,1)S(1)} %norm.1.normed) | copy-start | bytes 9437188
  92.8 19.9 %copy-start.1 = (bf16[256,768]{1,0:T(8,128)(2,1)S(1)}, bf16[256,768]{1,0:T(8,128)(2,1)}, u32[]{:S(2)}) copy-start(bf16[256,768]{1,0:T(8,128)(2,1)} %old_head.1) | copy-start | bytes 1179652
  92.8 19.9 %copy-start.2 = (bf16[256,768]{1,0:T(8,128)(2,1)S(1)}, bf16[256,768]{1,0:T(8,128)(2,1)}, u32[]{:S(2)}) copy-start(bf16[256,768]{1,0:T(8,128)(2,1)} %new_head.1) | copy-start | bytes 1179652
  100.6 22.0 %copy-start.5 = (s32[4]{0:T(128)S(1)}, s32[4]{0:T(128)}, u32[]{:S(2)}) copy-start(s32[4]{0:T(128)} %slot.1) | copy-start | bytes 52
  100.6 12.0 %all-to-all-start.1 = ((f32[16,8,256]{2,1,0:T(8,128)}), f32[16,8,256]{2,1,0:T(8,128)S(1)}, u32[]{:S(2)}, u32[]{:S(2)}) async-start(f32[16,8,256]{2,1,0:T(8,128)} %hidden.1), calls=%async_computation.1 | async-start | bytes 262144 | tf_op jit(solution)/shard_map/all_to_all | solution.py:431
  124.2 24.3 %all-to-all-start.4 = ((bf16[64,4,384]{2,1,0:T(4,128)(2,1)}), bf16[64,4,384]{2,1,0:T(4,128)(2,1)S(1)}, u32[]{:S(2)}, u32[]{:S(2)}) async-start(bf16[64,4,384]{2,1,0:T(4,128)(2,1)} %get-tuple-element.30), calls=%async_computation.4 | async-start | bytes 393216 | tf_op jit(solution)/shard_map/all_to_all | solution.py:476
Sparse Core Ops, SparseCore 0:
  36.1 53.7 all-gather.1

commit v6 on v4

--- a/solution.py
+++ b/solution.py
@@ -58,7 +58,7 @@
 
 
 def spread(block, low, high, wanted):
-    mine = jnp.concatenate([block, low, high, mp_move(block, 2, 0)], axis=0)
+    mine = jnp.concatenate([block, low, high, mp_move(low, 1, 0)], axis=0)
     mate, wanted = lax.optimization_barrier((mate_move(mine), wanted))
     mine = jnp.concatenate([mine, mate], axis=0)
     return mine, mp_move(mine, 0, 1), wanted
@@ -256,36 +256,41 @@
     own = held[:, pl.ds(pl.multiple_of(lax.axis_index("mp") * 128, 128), 128)]
     fresh_out[...] = own[:p_count, : fresh_out.shape[1]].astype(jnp.bfloat16)
     k_count = (rows.shape[1] - n * 8) // q_count
-    loss_rows, grad_rows = [], []
+    def each(parts):
+        return jnp.concatenate([jnp.broadcast_to(v, (k_count, v.shape[1])) for v in parts], axis=0)
+
+    def groups(values):
+        return [
+            jnp.sum(values[q * k_count : (q + 1) * k_count], axis=0, keepdims=True) for q in range(q_count)
+        ]
+
+    own_queries = [emb[p_count + q : p_count + q + 1] for q in range(q_count)]
+    positives = []
     for q in range(q_count):
-        query = emb[p_count + q : p_count + q + 1]
         positive = fresh[0:1]
         for k in range(1, p_count):
             positive = jnp.where(slot[q] == k, fresh[k : k + 1], positive)
-        tiles = [rows[a, n * 8 + q * k_count : n * 8 + (q + 1) * k_count] for a in range(n)]
-        inner = jnp.zeros((k_count, 128), jnp.float32)
-        square = inner
-        for a in range(n):
-            inner = inner + tiles[a] * query[:, a * 128 : (a + 1) * 128]
-            square = square + tiles[a] * tiles[a]
-        inner = jnp.sum(inner, axis=1, keepdims=True)
-        square = jnp.sum(square, axis=1, keepdims=True)
-        query_norm = jnp.sqrt(jnp.sum(query * query, axis=1, keepdims=True) + 1e-06)
-        below = jnp.sqrt(square + 1e-06) * query_norm * TAU
-        scores = inner / below
-        below_p = jnp.sqrt(jnp.sum(positive * positive, axis=1, keepdims=True) + 1e-06) * query_norm * TAU
-        score_p = jnp.sum(positive * query, axis=1, keepdims=True) / below_p
-        exps, exp_p = jnp.exp(scores), jnp.exp(score_p)
-        total = jnp.sum(exps, axis=0, keepdims=True) + exp_p
-        loss_rows.append(jnp.log(total) - score_p)
-        weights = exps / total / queries
-        weight_p = (exp_p / total - 1.0) / queries
-        radial = (jnp.sum(weights * scores, axis=0, keepdims=True) + weight_p * score_p) / (query_norm * query_norm)
-        share = weights / below
-        direct = jnp.concatenate([jnp.sum(share * tile, axis=0, keepdims=True) for tile in tiles], axis=1)
-        grad_rows.append(direct + (weight_p / below_p) * positive - radial * query)
-    losses = jnp.concatenate(loss_rows, axis=0)
-    loss_out[...] = jnp.broadcast_to(losses, loss_out.shape)
+        positives.append(positive)
+    query, positive = each(own_queries), each(positives)
+    cands = jnp.concatenate([rows[a, n * 8 :] for a in range(n)], axis=1)
+    query_norm = jnp.sqrt(jnp.sum(query * query, axis=1, keepdims=True) + 1e-06)
+    below = jnp.sqrt(jnp.sum(cands * cands, axis=1, keepdims=True) + 1e-06) * query_norm * TAU
+    scores = jnp.sum(cands * query, axis=1, keepdims=True) / below
+    below_p = jnp.sqrt(jnp.sum(positive * positive, axis=1, keepdims=True) + 1e-06) * query_norm * TAU
+    score_p = jnp.sum(positive * query, axis=1, keepdims=True) / below_p
+    exps, exp_p = jnp.exp(scores), jnp.exp(score_p)
+    total = each(groups(exps)) + exp_p
+    losses = jnp.log(total) - score_p
+    weights = exps / total / queries
+    weight_p = (exp_p / total - 1.0) / queries
+    radial = (each(groups(weights * scores)) + weight_p * score_p) / (query_norm * query_norm)
+    direct = groups((weights / below) * cands)
+    scale_p = weight_p / below_p
+    grad_rows = []
+    for q in range(q_count):
+        at = slice(q * k_count, q * k_count + 1)
+        grad_rows.append(direct[q] + scale_p[at] * positives[q] - radial[at] * own_queries[q])
+        loss_out[q : q + 1, :] = jnp.broadcast_to(losses[at], (1, loss_out.shape[1]))
     grads = jnp.concatenate(grad_rows, axis=0).astype(jnp.bfloat16)
     width = pooled.shape[1]
     features = pooled[...].astype(jnp.float32)[p_count : p_count + q_count].astype(jnp.bfloat16)

time: 156 us -> 155 us (level)
    all_to_all x1, starting transfers between devices: 5.12 us -> 3.52 us  [shards(): lax.all_to_all(parts, ('section', 'mp'), split_axis=0, concat_axis=0, axi...]
where the time goes in v6:
time: 155 us; the launch traced here: 154 us
  starting transfers between devices  52.9 us (34%)
  blocking collectives  31.5 us (20%)
  waiting for transfers between devices  30.1 us (19%)
  Pallas kernels  17.5 us (11%)
  between operations  14.3 us (9%)
  local copies, waits for them, and re-layouts  4.83 us (3%)
  other arithmetic  2.82 us (2%)
    all_to_all x1, blocking collectives, shards(): wanted = lax.all_to_all(requests, ('section', 'dp'), 0, 0, tiled=True)  22.2 us
    all_to_all x1, starting transfers between devices, shards(): arrived = lax.all_to_all(message, ('section', 'dp'), 0, 0, tiled=True)  12.6 us
    all_to_all x1, waiting for transfers between devices, shards(): arrived = lax.all_to_all(message, ('section', 'dp'), 0, 0, tiled=True)  12 us
    ppermute x4, starting transfers between devices, mp_move(): return lax.ppermute(block, 'mp', perm)  11.9 us
    ppermute x4, waiting for transfers between devices, mp_move(): return lax.ppermute(block, 'mp', perm)  11.4 us
    ppermute x1, starting transfers between devices, half_move(): return lax.ppermute(block, ('section', 'dp'), perm)  10.9 us
    all_to_all x1, blocking collectives, shards(): messages = lax.all_to_all(message, 'mp', 0, 0, tiled=True)  9.23 us
    all_to_all x1, starting transfers between devices, shards(): fetched = lax.all_to_all(found, ('section', 'dp'), 0, 0, tiled=True)  8.88 us
  transfers between devices with their start and end apart: 10, of which 6 were waited for; matrix products, arithmetic and copies ran while one was open for 3% of the time, Pallas kernels for 8%

profile of v6, /device:TPU:8, one launch (start us, length us, event | category | flops | bytes accessed | tf_op | source)
XLA Modules:
  0.0 153.9 jit_solution(6627365754684996453)
XLA Ops:
  7.2 2.2 %cut.1 = (bf16[128,1920]{1,0:T(8,128)(2,1)}, bf16[128,1024]{1,0:T(8,128)(2,1)}) custom-call(bf16[128,640]{1,0:T(8,128)(2,1)} %gate_in.1, bf16[128,640]{1,0:T(8,128)(2,1)} %up_in.1, bf16[640,128]{1,0:T(8,128)(2,1)} %down_in.1), custom_call_target="tpu_custom_call" | custom-call | tf_op jit(solution)/shard_map/cut/pallas_call | solution.py:343
  9.5 10.9 %collective-permute-start = (bf16[128,1024]{1,0:T(8,128)(2,1)}, bf16[128,1024]{1,0:T(8,128)(2,1)S(1)}, u32[]{:S(2)}, u32[]{:S(2)}) collective-permute-start(bf16[128,1024]{1,0:T(8,128)(2,1)} %get-tuple-element.15), channel_id=1, source_target_pairs={{0,320},{8,328},{16,336},{24,344},{32,352},{40,360},{48,368},{56,3... | collective-permute-start | bytes 786440 | tf_op jit(solution)/shard_map/ppermute | solution.py:51
  20.4 0.7 broadcast_in_dim.4
  21.1 1.0 pad_maximum_fusion
  22.0 3.4 %collective-permute-start.1 = (bf16[400,256]{1,0:T(8,128)(2,1)S(1)}, bf16[400,256]{1,0:T(8,128)(2,1)S(1)}, u32[]{:S(2)}, u32[]{:S(2)}) collective-permute-start(bf16[400,256]{1,0:T(8,128)(2,1)S(1)} %pad_maximum_fusion), channel_id=1, source_target_pairs={{0,2},{1,3},{2,4},{3,5},{4,6},{5,7},{6,0},{7,1},{8,10},{9,11},{10,... | collective-permute-start | bytes 614408 | tf_op jit(solution)/shard_map/ppermute | solution.py:36
  25.4 0.8 reshape.26.owner
  26.2 0.8 reshape.27.row
  27.0 0.2 ask.1
  27.2 4.5 %collective-permute-done.1 = bf16[400,256]{1,0:T(8,128)(2,1)S(1)} collective-permute-done((bf16[400,256]{1,0:T(8,128)(2,1)S(1)}, bf16[400,256]{1,0:T(8,128)(2,1)S(1)}, u32[]{:S(2)}, u32[]{:S(2)}) %collective-permute-start.1) | collective-permute-done | bytes 204832 | tf_op jit(solution)/shard_map/ppermute | solution.py:36
  31.7 0.2 collective-permute-done
  31.9 1.7 %add_dynamic-update-slice_fusion = bf16[128,1920]{1,0:T(8,128)(2,1)} fusion(bf16[128,1920]{1,0:T(8,128)(2,1)} %get-tuple-element.19, bf16[128,1024]{1,0:T(8,128)(2,1)S(1)} %collective-permute-done), kind=kLoop, calls=%fused_computation.1 | loop fusion | flops 524288 | bytes 786432 | tf_op jit(solution)/shard_map/dynamic_update_slice | solution.py:373
  33.6 4.7 %collective-permute-start.2 = (bf16[400,256]{1,0:T(8,128)(2,1)S(1)}, bf16[400,256]{1,0:T(8,128)(2,1)S(1)}, u32[]{:S(2)}, u32[]{:S(2)}) collective-permute-start(bf16[400,256]{1,0:T(8,128)(2,1)S(1)} %pad_maximum_fusion), channel_id=1, source_target_pairs={{0,6},{1,7},{2,0},{3,1},{4,2},{5,3},{6,4},{7,5},{8,14},{9,15},{10,... | collective-permute-start | bytes 614408 | tf_op jit(solution)/shard_map/ppermute | solution.py:36
  38.4 1.9 %collective-permute-start.3 = (bf16[400,256]{1,0:T(8,128)(2,1)S(1)}, bf16[400,256]{1,0:T(8,128)(2,1)S(1)}, u32[]{:S(2)}, u32[]{:S(2)}) collective-permute-start(bf16[400,256]{1,0:T(8,128)(2,1)S(1)} %collective-permute-done.1), channel_id=1, source_target_pairs={{0,2},{1,3},{2,4},{3,5},{4,6},{5,7},{6,0},{7,1},{8,10},{9,11},{10,... | collective-permute-start | bytes 614408 | tf_op jit(solution)/shard_map/ppermute | solution.py:36
  40.4 1.4 collective-permute-done.2
  41.8 5.5 %collective-permute-done.3 = bf16[400,256]{1,0:T(8,128)(2,1)S(1)} collective-permute-done((bf16[400,256]{1,0:T(8,128)(2,1)S(1)}, bf16[400,256]{1,0:T(8,128)(2,1)S(1)}, u32[]{:S(2)}, u32[]{:S(2)}) %collective-permute-start.3) | collective-permute-done | bytes 204832 | tf_op jit(solution)/shard_map/ppermute | solution.py:36
  47.3 5.0 %collective-permute-start.4 = (bf16[1600,256]{1,0:T(8,128)(2,1)S(1)}, bf16[1600,256]{1,0:T(8,128)(2,1)S(1)}, u32[]{:S(2)}, u32[]{:S(2)}) collective-permute-start(bf16[1600,256]{1,0:T(8,128)(2,1)S(1)} %get-tuple-element.27), channel_id=1, source_target_pairs={{0,128},{128,0},{256,384},{384,256},{1,129},{129,1},{257,385},{385... | collective-permute-start | bytes 2457608 | tf_op jit(solution)/shard_map/ppermute | solution.py:40
  52.3 22.2 %all_to_all.32 = s32[64,1,128]{2,1,0:T(1,128)S(1)} all-to-all(s32[64,1,128]{2,1,0:T(1,128)S(1)} %bitcast.9), channel_id=1, replica_groups=mesh['section'=4,'dp'=16,'mp'=8] {'section','dp'}, dimensions={0} | all-to-all | bytes 65536 | tf_op jit(solution)/shard_map/all_to_all | solution.py:375
  74.6 1.9 %collective-permute-start.5 = (bf16[3200,256]{1,0:T(8,128)(2,1)S(1)}, bf16[3200,256]{1,0:T(8,128)(2,1)S(1)}, u32[]{:S(2)}, u32[]{:S(2)}) collective-permute-start(bf16[3200,256]{1,0:T(8,128)(2,1)S(1)} %constant_dynamic-update-slice_fusion.6.near), channel_id=1, source_target_pairs={{0,1},{1,0},{2,3},{3,2},{4,5},{5,4},{6,7},{7,6},{8,9},{9,8},{10,11... | collective-permute-start | bytes 4915208 | tf_op jit(solution)/shard_map/ppermute | solution.py:36
  76.5 1.1 find.1
  77.6 8.9 %all-to-all-start.2 = ((f32[64,2,128]{2,1,0:T(2,128)}), f32[64,2,128]{2,1,0:T(2,128)S(1)}, u32[]{:S(2)}, u32[]{:S(2)}) async-start(f32[64,2,128]{2,1,0:T(2,128)} %find.1), calls=%async_computation.2 | async-start | bytes 131072 | tf_op jit(solution)/shard_map/all_to_all | solution.py:385
  86.6 3.2 %norm.1.normed = bf16[768,2048]{1,0:T(8,128)(2,1)S(1)} custom-call(bf16[3200,256]{1,0:T(8,128)(2,1)S(1)} %constant_dynamic-update-slice_fusion.6.near, bf16[3200,256]{1,0:T(8,128)(2,1)S(1)} %collective-permute-done.5.far), custom_call_target="tpu_custom_call" | custom-call | tf_op jit(solution)/shard_map/norm/pallas_call | solution.py:387
  89.8 1.7 %copy-done = bf16[768,2048]{1,0:T(8,128)(2,1)} copy-done((bf16[768,2048]{1,0:T(8,128)(2,1)}, bf16[768,2048]{1,0:T(8,128)(2,1)S(1)}, u32[]{:S(2)}) %copy-start) | copy-done | bytes 3145752
  91.5 7.8 %hidden.1 = f32[16,8,256]{2,1,0:T(8,128)} custom-call(bf16[768,2048]{1,0:T(8,128)(2,1)} %copy-done, bf16[16,768]{1,0:T(8,128)(2,1)S(1)} %copy-done.4, bf16[1024,1920]{1,0:T(8,128)(2,1)} %all-gather.2.cloned.1.call-done.weights), custom_call_target="tpu_custom_call" | custom-call | tf_op jit(solution)/shard_map/hidden/pallas_call | solution.py:405
  99.3 3.5 %all-to-all-start.1 = ((f32[16,8,256]{2,1,0:T(8,128)}), f32[16,8,256]{2,1,0:T(8,128)S(1)}, u32[]{:S(2)}, u32[]{:S(2)}) async-start(f32[16,8,256]{2,1,0:T(8,128)} %hidden.1), calls=%async_computation.1 | async-start | bytes 262144 | tf_op jit(solution)/shard_map/all_to_all | solution.py:421
  103.0 6.5 %all-to-all-done.1.parts = f32[16,8,256]{2,1,0:T(8,128)S(1)} async-done(((f32[16,8,256]{2,1,0:T(8,128)}), f32[16,8,256]{2,1,0:T(8,128)S(1)}, u32[]{:S(2)}, u32[]{:S(2)}) %all-to-all-start.1) | async-done | bytes 131104 | tf_op jit(solution)/shard_map/all_to_all | solution.py:421
  109.5 0.7 head.1
  110.2 9.2 %all_to_all.33.messages = bf16[8,96,128]{2,1,0:T(8,128)(2,1)S(1)} all-to-all(bf16[8,96,128]{2,1,0:T(8,128)(2,1)S(1)} %get-tuple-element.22), channel_id=1, replica_groups=mesh['section'=4,'dp'=16,'mp'=8] {'mp'}, dimensions={0} | all-to-all | bytes 393216 | tf_op jit(solution)/shard_map/all_to_all | solution.py:450
  119.5 1.6 %loss.1 = (bf16[2,96]{1,0:T(2,128)(2,1)}, f32[4,128]{1,0:T(4,128)S(1)}, bf16[64,4,384]{2,1,0:T(4,128)(2,1)}) custom-call(s32[4]{0:T(128)S(1)} %copy-done.5, bf16[8,96,128]{2,1,0:T(8,128)(2,1)S(1)} %all_to_all.33.messages, bf16[8,256]{1,0:T(8,128)(2,1)S(1)} %get-tuple-element.23.pooled), custom_call_target="tpu_custom_call" | custom-call | tf_op jit(solution)/shard_map/loss/pallas_call | solution.py:452
  121.0 12.6 %all-to-all-start.4 = ((bf16[64,4,384]{2,1,0:T(4,128)(2,1)}), bf16[64,4,384]{2,1,0:T(4,128)(2,1)S(1)}, u32[]{:S(2)}, u32[]{:S(2)}) async-start(bf16[64,4,384]{2,1,0:T(4,128)(2,1)} %get-tuple-element.26), calls=%async_computation.4 | async-start | bytes 393216 | tf_op jit(solution)/shard_map/all_to_all | solution.py:466
  133.6 0.6 slice_reduce_fusion
  134.2 12.0 %all-to-all-done.4 = bf16[64,4,384]{2,1,0:T(4,128)(2,1)S(1)} async-done(((bf16[64,4,384]{2,1,0:T(4,128)(2,1)}), bf16[64,4,384]{2,1,0:T(4,128)(2,1)S(1)}, u32[]{:S(2)}, u32[]{:S(2)}) %all-to-all-start.4) | async-done | bytes 196640 | tf_op jit(solution)/shard_map/all_to_all | solution.py:466
  146.2 0.8 grad.1
  (38 shorter events, 0.6 us)
Async XLA Ops:
  7.2 31.1 %copy-start.6 = (bf16[2,128,256]{2,1,0:T(8,128)(2,1)S(1)}, bf16[2,128,256]{2,1,0:T(8,128)(2,1)}, u32[]{:S(2)}) copy-start(bf16[2,128,256]{2,1,0:T(8,128)(2,1)} %param.13) | copy-start | bytes 393220
  7.2 31.2 %copy-start.7 = (bf16[4,32,256]{2,1,0:T(8,128)(2,1)S(1)}, bf16[4,32,256]{2,1,0:T(8,128)(2,1)}, u32[]{:S(2)}) copy-start(bf16[4,32,256]{2,1,0:T(8,128)(2,1)} %param.14) | copy-start | bytes 196612
  7.2 31.2 %copy-start.8 = (bf16[256]{0:T(256)(128)(2,1)S(1)}, bf16[256]{0:T(256)(128)(2,1)}, u32[]{:S(2)}) copy-start(bf16[256]{0:T(256)(128)(2,1)} %param.15) | copy-start | bytes 1540
  7.2 84.2 %all-gather.2.cloned.1.call-start = ((), (), s32[]{:S(2)}) async-start(), calls=%async_computation.5 | async-start | bytes 4423680 | tf_op jit(solution)/shard_map/all_gather | solution.py:57
  9.5 22.4 %collective-permute-start = (bf16[128,1024]{1,0:T(8,128)(2,1)}, bf16[128,1024]{1,0:T(8,128)(2,1)S(1)}, u32[]{:S(2)}, u32[]{:S(2)}) collective-permute-start(bf16[128,1024]{1,0:T(8,128)(2,1)} %get-tuple-element.15), channel_id=1, source_target_pairs={{0,320},{8,328},{16,336},{24,344},{32,352},{40,360},{48,368},{56,3... | collective-permute-start | bytes 786440 | tf_op jit(solution)/shard_map/ppermute | solution.py:51
  22.0 9.6 %collective-permute-start.1 = (bf16[400,256]{1,0:T(8,128)(2,1)S(1)}, bf16[400,256]{1,0:T(8,128)(2,1)S(1)}, u32[]{:S(2)}, u32[]{:S(2)}) collective-permute-start(bf16[400,256]{1,0:T(8,128)(2,1)S(1)} %pad_maximum_fusion), channel_id=1, source_target_pairs={{0,2},{1,3},{2,4},{3,5},{4,6},{5,7},{6,0},{7,1},{8,10},{9,11},{10,... | collective-permute-start | bytes 614408 | tf_op jit(solution)/shard_map/ppermute | solution.py:36
  33.6 8.1 %collective-permute-start.2 = (bf16[400,256]{1,0:T(8,128)(2,1)S(1)}, bf16[400,256]{1,0:T(8,128)(2,1)S(1)}, u32[]{:S(2)}, u32[]{:S(2)}) collective-permute-start(bf16[400,256]{1,0:T(8,128)(2,1)S(1)} %pad_maximum_fusion), channel_id=1, source_target_pairs={{0,6},{1,7},{2,0},{3,1},{4,2},{5,3},{6,4},{7,5},{8,14},{9,15},{10,... | collective-permute-start | bytes 614408 | tf_op jit(solution)/shard_map/ppermute | solution.py:36
  38.4 8.9 %collective-permute-start.3 = (bf16[400,256]{1,0:T(8,128)(2,1)S(1)}, bf16[400,256]{1,0:T(8,128)(2,1)S(1)}, u32[]{:S(2)}, u32[]{:S(2)}) collective-permute-start(bf16[400,256]{1,0:T(8,128)(2,1)S(1)} %collective-permute-done.1), channel_id=1, source_target_pairs={{0,2},{1,3},{2,4},{3,5},{4,6},{5,7},{6,0},{7,1},{8,10},{9,11},{10,... | collective-permute-start | bytes 614408 | tf_op jit(solution)/shard_map/ppermute | solution.py:36
  40.4 36.2 %copy-start.3 = (bf16[2048,96]{0,1:T(8,128)(2,1)S(1)}, bf16[2048,96]{0,1:T(8,128)(2,1)}, u32[]{:S(2)}) copy-start(bf16[2048,96]{0,1:T(8,128)(2,1)} %param.21) | copy-start | bytes 1179652
  47.3 27.2 %collective-permute-start.4 = (bf16[1600,256]{1,0:T(8,128)(2,1)S(1)}, bf16[1600,256]{1,0:T(8,128)(2,1)S(1)}, u32[]{:S(2)}, u32[]{:S(2)}) collective-permute-start(bf16[1600,256]{1,0:T(8,128)(2,1)S(1)} %get-tuple-element.27), channel_id=1, source_target_pairs={{0,128},{128,0},{256,384},{384,256},{1,129},{129,1},{257,385},{385... | collective-permute-start | bytes 2457608 | tf_op jit(solution)/shard_map/ppermute | solution.py:40
  74.6 12.0 %collective-permute-start.5 = (bf16[3200,256]{1,0:T(8,128)(2,1)S(1)}, bf16[3200,256]{1,0:T(8,128)(2,1)S(1)}, u32[]{:S(2)}, u32[]{:S(2)}) collective-permute-start(bf16[3200,256]{1,0:T(8,128)(2,1)S(1)} %constant_dynamic-update-slice_fusion.6.near), channel_id=1, source_target_pairs={{0,1},{1,0},{2,3},{3,2},{4,5},{5,4},{6,7},{7,6},{8,9},{9,8},{10,11... | collective-permute-start | bytes 4915208 | tf_op jit(solution)/shard_map/ppermute | solution.py:36
  77.6 21.7 %all-to-all-start.2 = ((f32[64,2,128]{2,1,0:T(2,128)}), f32[64,2,128]{2,1,0:T(2,128)S(1)}, u32[]{:S(2)}, u32[]{:S(2)}) async-start(f32[64,2,128]{2,1,0:T(2,128)} %find.1), calls=%async_computation.2 | async-start | bytes 131072 | tf_op jit(solution)/shard_map/all_to_all | solution.py:385
  86.6 4.9 %copy-start.4 = (bf16[16,768]{1,0:T(8,128)(2,1)S(1)}, bf16[16,768]{1,0:T(8,128)(2,1)}, u32[]{:S(2)}) copy-start(bf16[16,768]{1,0:T(8,128)(2,1)} %constant.15.clone.pool) | copy-start | bytes 73732
  89.8 1.7 %copy-start = (bf16[768,2048]{1,0:T(8,128)(2,1)}, bf16[768,2048]{1,0:T(8,128)(2,1)S(1)}, u32[]{:S(2)}) copy-start(bf16[768,2048]{1,0:T(8,128)(2,1)S(1)} %norm.1.normed) | copy-start | bytes 9437188
  91.4 18.1 %copy-start.1 = (bf16[256,768]{1,0:T(8,128)(2,1)S(1)}, bf16[256,768]{1,0:T(8,128)(2,1)}, u32[]{:S(2)}) copy-start(bf16[256,768]{1,0:T(8,128)(2,1)} %old_head.1) | copy-start | bytes 1179652
  91.4 18.1 %copy-start.2 = (bf16[256,768]{1,0:T(8,128)(2,1)S(1)}, bf16[256,768]{1,0:T(8,128)(2,1)}, u32[]{:S(2)}) copy-start(bf16[256,768]{1,0:T(8,128)(2,1)} %new_head.1) | copy-start | bytes 1179652
  99.3 20.2 %copy-start.5 = (s32[4]{0:T(128)S(1)}, s32[4]{0:T(128)}, u32[]{:S(2)}) copy-start(s32[4]{0:T(128)} %slot.1) | copy-start | bytes 52
  99.3 10.2 %all-to-all-start.1 = ((f32[16,8,256]{2,1,0:T(8,128)}), f32[16,8,256]{2,1,0:T(8,128)S(1)}, u32[]{:S(2)}, u32[]{:S(2)}) async-start(f32[16,8,256]{2,1,0:T(8,128)} %hidden.1), calls=%async_computation.1 | async-start | bytes 262144 | tf_op jit(solution)/shard_map/all_to_all | solution.py:421
  121.0 25.2 %all-to-all-start.4 = ((bf16[64,4,384]{2,1,0:T(4,128)(2,1)}), bf16[64,4,384]{2,1,0:T(4,128)(2,1)S(1)}, u32[]{:S(2)}, u32[]{:S(2)}) async-start(bf16[64,4,384]{2,1,0:T(4,128)(2,1)} %get-tuple-element.26), calls=%async_computation.4 | async-start | bytes 393216 | tf_op jit(solution)/shard_map/all_to_all | solution.py:466
Sparse Core Ops, SparseCore 0:
  33.8 54.0 all-gather.1
